TPU v7x, 32 devices: a whole 2x2x4 slice. The times are simulated.
32 devices in a mesh: grp: 2 (over y), row: 4 (over z), col: 4 (over x, core).
Axes of the slice: x: 2, y: 2, z: 4, core: 2. Of those that a mesh axis runs over, the one named last changes fastest.
Arguments:
- front: float32 [2048, 2048], P('col', ('grp', 'row')), may hold values from -9 to 11, as said below
- child_blocks: float32 [2, 2048, 2048], P('grp', ('row', 'col')), may hold values from -4.5 to 4.5, as said below
- child_map: int32 [2, 16], replicated, may hold values from 0 to 15, as said below
Outputs:
- factor: float32 [2048, 2048], P('col', ('grp', 'row'))
Inputs may be any that keep to these rules, and one draw needn't show every extreme that they name: `front`: symmetric positive definite. `child_blocks`: each child's block is symmetric positive semidefinite. `child_map`: the blocks of one child are distinct; block q of a child, with q modulo the size of the col axis equal to k, lies in parent blocks k * 2 * 2 to (k + 1) * 2 * 2 - 1; at most 2 blocks of one child fall in one aligned group of 2 parent blocks, and in every draw some group holds 2.
All inputs are finite; a program needn't handle non-finite values.
Results may differ from a plain program's by a relative error of at most 0.00005.
Values sent between devices are 32-bit elements; how exact they have to be, the bound alone decides.
No kernel may reach another device: no remote copies, remote signals or barrier semaphores. Data moves between devices by JAX's collectives and lax.ppermute only.
A program may use at most 128 MiB of HBM per device.

v0:
```python
import jax
import jax.numpy as jnp
from jax import lax
from jax.sharding import PartitionSpec as P

BLK = 128
PIVOTS = 256


def from_root(value, axis, root):
    mine = lax.axis_index(axis) == root
    return lax.psum(jnp.where(mine, value, jnp.zeros_like(value)), axis)


def solve_panel(panel_source, diag_all, global_rows, panel_start, panel_width, diag_off, on_root):
    lower_block = jnp.linalg.cholesky(diag_all)
    solved = lax.linalg.triangular_solve(
        lower_block, panel_source, left_side=False, lower=True, transpose_a=True
    )
    below = global_rows >= panel_start + panel_width
    result = jnp.where(below[:, None], solved, 0.0)
    diag_slot = result[diag_off : diag_off + panel_width]
    return result.at[diag_off : diag_off + panel_width].set(
        jnp.where(on_root, lower_block, diag_slot)
    )


def matching_rows(factor_rows, owner_index, panel_width, rows_dev):
    col_root = owner_index * panel_width // rows_dev
    col_piece = lax.dynamic_slice_in_dim(
        factor_rows, owner_index * panel_width % rows_dev, panel_width, 0
    )
    return from_root(col_piece, "col", col_root)


def body(front, child_blocks, child_map):
    n_grp = lax.axis_size("grp")
    n_row = lax.axis_size("row")
    n_col = lax.axis_size("col")
    owners = n_grp * n_row
    slot_count = max(1, n_col // n_grp)
    grp_index = lax.axis_index("grp")
    row_index = lax.axis_index("row")
    col_index = lax.axis_index("col")
    owner_index = grp_index * n_row + row_index
    rows_dev, panel_width = front.shape
    blocks_own = panel_width // BLK
    row_blocks = rows_dev // BLK
    child_count = child_map.shape[1]
    highest = lax.Precision.HIGHEST
    child_owner = child_map // blocks_own
    positions = jnp.arange(child_count)
    earlier = positions[None, :] < positions[:, None]
    same_owner = child_owner[:, :, None] == child_owner[:, None, :]
    owner_rank = jnp.sum(same_owner & earlier[None], axis=2)
    grp_pick = jnp.arange(n_grp)[:, None] == grp_index
    my_owner = jnp.sum(jnp.where(grp_pick, child_owner, 0), axis=0)
    my_rank = jnp.sum(jnp.where(grp_pick, owner_rank, 0), axis=0)
    owner_ids = jnp.arange(owners)
    slot_ids = jnp.arange(slot_count)
    selector = (
        (my_owner[None, None, :] == owner_ids[:, None, None])
        & (my_rank[None, None, :] == slot_ids[None, :, None])
    ).astype(jnp.float32)
    row_strip = child_blocks[0].reshape(BLK, child_count, BLK)
    outgoing = jnp.einsum("oka,iaj->okij", selector, row_strip, precision=highest)
    incoming = lax.all_to_all(outgoing, ("grp", "row"), split_axis=0, concat_axis=0, tiled=True)
    source_grp = owner_ids // n_row
    source_row = owner_ids % n_row
    flat_index = source_grp * child_count + source_row * n_col + col_index
    flat_map = child_map.reshape(-1)
    flat_hits = jnp.arange(flat_map.shape[0])[None, :] == flat_index[:, None]
    target_block = jnp.sum(jnp.where(flat_hits, flat_map[None, :], 0), axis=1)
    local_block = target_block - col_index * row_blocks
    row_select = (jnp.arange(row_blocks)[:, None] == local_block[None, :]).astype(jnp.float32)
    matches = (child_owner[:, None, :] == owner_index) & (
        owner_rank[:, None, :] == slot_ids[None, :, None]
    )
    present = jnp.any(matches, axis=2)
    column_local = jnp.sum(
        jnp.where(matches, child_map[:, None, :] - owner_index * blocks_own, 0), axis=2
    )
    column_select = (
        present[None] & (column_local[None] == jnp.arange(blocks_own)[:, None, None])
    ).astype(jnp.float32)
    column_select = jnp.repeat(column_select, n_row, axis=1)
    assembled_add = jnp.einsum(
        "bs,tsk,skij->bitj", row_select, column_select, incoming, precision=highest
    )
    assembled = front + assembled_add.reshape(rows_dev, panel_width)
    global_rows = col_index * rows_dev + jnp.arange(rows_dev)
    global_cols = owner_index * panel_width + jnp.arange(panel_width)
    eye_block = jnp.eye(panel_width, dtype=jnp.float32)
    diag_root = 0 // rows_dev
    diag_off = 0 - diag_root * rows_dev
    on_root = col_index == diag_root
    is_owner = owner_index == 0
    diag_all = from_root(assembled[diag_off : diag_off + panel_width], "col", diag_root)
    diag_all = jnp.where(is_owner, diag_all, eye_block)
    own_rows = solve_panel(assembled, diag_all, global_rows, 0, panel_width, diag_off, on_root)
    panel_rows = from_root(own_rows, ("grp", "row"), 0)
    assembled = jnp.where(is_owner, panel_rows, assembled)
    panel_cols = matching_rows(panel_rows, owner_index, panel_width, rows_dev)
    left_part = jnp.where((global_rows >= panel_width)[:, None], panel_rows, 0.0)
    right_part = jnp.where((global_cols >= panel_width)[:, None], panel_cols, 0.0)
    assembled = assembled - jnp.dot(left_part, right_part.T, precision=highest)
    upper_part = (global_rows[:, None] < PIVOTS) & (global_cols[None, :] >= PIVOTS)
    return jnp.where(upper_part, 0.0, assembled)


def solution(mesh):
    return jax.shard_map(
        body,
        mesh=mesh,
        in_specs=(P("col", ("grp", "row")), P("grp", ("row", "col"), None), P()),
        out_specs=P("col", ("grp", "row")),
        check_vma=False,
    )
```

profile of v0, /device:TPU:0, one launch (start us, length us, event | category | flops | bytes accessed | tf_op | source)
XLA Modules:
  0.0 259.8 jit_solution(5521632150350766861)
XLA Ops:
  6.6 0.0 copy-start.3
  6.6 0.7 copy-done.3
  7.3 0.2 convert_reduce_fusion
  7.4 0.1 select_reduce_fusion.5
  7.5 1.4 copy.34
  9.0 0.6 fusion.20
  9.6 1.2 copy.25
  10.8 0.0 copy-start.2
  10.8 7.4 %all-to-all-start = ((f32[8,2,128,128]{3,2,1,0:T(8,128)}), f32[8,2,128,128]{3,2,1,0:T(8,128)S(1)}, u32[]{:S(2)}, u32[]{:S(2)}) async-start(f32[8,2,128,128]{3,2,1,0:T(8,128)} %copy.25), calls=%async_computation | async-start | bytes 2097152 | tf_op jit(solution)/shard_map/all_to_all | solution.py:67
  18.2 0.0 all-reduce.5.cloned.1.call-start
  18.2 0.1 broadcast_in_dim.106
  18.3 0.1 select_reduce_fusion.3
  18.5 0.1 copy.14
  18.6 0.2 fusion.22
  18.7 0.1 copy.13
  18.8 0.1 copy.33
  18.9 0.0 copy-done.2
  18.9 0.2 copy.16
  19.2 0.2 select_reduce_fusion.2
  19.4 25.4 %all-to-all-done = f32[8,2,128,128]{3,2,1,0:T(8,128)S(1)} async-done(((f32[8,2,128,128]{3,2,1,0:T(8,128)}), f32[8,2,128,128]{3,2,1,0:T(8,128)S(1)}, u32[]{:S(2)}, u32[]{:S(2)}) %all-to-all-start) | async-done | bytes 1048608 | tf_op jit(solution)/shard_map/all_to_all | solution.py:67
  44.8 4.0 %fusion.2 = f32[8,128,128,2]{2,3,1,0:T(2,128)S(1)} fusion(f32[2,8,2,1]{0,2,3,1:T(2,128)S(1)} %bitcast.55, f32[8,2,128,128]{3,2,1,0:T(8,128)S(1)} %all-to-all-done), kind=kOutput, calls=%fused_computation.8 | convolution fusion | flops 6291456 | bytes 2097280 | tf_op jit(solution)/shard_map/bs,tsk,skij->bitj/dot_general | solution.py:87
  48.9 1.2 convolution_bitcast_fusion
  50.0 0.3 copy.15
  50.3 0.1 bitcast_add_fusion
  50.4 0.7 slice_select_fusion.1
  51.1 0.0 all-reduce.5.cloned.1.call-update
  51.2 0.2 all-reduce.7.cloned.1.call-start
  51.4 29.2 %all-reduce.5.cloned.1.call-done = f32[256,256]{0,1:T(8,128)} async-done(((f32[256,256]{0,1:T(8,128)}), f32[256,256]{0,1:T(8,128)}) %all-reduce.5.cloned.1.call-update) | async-done | bytes 262160 | tf_op jit(solution)/shard_map/psum | solution.py:12
  80.6 1.0 convert_select_fusion
  81.6 0.0 copy-start.1
  81.6 0.1 copy.17
  81.7 0.8 copy-done.1
  82.6 11.7 %cholesky.49 = f32[128,128]{1,0:T(8,128)S(1)} custom-call(f32[128,128]{1,0:T(8,128)S(1)} %cholesky.115), custom_call_target="Cholesky" | custom-call | tf_op jit(solution)/shard_map/jit(cholesky)/cholesky | solution.py:16
  94.3 9.8 %custom-call.14 = f32[1,128,128]{1,2,0:T(8,128)S(1)} custom-call(f32[1,128,128]{2,1,0:T(8,128)S(1)} %get-tuple-element.48), custom_call_target="InvertDiagBlocksLowerTriangular" | custom-call | tf_op jit(solution)/shard_map/jit(cholesky)/cholesky | solution.py:16
  104.1 0.2 fusion.17
  104.4 0.3 convolution_subtract_fusion.2
  104.6 11.7 %cholesky.103 = f32[128,128]{1,0:T(8,128)S(1)} custom-call(f32[128,128]{1,0:T(8,128)S(1)} %convolution_subtract_fusion.2), custom_call_target="Cholesky" | custom-call | tf_op jit(solution)/shard_map/jit(cholesky)/cholesky | solution.py:16
  116.4 0.1 copy.20
  116.5 0.1 copy.19
  116.6 0.1 copy.18
  116.7 0.7 compare_reduce_fusion
  118.8 0.1 triangular_solve.61
  118.9 4.5 %while.2 = (s32[]{:T(128)}, f32[256,256]{0,1:T(8,128)S(1)}, s32[2,2]{1,0:T(2,128)S(1)}, f32[2,128,128]{2,1,0:T(8,128)S(1)}, s32[]{:T(128)}) while((s32[]{:T(128)}, f32[256,256]{0,1:T(8,128)S(1)}, s32[2,2]{1,0:T(2,128)S(1)}, f32[2,128,128]{2,1,0:T(8,128)S(1)}, s32[]{:T(128)}) %tuple.29), condition=%wide.while_cond.1, body=%wide.while_body.1.sunk | while | flops 2 | bytes 393321 | solution.py:17
  119.1 0.6 fusion.41
  119.7 1.4 dynamic-slice.15
  121.1 0.1 copy.44
  121.3 0.6 fusion.41
  121.9 1.4 dynamic-slice.15
  123.3 0.1 copy.44
  123.4 19.7 %custom-call.15 = f32[2,128,128]{1,2,0:T(8,128)S(1)} custom-call(f32[2,128,128]{2,1,0:T(8,128)S(1)} %get-tuple-element.24), custom_call_target="InvertDiagBlocksLowerTriangular" | custom-call | tf_op jit(solution)/shard_map/triangular_solve | solution.py:17
  143.1 0.4 fusion.6
  143.5 0.4 convolution_subtract_fusion.1
  143.9 0.4 fusion.15
  144.4 0.1 fusion.5
  144.5 0.8 broadcast_select_fusion
  145.3 0.0 all-reduce.7.cloned.1.call-update
  145.4 0.0 all-reduce.9.cloned.1.call-start
  145.4 71.5 %all-reduce.7.cloned.1.call-done = f32[512,256]{0,1:T(8,128)} async-done(((f32[512,256]{0,1:T(8,128)}), f32[512,256]{0,1:T(8,128)}) %all-reduce.7.cloned.1.call-update) | async-done | bytes 524304 | tf_op jit(solution)/shard_map/psum | solution.py:12
  216.9 1.7 dynamic-slice_select_fusion
  218.7 0.0 all-reduce.9.cloned.1.call-update
  218.7 31.8 %all-reduce.9.cloned.1.call-done = f32[256,256]{0,1:T(8,128)} async-done(((f32[256,256]{0,1:T(8,128)}), f32[256,256]{0,1:T(8,128)}) %all-reduce.9.cloned.1.call-update) | async-done | bytes 262160 | tf_op jit(solution)/shard_map/psum | solution.py:12
  250.5 0.0 copy-done
  250.5 1.7 fusion
  252.2 1.0 copy.23
  (30 shorter events, 0.4 us)
Async XLA Ops:
  6.6 0.7 copy-start.3
  10.8 8.2 %copy-start.2 = (f32[512,256]{1,0:T(8,128)S(1)}, f32[512,256]{1,0:T(8,128)}, u32[]{:S(2)}) copy-start(f32[512,256]{1,0:T(8,128)} %param.5) | copy-start | bytes 1572868
  10.8 34.0 %all-to-all-start = ((f32[8,2,128,128]{3,2,1,0:T(8,128)}), f32[8,2,128,128]{3,2,1,0:T(8,128)S(1)}, u32[]{:S(2)}, u32[]{:S(2)}) async-start(f32[8,2,128,128]{3,2,1,0:T(8,128)} %copy.25), calls=%async_computation | async-start | bytes 2097152 | tf_op jit(solution)/shard_map/all_to_all | solution.py:67
  18.2 62.4 %all-reduce.5.cloned.1.call-start = ((), (), s32[]{:S(2)}) async-start(), calls=%async_computation.1 | async-start | bytes 524288 | tf_op jit(solution)/shard_map/psum | solution.py:12
  51.2 165.8 %all-reduce.7.cloned.1.call-start = ((), (), s32[]{:S(2)}) async-start(), calls=%async_computation.2 | async-start | bytes 1048576 | tf_op jit(solution)/shard_map/psum | solution.py:12
  81.6 1.0 copy-start.1
  145.4 105.2 %all-reduce.9.cloned.1.call-start = ((), (), s32[]{:S(2)}) async-start(), calls=%async_computation.3 | async-start | bytes 524288 | tf_op jit(solution)/shard_map/psum | solution.py:12
  216.9 33.6 %copy-start = (f32[512,256]{0,1:T(8,128)S(1)}, f32[512,256]{0,1:T(8,128)}, u32[]{:S(2)}) copy-start(f32[512,256]{0,1:T(8,128)} %all-reduce.7.cloned.1.call-done) | copy-start | bytes 1572868
Sparse Core Ops, SparseCore 0:
  51.3 29.2 all-reduce.4
  145.5 71.3 all-reduce.6
  219.3 31.2 all-reduce.8
where the time goes:
time: 260 us
  waiting for transfers between devices  158 us (61%)
  other arithmetic  59.1 us (23%)
  between operations  14.8 us (6%)
  local copies, waits for them, and re-layouts  10.7 us (4%)
  matrix products  9.23 us (4%)
  starting transfers between devices  7.71 us (3%)
    psum x3, waiting for transfers between devices, from_root(): return lax.psum(jnp.where(mine, value, jnp.zeros_like(value)), axis)  132 us
    another operation x6, other arithmetic, solve_panel(): lower_block = jnp.linalg.cholesky(diag_all)  34 us
    all_to_all x1, waiting for transfers between devices, body(): lax.all_to_all(outgoing, ('grp', 'row'), split_axis=0, concat_axis=0, til...  25.4 us
    another operation x3, other arithmetic, solve_panel(): lax.linalg.triangular_solve(lower_block, panel_source, left_side=False, l...  19.7 us
    all_to_all x1, starting transfers between devices, body(): lax.all_to_all(outgoing, ('grp', 'row'), split_axis=0, concat_axis=0, til...  7.41 us
    dot_general x2, matrix products, body(): jnp.einsum('bs,tsk,skij->bitj', row_select, column_select, incoming, prec...  5.2 us
  transfers between devices with their start and end apart: 4, of which 4 were waited for; matrix products, arithmetic and copies ran while one was open for 0% of the time, Pallas kernels for 0%

commit v1 on v0

v1 whole, which is shorter than its diff:
```python
import functools

import jax
import jax.numpy as jnp
from jax import lax
from jax.experimental import pallas as pl
from jax.experimental.pallas import tpu as pltpu
from jax.sharding import PartitionSpec as P

BLK = 128
PIVOTS = 256
OWNER = ("grp", "row")
HIGHEST = lax.Precision.HIGHEST
VMEM = pl.BlockSpec(memory_space=pltpu.VMEM)
SMEM = pl.BlockSpec(memory_space=pltpu.SMEM)
ANY = pl.BlockSpec(memory_space=pl.ANY)
PARAMS = pltpu.CompilerParams(vmem_limit_bytes=48 * 1024 * 1024)


def f32(*shape):
    return jax.ShapeDtypeStruct(shape, jnp.float32)


def owner_of():
    return lax.axis_index("grp") * lax.axis_size("row") + lax.axis_index("row")


def invert_map(map_ref, inv_ref, grp):
    blocks = inv_ref.shape[0]
    for q in range(blocks):
        inv_ref[map_ref[grp, q]] = q


def split_panel_kernel(map_ref, strip_ref, *refs):
    outs, (inv_ref, sems) = refs[:-2], refs[-2:]
    pieces = len(outs)
    rows, width = outs[0].shape
    grp = lax.axis_index("grp")
    me = owner_of()
    invert_map(map_ref, inv_ref, grp)
    copies = []
    for d in range(pieces):
        for s in range(width // BLK):
            source = inv_ref[s]
            copies.append(
                pltpu.make_async_copy(
                    strip_ref.at[pl.ds((me ^ d) * rows, rows), pl.ds(source * BLK, BLK)],
                    outs[d].at[:, pl.ds(s * BLK, BLK)],
                    sems.at[d, s],
                )
            )
    for copy in copies:
        copy.start()
    for copy in copies:
        copy.wait()


def split_strip_kernel(map_ref, strip_ref, *refs):
    outs, (inv_ref, sems) = refs[:-2], refs[-2:]
    pieces = len(outs)
    _, width = outs[0].shape
    per = width // BLK
    grp = lax.axis_index("grp")
    me = owner_of()
    invert_map(map_ref, inv_ref, grp)
    copies = []
    for d in range(pieces):
        for s in range(per):
            source = inv_ref[(me ^ d) * per + s]
            copies.append(
                pltpu.make_async_copy(
                    strip_ref.at[:, pl.ds(source * BLK, BLK)],
                    outs[d].at[:, pl.ds(s * BLK, BLK)],
                    sems.at[d, s],
                )
            )
    for copy in copies:
        copy.start()
    for copy in copies:
        copy.wait()


def local_block(map_ref, source, row_blocks):
    n_row, n_col = lax.axis_size("row"), lax.axis_size("col")
    col = lax.axis_index("col")
    grp, row = source // n_row, source % n_row
    return map_ref[grp, row * n_col + col] - col * row_blocks


def sum_panel_kernel(map_ref, *refs):
    out_ref = refs[-1]
    pieces = (len(refs) - 1) // 2
    fronts, strips = refs[:pieces], refs[pieces:-1]
    me = owner_of()
    total = jnp.where(me == 0, fronts[0][...], 0.0)
    for ref in fronts[1:]:
        total = total + ref[...]
    out_ref[...] = total
    for d in range(pieces):
        block = local_block(map_ref, me ^ d, out_ref.shape[0])
        out_ref[block] = out_ref[block] + strips[d][...]


def finish_kernel(map_ref, front_ref, rows_c_ref, rows_o_ref, inv_ref, lower_ref, *refs):
    strips, out_ref = refs[:-1], refs[-1]
    rows, width = out_ref.shape
    col = lax.axis_index("col")
    me = owner_of()
    row_blocks = rows // BLK
    inv = inv_ref[...]
    dims = (((1,), (1,)), ((), ()))
    dot = functools.partial(
        lax.dot_general, dimension_numbers=dims, precision=HIGHEST, preferred_element_type=jnp.float32
    )
    left = dot(rows_c_ref[...], inv)

    @pl.when(me == 0)
    def _():
        out_ref[...] = left

        @pl.when(col == 0)
        def _():
            out_ref[:PIVOTS, :] = lower_ref[...]

    @pl.when(me != 0)
    def _():
        right = dot(rows_o_ref[...], inv)
        out_ref[...] = front_ref[...] - dot(left, right)
        for d, ref in enumerate(strips):
            start = pl.multiple_of(local_block(map_ref, me ^ d, row_blocks) * BLK, BLK)
            out_ref[pl.ds(start, BLK), :] += ref[...]

        @pl.when(col == 0)
        def _():
            out_ref[:PIVOTS, :] = jnp.zeros((PIVOTS, width), jnp.float32)


def exchange(value, d, skip_root=False):
    owners = lax.axis_size(OWNER)
    perm = [(i, i ^ d) for i in range(owners) if not (skip_root and i == d)]
    return lax.ppermute(value, OWNER, perm)


def from_root(value, axis, root):
    mine = lax.axis_index(axis) == root
    return lax.psum(jnp.where(mine, value, jnp.zeros_like(value)), axis)


def gather_wide(front, strip, child_map):
    n_row, n_col = lax.axis_size("row"), lax.axis_size("col")
    owners = lax.axis_size(OWNER)
    rows, width = front.shape
    row_blocks = rows // BLK
    blocks = owners * width // BLK
    me = owner_of()
    col = lax.axis_index("col")
    hits = child_map[lax.axis_index("grp")][None, :] == jnp.arange(blocks)[:, None]
    source = jnp.argmax(hits, axis=1)
    taken = jnp.take(strip.reshape(BLK, -1, BLK), source, axis=1)
    taken = jnp.where(jnp.any(hits, axis=1)[None, :, None], taken, 0.0)
    outgoing = taken.reshape(BLK, owners, width).transpose(1, 0, 2)
    incoming = lax.all_to_all(outgoing, OWNER, split_axis=0, concat_axis=0, tiled=True)
    ids = jnp.arange(owners)
    places = child_map[ids // n_row, ids % n_row * n_col + col] - col * row_blocks
    assembled = front.reshape(row_blocks, BLK, width).at[places].add(incoming).reshape(rows, width)
    rows_c = from_root(assembled, OWNER, 0)
    pivot = from_root(rows_c[:PIVOTS], "col", 0)
    part = lax.dynamic_slice_in_dim(rows_c, me * width % rows, width, 0)
    rows_o = jnp.zeros((width, width), jnp.float32)
    for c in range(n_col):
        low = c * rows // width
        sent = from_root(part, "col", c)
        rows_o = jnp.where((me >= low) & (me < low + rows // width), sent, rows_o)
    return assembled, rows_c, rows_o, pivot, []


def gather_pieces(front, strip, child_map):
    n_col = lax.axis_size("col")
    owners = lax.axis_size(OWNER)
    rows, width = front.shape
    row_blocks = rows // BLK
    part = BLK // owners
    blocks = owners * width // BLK
    me = owner_of()
    col = lax.axis_index("col")

    split = functools.partial(
        pl.pallas_call,
        in_specs=[SMEM, ANY],
        out_specs=[ANY] * owners,
        scratch_shapes=[pltpu.SMEM((blocks,), jnp.int32), pltpu.SemaphoreType.DMA((owners, width // BLK))],
    )
    panel_pieces = split(split_panel_kernel, out_shape=[f32(part, width)] * owners, name="split_panel")(child_map, strip)
    strip_pieces = split(split_strip_kernel, out_shape=[f32(BLK, width)] * owners, name="split_strip")(child_map, strip)

    front_parts = front.reshape(row_blocks, owners, part, width)
    fronts = [front_parts[:, 0]] + [
        lax.ppermute(front_parts[:, k], OWNER, [(0, k)]) for k in range(1, owners)
    ]
    strips = [panel_pieces[0]] + [exchange(panel_pieces[d], d) for d in range(1, owners)]
    mine = pl.pallas_call(
        sum_panel_kernel,
        out_shape=f32(row_blocks, part, width),
        in_specs=[SMEM] + [VMEM] * (2 * owners),
        out_specs=VMEM,
        compiler_params=PARAMS,
        name="sum_panel",
    )(child_map, *fronts, *strips)

    top = mine[: PIVOTS // BLK]
    tops = jnp.where(col == 0, top, 0.0)
    for c in range(1, n_col):
        tops = tops + lax.ppermute(top, "col", [(0, c)])
    gathered = [tops] + [exchange(tops, d) for d in range(1, owners)]
    order = jnp.arange(owners) ^ me
    pivot = jnp.stack(gathered)[order]
    pivot = pivot.transpose(1, 0, 2, 3).reshape(PIVOTS, width)

    arrived = [strip_pieces[0]] + [exchange(strip_pieces[d], d, True) for d in range(1, owners)]

    rows_c = lax.all_gather(mine, OWNER).transpose(1, 0, 2, 3).reshape(rows, width)
    root = me * width // rows
    own_part = lax.dynamic_slice_in_dim(rows_c, me * width % rows, width, 0)
    rows_o = jnp.where(col == root, own_part, 0.0)
    for e in range(1, n_col):
        perm = []
        for o in range(owners):
            c = o * width // rows
            perm.append((o * n_col + c, o * n_col + (c ^ e)))
        rows_o = rows_o + lax.ppermute(own_part, OWNER + ("col",), perm)

    return front, rows_c, rows_o, pivot, arrived


def body(front, child_blocks, child_map):
    owners = lax.axis_size(OWNER)
    rows, width = front.shape
    blocks = owners * width // BLK
    few = BLK % (owners * 8) == 0 and child_map.shape[1] == blocks
    gather = gather_pieces if few else gather_wide
    base, rows_c, rows_o, pivot, arrived = gather(front, child_blocks[0], child_map)
    lower = jnp.linalg.cholesky(pivot)
    inverse = lax.linalg.triangular_solve(
        lower, jnp.eye(PIVOTS, dtype=jnp.float32), left_side=True, lower=True
    )
    return pl.pallas_call(
        finish_kernel,
        out_shape=f32(rows, width),
        in_specs=[SMEM] + [VMEM] * (5 + len(arrived)),
        out_specs=VMEM,
        compiler_params=PARAMS,
        name="finish",
    )(child_map, base, rows_c, rows_o, inverse, lower, *arrived)


def solution(mesh):
    return jax.shard_map(
        body,
        mesh=mesh,
        in_specs=(P("col", ("grp", "row")), P("grp", ("row", "col"), None), P()),
        out_specs=P("col", ("grp", "row")),
        check_vma=False,
    )
```

time: 260 us -> 239 us (0.919)
  the two profiles are of different devices: /device:TPU:0 before, /device:TPU:18 now
where the time goes in v1:
time: 239 us
  starting transfers between devices  67.6 us (28%)
  other arithmetic  54.7 us (23%)
  Pallas kernels  43.9 us (18%)
  blocking collectives  31.6 us (13%)
  waiting for transfers between devices  29.2 us (12%)
  local copies, waits for them, and re-layouts  8.07 us (3%)
    ppermute x21, starting transfers between devices, exchange(): return lax.ppermute(value, OWNER, perm)  56.9 us
    another operation x6, other arithmetic, body(): lower = jnp.linalg.cholesky(pivot)  34 us
    pallas_call x1, Pallas kernels, gather_pieces(): split(split_strip_kernel, out_shape=[f32(BLK, width)] * owners, name='spl...  33.7 us
    all_gather x1, blocking collectives, gather_pieces(): lax.all_gather(mine, OWNER).transpose(1, 0, 2, 3).reshape(rows, width)  31.6 us
    ppermute x21, waiting for transfers between devices, exchange(): return lax.ppermute(value, OWNER, perm)  23.2 us
    another operation x4, other arithmetic, body(): lax.linalg.triangular_solve(lower, jnp.eye(PIVOTS, dtype=jnp.float32), le...  20.5 us
    pallas_call x1, Pallas kernels, gather_pieces(): split(split_panel_kernel, out_shape=[f32(part, width)] * owners, name='sp...  6.07 us
    ppermute x7, waiting for transfers between devices, gather_pieces(): lax.ppermute(front_parts[:, k], OWNER, [(0, k)])  6.07 us
  transfers between devices with their start and end apart: 34, of which 10 were waited for; matrix products, arithmetic and copies ran while one was open for 26% of the time, Pallas kernels for 14%

profile of v1, /device:TPU:18, one launch (start us, length us, event | category | flops | bytes accessed | tf_op | source)
XLA Modules:
  0.0 238.7 jit_solution(2975517459168165396)
XLA Ops:
  0.0 6.1 %split_panel.1 = (f32[16,256]{1,0:T(8,128)}, f32[16,256]{1,0:T(8,128)}, f32[16,256]{1,0:T(8,128)}, f32[16,256]{1,0:T(8,128)}, f32[16,256]{1,0:T(8,128)}, /*index...) custom-call(s32[2,16]{1,0:T(2,128)} %map_ref.7, f32[128,2048]{1,0:T(8,128)} %bitcast.94), custom_call_target="tpu_custom_call" | custom-call | tf_op jit(solution)/shard_map/split_panel/pallas_call | solution.py:193
  6.1 1.6 collective-permute-start.7
  7.7 0.3 collective-permute-start.8
  8.1 1.6 collective-permute-start.9
  9.6 1.5 collective-permute-start.10
  11.2 2.4 %collective-permute-start.11 = (f32[16,256]{1,0:T(8,128)}, f32[16,256]{1,0:T(8,128)S(1)}, u32[]{:S(2)}, u32[]{:S(2)}) collective-permute-start(f32[16,256]{1,0:T(8,128)} %get-tuple-element.26), channel_id=1, source_target_pairs={{0,20},{4,16},{8,28},{12,24},{16,4},{20,0},{24,12},{28,8},{1,21},{... | collective-permute-start | bytes 49160 | tf_op jit(solution)/shard_map/ppermute | solution.py:141
  13.7 0.6 copy-done.10
  14.3 0.4 collective-permute-start.12
  14.7 2.0 collective-permute-start.13
  16.8 0.7 collective-permute-start.6
  17.4 0.7 collective-permute-start.5
  18.2 33.7 %split_strip.1 = (f32[128,256]{1,0:T(8,128)}, f32[128,256]{1,0:T(8,128)}, f32[128,256]{1,0:T(8,128)}, f32[128,256]{1,0:T(8,128)}, f32[128,256]{1,0:T(8,128)}, /*...) custom-call(s32[2,16]{1,0:T(2,128)} %map_ref.7, f32[128,2048]{1,0:T(8,128)} %bitcast.95), custom_call_target="tpu_custom_call" | custom-call | tf_op jit(solution)/shard_map/split_strip/pallas_call | solution.py:194
  52.0 0.7 collective-permute-start.4
  52.7 0.7 collective-permute-start.3
  53.3 0.7 collective-permute-start.2
  54.0 1.3 collective-permute-start.1
  55.3 0.7 collective-permute-start
  56.0 4.8 %collective-permute-start.27 = (f32[128,256]{1,0:T(8,128)}, f32[128,256]{1,0:T(8,128)S(1)}, u32[]{:S(2)}, u32[]{:S(2)}) collective-permute-start(f32[128,256]{1,0:T(8,128)} %get-tuple-element.30), channel_id=1, source_target_pairs={{0,4},{8,12},{12,8},{16,20},{20,16},{24,28},{28,24},{1,5},{9,13},{... | collective-permute-start | bytes 393224 | tf_op jit(solution)/shard_map/ppermute | solution.py:141
  60.8 1.3 collective-permute-start.28
  62.1 6.1 %collective-permute-done.1.refs_2_ = f32[4,16,256]{2,1,0:T(8,128)S(1)} collective-permute-done((f32[4,16,256]{2,1,0:T(8,128)S(1)}, f32[4,16,256]{2,1,0:T(8,128)S(1)}, u32[]{:S(2)}, u32[]{:S(2)}) %collective-permute-start.1) | collective-permute-done | bytes 65568 | tf_op jit(solution)/shard_map/ppermute | solution.py:198
  68.2 0.7 copy-done.2
  68.9 0.6 sum_panel.1
  69.5 1.3 collective-permute-start.18
  70.8 0.7 collective-permute-start.17
  71.5 0.7 collective-permute-start.19
  72.2 31.6 %all-gather = f32[32,16,256]{2,1,0:T(8,128)S(1)} all-gather(f32[4,16,256]{2,1,0:T(8,128)S(1)} %sum_panel.1), channel_id=2, replica_groups=mesh['grp'=2,'row'=4,'col'=4] {'grp','row'}, dimensions={0}, use_global_device_ids=true | all-gather | bytes 589824 | tf_op jit(solution)/shard_map/all_gather | solution.py:221
  103.9 1.2 collective-permute-start.20
  105.1 0.7 collective-permute-start.15
  105.8 0.7 collective-permute-start.14
  106.5 1.6 collective-permute-done.20
  108.0 2.9 %collective-permute-start.21 = (f32[2,16,256]{2,1,0:T(8,128)S(1)}, f32[2,16,256]{2,1,0:T(8,128)S(1)}, u32[]{:S(2)}, u32[]{:S(2)}) collective-permute-start(f32[2,16,256]{2,1,0:T(8,128)S(1)} %get-tuple-element.56), channel_id=1, source_target_pairs={{0,8},{4,12},{8,0},{12,4},{16,24},{20,28},{24,16},{28,20},{1,9},{5... | collective-permute-start | bytes 98312 | tf_op jit(solution)/shard_map/ppermute | solution.py:141
  110.9 1.9 collective-permute-done.21
  112.9 1.5 collective-permute-start.22
  114.3 2.5 %collective-permute-done.22 = f32[2,16,256]{2,1,0:T(8,128)S(1)} collective-permute-done((f32[2,16,256]{2,1,0:T(8,128)S(1)}, f32[2,16,256]{2,1,0:T(8,128)S(1)}, u32[]{:S(2)}, u32[]{:S(2)}) %collective-permute-start.22) | collective-permute-done | bytes 32800 | tf_op jit(solution)/shard_map/ppermute | solution.py:141
  116.8 5.5 %collective-permute-start.23 = (f32[2,16,256]{2,1,0:T(8,128)S(1)}, f32[2,16,256]{2,1,0:T(8,128)S(1)}, u32[]{:S(2)}, u32[]{:S(2)}) collective-permute-start(f32[2,16,256]{2,1,0:T(8,128)S(1)} %get-tuple-element.56), channel_id=1, source_target_pairs={{0,16},{4,20},{8,24},{12,28},{16,0},{20,4},{24,8},{28,12},{1,17},{... | collective-permute-start | bytes 98312 | tf_op jit(solution)/shard_map/ppermute | solution.py:141
  122.2 1.9 collective-permute-done.23
  124.1 3.9 %collective-permute-start.24 = (f32[2,16,256]{2,1,0:T(8,128)S(1)}, f32[2,16,256]{2,1,0:T(8,128)S(1)}, u32[]{:S(2)}, u32[]{:S(2)}) collective-permute-start(f32[2,16,256]{2,1,0:T(8,128)S(1)} %get-tuple-element.56), channel_id=1, source_target_pairs={{0,20},{4,16},{8,28},{12,24},{16,4},{20,0},{24,12},{28,8},{1,21},{... | collective-permute-start | bytes 98312 | tf_op jit(solution)/shard_map/ppermute | solution.py:141
  128.0 1.9 collective-permute-done.24
  129.9 4.3 %collective-permute-start.25 = (f32[2,16,256]{2,1,0:T(8,128)S(1)}, f32[2,16,256]{2,1,0:T(8,128)S(1)}, u32[]{:S(2)}, u32[]{:S(2)}) collective-permute-start(f32[2,16,256]{2,1,0:T(8,128)S(1)} %get-tuple-element.56), channel_id=1, source_target_pairs={{0,24},{4,28},{8,16},{12,20},{16,8},{20,12},{24,0},{28,4},{1,25},{... | collective-permute-start | bytes 98312 | tf_op jit(solution)/shard_map/ppermute | solution.py:141
  134.3 1.9 collective-permute-done.25
  136.1 2.0 collective-permute-start.26
  138.1 2.8 %collective-permute-done.26 = f32[2,16,256]{2,1,0:T(8,128)S(1)} collective-permute-done((f32[2,16,256]{2,1,0:T(8,128)S(1)}, f32[2,16,256]{2,1,0:T(8,128)S(1)}, u32[]{:S(2)}, u32[]{:S(2)}) %collective-permute-start.26) | collective-permute-done | bytes 32800 | tf_op jit(solution)/shard_map/ppermute | solution.py:141
  141.0 1.5 collective-permute-start.16
  142.4 0.6 gather_fusion
  143.2 11.7 %cholesky.49 = f32[128,128]{1,0:T(8,128)S(1)} custom-call(f32[128,128]{1,0:T(8,128)S(1)} %cholesky.115), custom_call_target="Cholesky" | custom-call | tf_op jit(solution)/shard_map/jit(cholesky)/cholesky | solution.py:242
  155.0 9.8 %custom-call.14 = f32[1,128,128]{1,2,0:T(8,128)S(1)} custom-call(f32[1,128,128]{2,1,0:T(8,128)S(1)} %get-tuple-element.70), custom_call_target="InvertDiagBlocksLowerTriangular" | custom-call | tf_op jit(solution)/shard_map/jit(cholesky)/cholesky | solution.py:242
  165.3 11.7 %cholesky.103 = f32[128,128]{1,0:T(8,128)S(1)} custom-call(f32[128,128]{1,0:T(8,128)S(1)} %convolution_subtract_fusion.1), custom_call_target="Cholesky" | custom-call | tf_op jit(solution)/shard_map/jit(cholesky)/cholesky | solution.py:242
  177.1 0.7 compare_reduce_fusion
  179.2 5.5 %while.1 = (s32[]{:T(128)}, f32[256,256]{1,0:T(8,128)S(1)}, s32[2,2]{1,0:T(2,128)S(1)}, f32[2,128,128]{2,1,0:T(8,128)}, s32[]{:T(128)}) while((s32[]{:T(128)}, f32[256,256]{1,0:T(8,128)S(1)}, s32[2,2]{1,0:T(2,128)S(1)}, f32[2,128,128]{2,1,0:T(8,128)}, s32[]{:T(128)}) %tuple.32), condition=%wide.while_cond, body=%wide.while_body.sunk | while | flops 2 | bytes 132205 | solution.py:243
  179.4 0.6 fusion.16
  180.0 2.0 bitcast_dynamic-update-slice_fusion.10
  182.0 0.6 fusion.16
  182.7 2.0 bitcast_dynamic-update-slice_fusion.10
  184.7 20.5 %custom-call.15 = f32[2,128,128]{1,2,0:T(8,128)S(1)} custom-call(f32[2,128,128]{2,1,0:T(8,128)} %get-tuple-element.44), custom_call_target="InvertDiagBlocksLowerTriangular" | custom-call | tf_op jit(solution)/shard_map/triangular_solve | solution.py:243
  205.7 0.3 fusion.5
  206.1 0.5 copy-done.8
  206.6 3.1 %collective-permute-start.29 = (f32[128,256]{1,0:T(8,128)S(1)}, f32[128,256]{1,0:T(8,128)S(1)}, u32[]{:S(2)}, u32[]{:S(2)}) collective-permute-start(f32[128,256]{1,0:T(8,128)S(1)} %copy-done.8), channel_id=1, source_target_pairs={{0,12},{4,8},{8,4},{16,28},{20,24},{24,20},{28,16},{1,13},{5,9},{9... | collective-permute-start | bytes 393224 | tf_op jit(solution)/shard_map/ppermute | solution.py:141
  209.8 3.3 %collective-permute-start.30 = (f32[128,256]{1,0:T(8,128)S(1)}, f32[128,256]{1,0:T(8,128)S(1)}, u32[]{:S(2)}, u32[]{:S(2)}) collective-permute-start(f32[128,256]{1,0:T(8,128)S(1)} %copy-done.7), channel_id=1, source_target_pairs={{0,16},{4,20},{8,24},{12,28},{20,4},{24,8},{28,12},{1,17},{5,21},{... | collective-permute-start | bytes 393224 | tf_op jit(solution)/shard_map/ppermute | solution.py:141
  213.1 6.4 %collective-permute-start.31 = (f32[128,256]{1,0:T(8,128)S(1)}, f32[128,256]{1,0:T(8,128)S(1)}, u32[]{:S(2)}, u32[]{:S(2)}) collective-permute-start(f32[128,256]{1,0:T(8,128)S(1)} %copy-done.6), channel_id=1, source_target_pairs={{0,20},{4,16},{8,28},{12,24},{16,4},{24,12},{28,8},{1,21},{5,17},{... | collective-permute-start | bytes 393224 | tf_op jit(solution)/shard_map/ppermute | solution.py:141
  219.5 1.9 collective-permute-start.32
  221.5 5.0 %collective-permute-start.33 = (f32[128,256]{1,0:T(8,128)S(1)}, f32[128,256]{1,0:T(8,128)S(1)}, u32[]{:S(2)}, u32[]{:S(2)}) collective-permute-start(f32[128,256]{1,0:T(8,128)S(1)} %copy-done.4), channel_id=1, source_target_pairs={{0,28},{4,24},{8,20},{12,16},{16,12},{20,8},{24,4},{1,29},{5,25},{... | collective-permute-start | bytes 393224 | tf_op jit(solution)/shard_map/ppermute | solution.py:141
  226.6 2.8 %collective-permute-done.32.refs_6_ = f32[128,256]{1,0:T(8,128)S(1)} collective-permute-done((f32[128,256]{1,0:T(8,128)S(1)}, f32[128,256]{1,0:T(8,128)S(1)}, u32[]{:S(2)}, u32[]{:S(2)}) %collective-permute-start.32) | collective-permute-done | bytes 131104 | tf_op jit(solution)/shard_map/ppermute | solution.py:141
  229.4 5.9 %collective-permute-done.33.refs_7_ = f32[128,256]{1,0:T(8,128)S(1)} collective-permute-done((f32[128,256]{1,0:T(8,128)S(1)}, f32[128,256]{1,0:T(8,128)S(1)}, u32[]{:S(2)}, u32[]{:S(2)}) %collective-permute-start.33) | collective-permute-done | bytes 131104 | tf_op jit(solution)/shard_map/ppermute | solution.py:141
  235.3 3.4 %finish.1 = f32[512,256]{1,0:T(8,128)} custom-call(s32[2,16]{1,0:T(2,128)S(1)} %copy-done.2, f32[512,256]{1,0:T(8,128)S(1)} %copy-done, f32[512,256]{1,0:T(8,128)S(1)} %bitcast.92, f32[256,256]{1,0:T(8,128)S(1)} %add_add_fusion.rows_o_ref, f32[256,256]{1,0:T(8,128)S(1)} %pad_maximum_fusion.inv_ref, f32[256,256]{1,0:T(8,128)S(1)} %get-tuple-element.54.lower_ref, ...), custom_call_target="tpu_custom_call" | custom-call | tf_op jit(solution)/shard_map/finish/pallas_call | solution.py:246
  (77 shorter events, 1.8 us)
Async XLA Ops:
  0.0 13.6 %copy-start = (f32[512,256]{1,0:T(8,128)S(1)}, f32[512,256]{1,0:T(8,128)}, u32[]{:S(2)}) copy-start(f32[512,256]{1,0:T(8,128)} %front_ref.1) | copy-start | bytes 1572868
  6.1 7.6 %collective-permute-start.7 = (f32[16,256]{1,0:T(8,128)}, f32[16,256]{1,0:T(8,128)S(1)}, u32[]{:S(2)}, u32[]{:S(2)}) collective-permute-start(f32[16,256]{1,0:T(8,128)} %get-tuple-element.22), channel_id=1, source_target_pairs={{0,4},{4,0},{8,12},{12,8},{16,20},{20,16},{24,28},{28,24},{1,5},{5... | collective-permute-start | bytes 49160 | tf_op jit(solution)/shard_map/ppermute | solution.py:141
  7.7 7.0 %collective-permute-start.8 = (f32[16,256]{1,0:T(8,128)}, f32[16,256]{1,0:T(8,128)S(1)}, u32[]{:S(2)}, u32[]{:S(2)}) collective-permute-start(f32[16,256]{1,0:T(8,128)} %get-tuple-element.23), channel_id=1, source_target_pairs={{0,8},{4,12},{8,0},{12,4},{16,24},{20,28},{24,16},{28,20},{1,9},{5... | collective-permute-start | bytes 49160 | tf_op jit(solution)/shard_map/ppermute | solution.py:141
  8.1 8.7 %collective-permute-start.9 = (f32[16,256]{1,0:T(8,128)}, f32[16,256]{1,0:T(8,128)S(1)}, u32[]{:S(2)}, u32[]{:S(2)}) collective-permute-start(f32[16,256]{1,0:T(8,128)} %get-tuple-element.24), channel_id=1, source_target_pairs={{0,12},{4,8},{8,4},{12,0},{16,28},{20,24},{24,20},{28,16},{1,13},{... | collective-permute-start | bytes 49160 | tf_op jit(solution)/shard_map/ppermute | solution.py:141
  9.6 7.8 %collective-permute-start.10 = (f32[16,256]{1,0:T(8,128)}, f32[16,256]{1,0:T(8,128)S(1)}, u32[]{:S(2)}, u32[]{:S(2)}) collective-permute-start(f32[16,256]{1,0:T(8,128)} %get-tuple-element.25), channel_id=1, source_target_pairs={{0,16},{4,20},{8,24},{12,28},{16,0},{20,4},{24,8},{28,12},{1,17},{... | collective-permute-start | bytes 49160 | tf_op jit(solution)/shard_map/ppermute | solution.py:141
  11.2 40.8 %collective-permute-start.11 = (f32[16,256]{1,0:T(8,128)}, f32[16,256]{1,0:T(8,128)S(1)}, u32[]{:S(2)}, u32[]{:S(2)}) collective-permute-start(f32[16,256]{1,0:T(8,128)} %get-tuple-element.26), channel_id=1, source_target_pairs={{0,20},{4,16},{8,28},{12,24},{16,4},{20,0},{24,12},{28,8},{1,21},{... | collective-permute-start | bytes 49160 | tf_op jit(solution)/shard_map/ppermute | solution.py:141
  13.6 0.7 copy-start.10
  13.6 1.1 copy-start.9
  14.3 38.3 %collective-permute-start.12 = (f32[16,256]{1,0:T(8,128)S(1)}, f32[16,256]{1,0:T(8,128)S(1)}, u32[]{:S(2)}, u32[]{:S(2)}) collective-permute-start(f32[16,256]{1,0:T(8,128)S(1)} %copy-done.10), channel_id=1, source_target_pairs={{0,24},{4,28},{8,16},{12,20},{16,8},{20,12},{24,0},{28,4},{1,25},{... | collective-permute-start | bytes 49160 | tf_op jit(solution)/shard_map/ppermute | solution.py:141
  14.7 38.6 %collective-permute-start.13 = (f32[16,256]{1,0:T(8,128)S(1)}, f32[16,256]{1,0:T(8,128)S(1)}, u32[]{:S(2)}, u32[]{:S(2)}) collective-permute-start(f32[16,256]{1,0:T(8,128)S(1)} %copy-done.9), channel_id=1, source_target_pairs={{0,28},{4,24},{8,20},{12,16},{16,12},{20,8},{24,4},{28,0},{1,29},{... | collective-permute-start | bytes 49160 | tf_op jit(solution)/shard_map/ppermute | solution.py:141
  16.8 37.2 %collective-permute-start.6 = (f32[4,16,256]{2,1,0:T(8,128)S(1)}, f32[4,16,256]{2,1,0:T(8,128)S(1)}, u32[]{:S(2)}, u32[]{:S(2)}) collective-permute-start(f32[4,16,256]{2,1,0:T(8,128)S(1)} %get-tuple-element.59), channel_id=1, source_target_pairs={{0,28},{1,29},{2,30},{3,31}} | collective-permute-start | bytes 196616 | tf_op jit(solution)/shard_map/ppermute | solution.py:198
  17.4 37.9 %collective-permute-start.5 = (f32[4,16,256]{2,1,0:T(8,128)S(1)}, f32[4,16,256]{2,1,0:T(8,128)S(1)}, u32[]{:S(2)}, u32[]{:S(2)}) collective-permute-start(f32[4,16,256]{2,1,0:T(8,128)S(1)} %get-tuple-element.60), channel_id=1, source_target_pairs={{0,24},{1,25},{2,26},{3,27}} | collective-permute-start | bytes 196616 | tf_op jit(solution)/shard_map/ppermute | solution.py:198
  51.9 16.3 %copy-start.3 = (f32[16,256]{1,0:T(8,128)S(1)}, f32[16,256]{1,0:T(8,128)}, u32[]{:S(2)}) copy-start(f32[16,256]{1,0:T(8,128)} %get-tuple-element.21.refs_8_) | copy-start | bytes 49156
  52.0 4.0 %collective-permute-start.4 = (f32[4,16,256]{2,1,0:T(8,128)S(1)}, f32[4,16,256]{2,1,0:T(8,128)S(1)}, u32[]{:S(2)}, u32[]{:S(2)}) collective-permute-start(f32[4,16,256]{2,1,0:T(8,128)S(1)} %get-tuple-element.61), channel_id=1, source_target_pairs={{0,20},{1,21},{2,22},{3,23}} | collective-permute-start | bytes 196616 | tf_op jit(solution)/shard_map/ppermute | solution.py:198
  52.7 8.2 %collective-permute-start.3 = (f32[4,16,256]{2,1,0:T(8,128)S(1)}, f32[4,16,256]{2,1,0:T(8,128)S(1)}, u32[]{:S(2)}, u32[]{:S(2)}) collective-permute-start(f32[4,16,256]{2,1,0:T(8,128)S(1)} %get-tuple-element.62), channel_id=1, source_target_pairs={{0,16},{1,17},{2,18},{3,19}} | collective-permute-start | bytes 196616 | tf_op jit(solution)/shard_map/ppermute | solution.py:198
  53.3 8.8 %collective-permute-start.2 = (f32[4,16,256]{2,1,0:T(8,128)S(1)}, f32[4,16,256]{2,1,0:T(8,128)S(1)}, u32[]{:S(2)}, u32[]{:S(2)}) collective-permute-start(f32[4,16,256]{2,1,0:T(8,128)S(1)} %get-tuple-element.63), channel_id=1, source_target_pairs={{0,12},{1,13},{2,14},{3,15}} | collective-permute-start | bytes 196616 | tf_op jit(solution)/shard_map/ppermute | solution.py:198
  54.0 14.2 %collective-permute-start.1 = (f32[4,16,256]{2,1,0:T(8,128)S(1)}, f32[4,16,256]{2,1,0:T(8,128)S(1)}, u32[]{:S(2)}, u32[]{:S(2)}) collective-permute-start(f32[4,16,256]{2,1,0:T(8,128)S(1)} %get-tuple-element.64), channel_id=1, source_target_pairs={{0,8},{1,9},{2,10},{3,11}} | collective-permute-start | bytes 196616 | tf_op jit(solution)/shard_map/ppermute | solution.py:198
  55.3 12.9 %collective-permute-start = (f32[4,16,256]{2,1,0:T(8,128)S(1)}, f32[4,16,256]{2,1,0:T(8,128)S(1)}, u32[]{:S(2)}, u32[]{:S(2)}) collective-permute-start(f32[4,16,256]{2,1,0:T(8,128)S(1)} %get-tuple-element.65), channel_id=1, source_target_pairs={{0,4},{1,5},{2,6},{3,7}} | collective-permute-start | bytes 196616 | tf_op jit(solution)/shard_map/ppermute | solution.py:198
  56.0 150.1 %collective-permute-start.27 = (f32[128,256]{1,0:T(8,128)}, f32[128,256]{1,0:T(8,128)S(1)}, u32[]{:S(2)}, u32[]{:S(2)}) collective-permute-start(f32[128,256]{1,0:T(8,128)} %get-tuple-element.30), channel_id=1, source_target_pairs={{0,4},{8,12},{12,8},{16,20},{20,16},{24,28},{28,24},{1,5},{9,13},{... | collective-permute-start | bytes 393224 | tf_op jit(solution)/shard_map/ppermute | solution.py:141
  60.8 148.9 %collective-permute-start.28 = (f32[128,256]{1,0:T(8,128)}, f32[128,256]{1,0:T(8,128)S(1)}, u32[]{:S(2)}, u32[]{:S(2)}) collective-permute-start(f32[128,256]{1,0:T(8,128)} %get-tuple-element.31), channel_id=1, source_target_pairs={{0,8},{4,12},{12,4},{16,24},{20,28},{24,16},{28,20},{1,9},{5,13},{... | collective-permute-start | bytes 393224 | tf_op jit(solution)/shard_map/ppermute | solution.py:141
  68.2 0.7 copy-start.2
  69.5 34.3 %collective-permute-start.18 = (f32[2,16,256]{2,1,0:T(8,128)S(1)}, f32[2,16,256]{2,1,0:T(8,128)S(1)}, u32[]{:S(2)}, u32[]{:S(2)}) collective-permute-start(f32[2,16,256]{2,1,0:T(8,128)S(1)} %slice.100), channel_id=1, source_target_pairs={{0,2},{4,6},{8,10},{12,14},{16,18},{20,22},{24,26},{28,30}} | collective-permute-start | bytes 98312 | tf_op jit(solution)/shard_map/ppermute | solution.py:213
  70.8 33.0 %collective-permute-start.17 = (f32[2,16,256]{2,1,0:T(8,128)S(1)}, f32[2,16,256]{2,1,0:T(8,128)S(1)}, u32[]{:S(2)}, u32[]{:S(2)}) collective-permute-start(f32[2,16,256]{2,1,0:T(8,128)S(1)} %slice.100), channel_id=1, source_target_pairs={{0,1},{4,5},{8,9},{12,13},{16,17},{20,21},{24,25},{28,29}} | collective-permute-start | bytes 98312 | tf_op jit(solution)/shard_map/ppermute | solution.py:213
  71.5 32.4 %collective-permute-start.19 = (f32[2,16,256]{2,1,0:T(8,128)S(1)}, f32[2,16,256]{2,1,0:T(8,128)S(1)}, u32[]{:S(2)}, u32[]{:S(2)}) collective-permute-start(f32[2,16,256]{2,1,0:T(8,128)S(1)} %slice.100), channel_id=1, source_target_pairs={{0,3},{4,7},{8,11},{12,15},{16,19},{20,23},{24,27},{28,31}} | collective-permute-start | bytes 98312 | tf_op jit(solution)/shard_map/ppermute | solution.py:213
  103.9 4.2 %collective-permute-start.20 = (f32[2,16,256]{2,1,0:T(8,128)S(1)}, f32[2,16,256]{2,1,0:T(8,128)S(1)}, u32[]{:S(2)}, u32[]{:S(2)}) collective-permute-start(f32[2,16,256]{2,1,0:T(8,128)S(1)} %get-tuple-element.56), channel_id=1, source_target_pairs={{0,4},{4,0},{8,12},{12,8},{16,20},{20,16},{24,28},{28,24},{1,5},{5... | collective-permute-start | bytes 98312 | tf_op jit(solution)/shard_map/ppermute | solution.py:141
  105.1 107.9 %collective-permute-start.15 = (f32[256,256]{1,0:T(8,128)S(1)}, f32[256,256]{1,0:T(8,128)S(1)}, u32[]{:S(2)}, u32[]{:S(2)}) collective-permute-start(f32[256,256]{1,0:T(8,128)S(1)} %constant_dynamic-slice_fusion.1), channel_id=1, source_target_pairs={{0,2},{4,6},{9,11},{13,15},{18,16},{22,20},{27,25},{31,29}} | collective-permute-start | bytes 786440 | tf_op jit(solution)/shard_map/ppermute | solution.py:230
  105.8 113.7 %collective-permute-start.14 = (f32[256,256]{1,0:T(8,128)S(1)}, f32[256,256]{1,0:T(8,128)S(1)}, u32[]{:S(2)}, u32[]{:S(2)}) collective-permute-start(f32[256,256]{1,0:T(8,128)S(1)} %constant_dynamic-slice_fusion.1), channel_id=1, source_target_pairs={{0,1},{4,5},{9,8},{13,12},{18,19},{22,23},{27,26},{31,30}} | collective-permute-start | bytes 786440 | tf_op jit(solution)/shard_map/ppermute | solution.py:230
  108.0 4.8 %collective-permute-start.21 = (f32[2,16,256]{2,1,0:T(8,128)S(1)}, f32[2,16,256]{2,1,0:T(8,128)S(1)}, u32[]{:S(2)}, u32[]{:S(2)}) collective-permute-start(f32[2,16,256]{2,1,0:T(8,128)S(1)} %get-tuple-element.56), channel_id=1, source_target_pairs={{0,8},{4,12},{8,0},{12,4},{16,24},{20,28},{24,16},{28,20},{1,9},{5... | collective-permute-start | bytes 98312 | tf_op jit(solution)/shard_map/ppermute | solution.py:141
  112.9 3.9 %collective-permute-start.22 = (f32[2,16,256]{2,1,0:T(8,128)S(1)}, f32[2,16,256]{2,1,0:T(8,128)S(1)}, u32[]{:S(2)}, u32[]{:S(2)}) collective-permute-start(f32[2,16,256]{2,1,0:T(8,128)S(1)} %get-tuple-element.56), channel_id=1, source_target_pairs={{0,12},{4,8},{8,4},{12,0},{16,28},{20,24},{24,20},{28,16},{1,13},{... | collective-permute-start | bytes 98312 | tf_op jit(solution)/shard_map/ppermute | solution.py:141
  116.8 7.4 %collective-permute-start.23 = (f32[2,16,256]{2,1,0:T(8,128)S(1)}, f32[2,16,256]{2,1,0:T(8,128)S(1)}, u32[]{:S(2)}, u32[]{:S(2)}) collective-permute-start(f32[2,16,256]{2,1,0:T(8,128)S(1)} %get-tuple-element.56), channel_id=1, source_target_pairs={{0,16},{4,20},{8,24},{12,28},{16,0},{20,4},{24,8},{28,12},{1,17},{... | collective-permute-start | bytes 98312 | tf_op jit(solution)/shard_map/ppermute | solution.py:141
  124.1 5.8 %collective-permute-start.24 = (f32[2,16,256]{2,1,0:T(8,128)S(1)}, f32[2,16,256]{2,1,0:T(8,128)S(1)}, u32[]{:S(2)}, u32[]{:S(2)}) collective-permute-start(f32[2,16,256]{2,1,0:T(8,128)S(1)} %get-tuple-element.56), channel_id=1, source_target_pairs={{0,20},{4,16},{8,28},{12,24},{16,4},{20,0},{24,12},{28,8},{1,21},{... | collective-permute-start | bytes 98312 | tf_op jit(solution)/shard_map/ppermute | solution.py:141
  129.9 6.2 %collective-permute-start.25 = (f32[2,16,256]{2,1,0:T(8,128)S(1)}, f32[2,16,256]{2,1,0:T(8,128)S(1)}, u32[]{:S(2)}, u32[]{:S(2)}) collective-permute-start(f32[2,16,256]{2,1,0:T(8,128)S(1)} %get-tuple-element.56), channel_id=1, source_target_pairs={{0,24},{4,28},{8,16},{12,20},{16,8},{20,12},{24,0},{28,4},{1,25},{... | collective-permute-start | bytes 98312 | tf_op jit(solution)/shard_map/ppermute | solution.py:141
  136.1 4.8 %collective-permute-start.26 = (f32[2,16,256]{2,1,0:T(8,128)S(1)}, f32[2,16,256]{2,1,0:T(8,128)S(1)}, u32[]{:S(2)}, u32[]{:S(2)}) collective-permute-start(f32[2,16,256]{2,1,0:T(8,128)S(1)} %get-tuple-element.56), channel_id=1, source_target_pairs={{0,28},{4,24},{8,20},{12,16},{16,12},{20,8},{24,4},{28,0},{1,29},{... | collective-permute-start | bytes 98312 | tf_op jit(solution)/shard_map/ppermute | solution.py:141
  141.0 80.5 %collective-permute-start.16 = (f32[256,256]{1,0:T(8,128)S(1)}, f32[256,256]{1,0:T(8,128)S(1)}, u32[]{:S(2)}, u32[]{:S(2)}) collective-permute-start(f32[256,256]{1,0:T(8,128)S(1)} %constant_dynamic-slice_fusion.1), channel_id=1, source_target_pairs={{0,3},{4,7},{9,10},{13,14},{18,17},{22,21},{27,24},{31,28}} | collective-permute-start | bytes 786440 | tf_op jit(solution)/shard_map/ppermute | solution.py:230
  205.7 0.9 copy-start.8
  206.1 3.7 %copy-start.7 = (f32[128,256]{1,0:T(8,128)S(1)}, f32[128,256]{1,0:T(8,128)}, u32[]{:S(2)}) copy-start(f32[128,256]{1,0:T(8,128)} %get-tuple-element.33) | copy-start | bytes 393220
  206.1 7.0 %copy-start.6 = (f32[128,256]{1,0:T(8,128)S(1)}, f32[128,256]{1,0:T(8,128)}, u32[]{:S(2)}) copy-start(f32[128,256]{1,0:T(8,128)} %get-tuple-element.34) | copy-start | bytes 393220
  206.1 13.5 %copy-start.5 = (f32[128,256]{1,0:T(8,128)S(1)}, f32[128,256]{1,0:T(8,128)}, u32[]{:S(2)}) copy-start(f32[128,256]{1,0:T(8,128)} %get-tuple-element.35) | copy-start | bytes 393220
  206.1 15.4 %copy-start.4 = (f32[128,256]{1,0:T(8,128)S(1)}, f32[128,256]{1,0:T(8,128)}, u32[]{:S(2)}) copy-start(f32[128,256]{1,0:T(8,128)} %get-tuple-element.36) | copy-start | bytes 393220
  206.6 19.9 %collective-permute-start.29 = (f32[128,256]{1,0:T(8,128)S(1)}, f32[128,256]{1,0:T(8,128)S(1)}, u32[]{:S(2)}, u32[]{:S(2)}) collective-permute-start(f32[128,256]{1,0:T(8,128)S(1)} %copy-done.8), channel_id=1, source_target_pairs={{0,12},{4,8},{8,4},{16,28},{20,24},{24,20},{28,16},{1,13},{5,9},{9... | collective-permute-start | bytes 393224 | tf_op jit(solution)/shard_map/ppermute | solution.py:141
  209.8 16.8 %collective-permute-start.30 = (f32[128,256]{1,0:T(8,128)S(1)}, f32[128,256]{1,0:T(8,128)S(1)}, u32[]{:S(2)}, u32[]{:S(2)}) collective-permute-start(f32[128,256]{1,0:T(8,128)S(1)} %copy-done.7), channel_id=1, source_target_pairs={{0,16},{4,20},{8,24},{12,28},{20,4},{24,8},{28,12},{1,17},{5,21},{... | collective-permute-start | bytes 393224 | tf_op jit(solution)/shard_map/ppermute | solution.py:141
  213.1 13.5 %collective-permute-start.31 = (f32[128,256]{1,0:T(8,128)S(1)}, f32[128,256]{1,0:T(8,128)S(1)}, u32[]{:S(2)}, u32[]{:S(2)}) collective-permute-start(f32[128,256]{1,0:T(8,128)S(1)} %copy-done.6), channel_id=1, source_target_pairs={{0,20},{4,16},{8,28},{12,24},{16,4},{24,12},{28,8},{1,21},{5,17},{... | collective-permute-start | bytes 393224 | tf_op jit(solution)/shard_map/ppermute | solution.py:141
  219.5 9.8 %collective-permute-start.32 = (f32[128,256]{1,0:T(8,128)S(1)}, f32[128,256]{1,0:T(8,128)S(1)}, u32[]{:S(2)}, u32[]{:S(2)}) collective-permute-start(f32[128,256]{1,0:T(8,128)S(1)} %copy-done.5), channel_id=1, source_target_pairs={{0,24},{4,28},{8,16},{12,20},{16,8},{20,12},{28,4},{1,25},{5,29},{... | collective-permute-start | bytes 393224 | tf_op jit(solution)/shard_map/ppermute | solution.py:141
  221.5 13.8 %copy-start.1 = (f32[128,256]{1,0:T(8,128)S(1)}, f32[128,256]{1,0:T(8,128)}, u32[]{:S(2)}) copy-start(f32[128,256]{1,0:T(8,128)} %get-tuple-element.29.refs_0_) | copy-start | bytes 393220
  221.5 13.8 %collective-permute-start.33 = (f32[128,256]{1,0:T(8,128)S(1)}, f32[128,256]{1,0:T(8,128)S(1)}, u32[]{:S(2)}, u32[]{:S(2)}) collective-permute-start(f32[128,256]{1,0:T(8,128)S(1)} %copy-done.4), channel_id=1, source_target_pairs={{0,28},{4,24},{8,20},{12,16},{16,12},{20,8},{24,4},{1,29},{5,25},{... | collective-permute-start | bytes 393224 | tf_op jit(solution)/shard_map/ppermute | solution.py:141

commit v2 on v1

v2 whole, which is shorter than its diff:
```python
import jax
import jax.numpy as jnp
from jax import lax
from jax.experimental import pallas as pl
from jax.experimental.pallas import tpu as pltpu
from jax.sharding import PartitionSpec as P

BLK = 128
PIVOTS = 256
OWNER = ("grp", "row")
HIGHEST = lax.Precision.HIGHEST
SUB = 8
VMEM = pl.BlockSpec(memory_space=pltpu.VMEM)
SMEM = pl.BlockSpec(memory_space=pltpu.SMEM)
PARAMS = pltpu.CompilerParams(vmem_limit_bytes=48 * 1024 * 1024)


def f32(*shape):
    return jax.ShapeDtypeStruct(shape, jnp.float32)


def owner_of():
    return lax.axis_index("grp") * lax.axis_size("row") + lax.axis_index("row")


def dot(a, b, ca, cb):
    return lax.dot_general(
        a, b, (((ca,), (cb,)), ((), ())), precision=HIGHEST, preferred_element_type=jnp.float32
    )


def factor_small(cols):
    n = len(cols)
    d = [[cols[k][i] if i >= k else None for k in range(n)] for i in range(n)]
    low = [[None] * n for _ in range(n)]
    inv = [[None] * n for _ in range(n)]
    for k in range(n):
        root = lax.rsqrt(d[k][k])
        root = root * (1.5 - 0.5 * d[k][k] * root * root)
        inv[k][k] = root
        for i in range(k + 1, n):
            low[i][k] = d[i][k] * root
        for i in range(k + 1, n):
            for j in range(k + 1, i + 1):
                d[i][j] = d[i][j] - low[i][k] * low[j][k]
        for j in range(k):
            total = low[k][j] * inv[j][j]
            for m in range(j + 1, k):
                total = total + low[k][m] * inv[m][j]
            inv[k][j] = -root * total
    return inv


def factor_block(groups):
    count = len(groups)
    shape = (SUB, BLK)
    sub = lax.broadcasted_iota(jnp.int32, shape, 0)
    lane = lax.broadcasted_iota(jnp.int32, shape, 1)
    spread_row = lambda v, i: jnp.broadcast_to(v[i : i + 1, :], shape)
    spread_col = lambda v, c: jnp.broadcast_to(v[:, c : c + 1], shape)
    upper, inverse = [], []
    groups = list(groups)
    for b in range(count):
        base = SUB * b
        cur = groups[b]
        here = [spread_col(cur, base + k) for k in range(SUB)]
        inv = factor_small([[spread_row(here[k], i) for i in range(SUB)] for k in range(SUB)])
        inv_col = []
        for k in range(SUB):
            col = jnp.where(sub == k, inv[k][k], 0.0)
            for i in range(k + 1, SUB):
                col = jnp.where(sub == i, inv[i][k], col)
            inv_col.append(col)
        done = inv_col[0] * spread_row(cur, 0)
        for k in range(1, SUB):
            done = done + inv_col[k] * spread_row(cur, k)
        upper.append(jnp.where(lane >= base + sub, done, 0.0))
        kept = done
        for k in range(SUB):
            kept = jnp.where(lane == base + k, inv_col[k], kept)
        inverse.append(jnp.where(lane <= base + sub, kept, 0.0))
        if b + 1 == count:
            break
        inside = (lane >= base) & (lane < base + SUB)
        nxt = groups[b + 1]
        after = [spread_col(nxt, base + k) for k in range(SUB)]
        nxt = jnp.where(inside, 0.0, nxt)
        for i in range(SUB):
            low = after[0] * inv[i][0]
            for k in range(1, i + 1):
                low = low + after[k] * inv[i][k]
            nxt = nxt - low * spread_row(kept, i)
        groups[b + 1] = nxt
        if b + 2 < count:
            change = dot(done[:, base + 2 * SUB :], kept, 0, 0)
            for j in range(b + 2, count):
                at = SUB * (j - b - 2)
                groups[j] = jnp.where(inside, 0.0, groups[j]) - change[at : at + SUB]
    return upper, inverse


def factor_pivot(pivot_ref, upper_ref, inverse_ref):
    halves = pivot_ref.shape[0] // BLK
    assert halves == 2
    zero = jnp.zeros((BLK, BLK), jnp.float32)

    def run(h, source):
        rows = slice(h * BLK, (h + 1) * BLK)
        upper, inverse = factor_block([source[SUB * g : SUB * (g + 1)] for g in range(BLK // SUB)])
        for g in range(BLK // SUB):
            at = slice(h * BLK + SUB * g, h * BLK + SUB * (g + 1))
            upper_ref[at, rows] = upper[g]
            inverse_ref[at, rows] = inverse[g]

    run(0, pivot_ref[:BLK, :BLK])
    first = inverse_ref[:BLK, :BLK]
    side = dot(first, pivot_ref[:BLK, BLK:], 1, 0)
    upper_ref[:BLK, BLK:] = side
    upper_ref[BLK:, :BLK] = zero
    inverse_ref[:BLK, BLK:] = zero
    run(1, pivot_ref[BLK:, BLK:] - dot(side, side, 0, 0))
    second = inverse_ref[BLK:, BLK:]
    inverse_ref[BLK:, :BLK] = -dot(second, dot(side, first, 0, 0), 1, 0)


def split_kernel(map_ref, strip_ref, front_ref, *refs):
    top_ref, rest_ref, out_ref, inv_ref = refs
    owners, part = top_ref.shape[0], top_ref.shape[2]
    per = out_ref.shape[2] // BLK
    grp, row, col = (lax.axis_index(a) for a in ("grp", "row", "col"))
    n_row, n_col = lax.axis_size("row"), lax.axis_size("col")
    me = grp * n_row + row
    for q in range(map_ref.shape[1]):
        inv_ref[map_ref[grp, q]] = q
    for k in range(owners):
        for s in range(per):
            at = pl.multiple_of(inv_ref[k * per + s] * BLK, BLK)
            out_ref[k, :, s * BLK : (s + 1) * BLK] = strip_ref[:, pl.ds(at, BLK)]
    row_blocks = front_ref.shape[0] // BLK
    tops = top_ref.shape[1]
    mine = map_ref[grp, row * n_col + col] - col * row_blocks
    for k in range(owners):
        piece = out_ref[0, part * k : part * (k + 1), :]
        for b in range(row_blocks):
            at = b * BLK + part * k
            value = jnp.where(mine == b, piece, 0.0)
            value = value + jnp.where(me == 0, front_ref[at : at + part, :], 0.0)
            if b < tops:
                top_ref[k, b] = value
            else:
                rest_ref[k, b - tops] = value


def pivot_kernel(pieces_ref, upper_ref, inverse_ref, pivot_ref):
    owners, blocks, part, _ = pieces_ref.shape
    for b in range(blocks):
        for k in range(owners):
            at = b * BLK + part * k
            pivot_ref[at : at + part, :] = pieces_ref[k, b]
    factor_pivot(pivot_ref, upper_ref, inverse_ref)


def finish_kernel(map_ref, front_ref, rows_c_ref, rows_o_ref, upper_ref, inverse_ref, *refs):
    strips_ref, out_ref = (refs[0] if len(refs) == 2 else None), refs[-1]
    rows, width = out_ref.shape
    n_row, n_col = lax.axis_size("row"), lax.axis_size("col")
    col = lax.axis_index("col")
    me = owner_of()
    row_blocks = rows // BLK
    inv = inverse_ref[...]

    def solved(ref):
        if len(ref.shape) == 2:
            return dot(ref[...], inv, 1, 1)
        owners, blocks = ref.shape[:2]
        whole = jnp.concatenate([ref[k, b] for b in range(blocks) for k in range(owners)], axis=0)
        return dot(whole, inv, 1, 1)

    left = solved(rows_c_ref)

    @pl.when(me == 0)
    def _():
        out_ref[...] = left

        @pl.when(col == 0)
        def _():
            out_ref[:PIVOTS, :] = upper_ref[...].T

    @pl.when(me != 0)
    def _():
        right = solved(rows_o_ref)
        out_ref[...] = front_ref[...] - dot(left, right, 1, 1)
        if strips_ref is not None:
            for i in range(strips_ref.shape[0]):
                local = map_ref[i // n_row, i % n_row * n_col + col] - col * row_blocks
                start = pl.multiple_of(local * BLK, BLK)
                out_ref[pl.ds(start, BLK), :] += strips_ref[i]

        @pl.when(col == 0)
        def _():
            out_ref[:PIVOTS, :] = jnp.zeros((PIVOTS, width), jnp.float32)


def from_root(value, axis, root):
    mine = lax.axis_index(axis) == root
    return lax.psum(jnp.where(mine, value, jnp.zeros_like(value)), axis)


def gather_wide(front, strip, child_map):
    n_row, n_col = lax.axis_size("row"), lax.axis_size("col")
    owners = lax.axis_size(OWNER)
    rows, width = front.shape
    row_blocks = rows // BLK
    blocks = owners * width // BLK
    me = owner_of()
    col = lax.axis_index("col")
    hits = child_map[lax.axis_index("grp")][None, :] == jnp.arange(blocks)[:, None]
    source = jnp.argmax(hits, axis=1)
    taken = jnp.take(strip.reshape(BLK, -1, BLK), source, axis=1)
    taken = jnp.where(jnp.any(hits, axis=1)[None, :, None], taken, 0.0)
    outgoing = taken.reshape(BLK, owners, width).transpose(1, 0, 2)
    incoming = lax.all_to_all(outgoing, OWNER, split_axis=0, concat_axis=0, tiled=True)
    ids = jnp.arange(owners)
    places = child_map[ids // n_row, ids % n_row * n_col + col] - col * row_blocks
    assembled = front.reshape(row_blocks, BLK, width).at[places].add(incoming).reshape(rows, width)
    rows_c = from_root(assembled, OWNER, 0)
    pivot = from_root(rows_c[:PIVOTS], "col", 0)
    part = lax.dynamic_slice_in_dim(rows_c, me * width % rows, width, 0)
    rows_o = jnp.zeros((width, width), jnp.float32)
    for c in range(n_col):
        low = c * rows // width
        sent = from_root(part, "col", c)
        rows_o = jnp.where((me >= low) & (me < low + rows // width), sent, rows_o)
    return assembled, rows_c, rows_o, pivot.reshape(1, PIVOTS // BLK, BLK, width), []


def swap(pieces):
    return lax.all_to_all(pieces, OWNER, split_axis=0, concat_axis=0, tiled=True)


def spread(piece):
    return swap(jnp.broadcast_to(piece[None], (lax.axis_size(OWNER),) + piece.shape))


def gather_pieces(front, strip, child_map):
    n_col = lax.axis_size("col")
    owners = lax.axis_size(OWNER)
    rows, width = front.shape
    row_blocks = rows // BLK
    tops = PIVOTS // BLK
    part = BLK // owners
    me = owner_of()
    col = lax.axis_index("col")
    top, rest, strips = pl.pallas_call(
        split_kernel,
        out_shape=[f32(owners, tops, part, width), f32(owners, row_blocks - tops, part, width), f32(owners, BLK, width)],
        in_specs=[SMEM, VMEM, VMEM],
        out_specs=[VMEM] * 3,
        scratch_shapes=[pltpu.SMEM((child_map.shape[1],), jnp.int32)],
        compiler_params=PARAMS,
        name="split",
    )(child_map, strip, front)

    top = jnp.sum(swap(top), axis=0)
    pivot = jnp.where(col == 0, top, 0.0)
    for c in range(1, n_col):
        pivot = pivot + lax.ppermute(top, "col", [(0, c)])
    pivot = spread(pivot)
    rest = jnp.sum(swap(rest), axis=0)
    rows_c = spread(jnp.concatenate([top, rest], axis=0))
    strips = swap(strips)

    root = me * width // rows
    own_part = lax.dynamic_slice_in_dim(rows_c, me * width % rows // BLK, width // BLK, 1)
    rows_o = jnp.where(col == root, own_part, 0.0)
    for e in range(1, n_col):
        perm = []
        for o in range(owners):
            c = o * width // rows
            perm.append((o * n_col + c, o * n_col + (c ^ e)))
        rows_o = rows_o + lax.ppermute(own_part, OWNER + ("col",), perm)
    return front, rows_c, rows_o, pivot, [strips]


def body(front, child_blocks, child_map):
    owners = lax.axis_size(OWNER)
    rows, width = front.shape
    blocks = owners * width // BLK
    few = BLK % (owners * 8) == 0 and child_map.shape[1] == blocks
    gather = gather_pieces if few else gather_wide
    base, rows_c, rows_o, pivot, strips = gather(front, child_blocks[0], child_map)
    upper, inverse = pl.pallas_call(
        pivot_kernel,
        out_shape=[f32(PIVOTS, PIVOTS)] * 2,
        in_specs=[VMEM],
        out_specs=[VMEM] * 2,
        scratch_shapes=[pltpu.VMEM((PIVOTS, PIVOTS), jnp.float32)],
        compiler_params=PARAMS,
        cost_estimate=pl.CostEstimate(flops=20_000_000_000, bytes_accessed=1 << 20, transcendentals=0),
        name="pivot",
    )(pivot)
    return pl.pallas_call(
        finish_kernel,
        out_shape=f32(rows, width),
        in_specs=[SMEM] + [VMEM] * (5 + len(strips)),
        out_specs=VMEM,
        compiler_params=PARAMS,
        name="finish",
    )(child_map, base, rows_c, rows_o, upper, inverse, *strips)


def solution(mesh):
    return jax.shard_map(
        body,
        mesh=mesh,
        in_specs=(P("col", ("grp", "row")), P("grp", ("row", "col"), None), P()),
        out_specs=P("col", ("grp", "row")),
        check_vma=False,
    )
```

time: 239 us -> 95.4 us (0.40)
  the two profiles are of different devices: /device:TPU:18 before, /device:TPU:0 now
where the time goes in v2:
time: 95.4 us; the launch traced here: 94.6 us
  waiting for transfers between devices  30.8 us (32%)
  starting transfers between devices  26 us (27%)
  blocking collectives  16.8 us (18%)
  Pallas kernels  15.1 us (16%)
  local copies, waits for them, and re-layouts  4.56 us (5%)
  other arithmetic  1.16 us (1%)
    all_to_all x4, waiting for transfers between devices, swap(): lax.all_to_all(pieces, OWNER, split_axis=0, concat_axis=0, tiled=True)  30 us
    all_to_all x1, blocking collectives, swap(): lax.all_to_all(pieces, OWNER, split_axis=0, concat_axis=0, tiled=True)  16.8 us
    all_to_all x4, starting transfers between devices, swap(): lax.all_to_all(pieces, OWNER, split_axis=0, concat_axis=0, tiled=True)  13.9 us
    pallas_call x1, Pallas kernels, body(): pl.pallas_call(pivot_kernel, out_shape=[f32(PIVOTS, PIVOTS)] * 2, in_spec...  11.2 us
    ppermute x3, starting transfers between devices, gather_pieces(): rows_o = rows_o + lax.ppermute(own_part, OWNER + ('col',), perm)  6.74 us
    ppermute x3, starting transfers between devices, gather_pieces(): pivot = pivot + lax.ppermute(top, 'col', [(0, c)])  5.35 us
    unnamed x8, local copies, waits for them, and re-layouts  2.95 us
    pallas_call x1, Pallas kernels, body(): pl.pallas_call(finish_kernel, out_shape=f32(rows, width), in_specs=[SMEM]...  2.11 us
  transfers between devices with their start and end apart: 10, of which 6 were waited for; matrix products, arithmetic and copies ran while one was open for 1% of the time, Pallas kernels for 12%

profile of v2, /device:TPU:0, one launch (start us, length us, event | category | flops | bytes accessed | tf_op | source)
XLA Modules:
  0.0 94.6 jit_solution(1283056208257634629)
XLA Ops:
  0.0 0.0 copy-start.3
  0.0 0.7 copy-done.3
  0.7 0.0 copy-start
  0.7 1.0 %copy-done = f32[512,256]{1,0:T(8,128)S(1)} copy-done((f32[512,256]{1,0:T(8,128)S(1)}, f32[512,256]{1,0:T(8,128)}, u32[]{:S(2)}) %copy-start) | copy-done | bytes 524312
  1.7 0.0 copy-start.2
  1.7 1.2 %copy-done.2 = f32[1,128,2048]{2,1,0:T(8,128)S(1)} copy-done((f32[1,128,2048]{2,1,0:T(8,128)S(1)}, f32[1,128,2048]{2,1,0:T(8,128)}, u32[]{:S(2)}) %copy-start.2) | copy-done | bytes 1048600
  2.9 1.8 %split.1 = (f32[8,2,16,256]{3,2,1,0:T(8,128)S(1)}, f32[8,2,16,256]{3,2,1,0:T(8,128)}, f32[8,128,256]{2,1,0:T(8,128)}) custom-call(s32[2,16]{1,0:T(2,128)S(1)} %copy-done.3, f32[128,2048]{1,0:T(8,128)S(1)} %bitcast.1, f32[512,256]{1,0:T(8,128)S(1)} %copy-done), custom_call_target="tpu_custom_call" | custom-call | tf_op jit(solution)/shard_map/split/pallas_call | solution.py:254
  4.8 16.8 %all_to_all.25 = f32[8,2,16,256]{3,2,1,0:T(8,128)S(1)} all-to-all(f32[8,2,16,256]{3,2,1,0:T(8,128)S(1)} %get-tuple-element.10), channel_id=1, replica_groups=mesh['grp'=2,'row'=4,'col'=4] {'grp','row'}, dimensions={0} | all-to-all | bytes 524288 | tf_op jit(solution)/shard_map/all_to_all | solution.py:238
  21.6 3.4 %all-to-all-start.1 = ((f32[8,2,16,256]{3,2,1,0:T(8,128)}), f32[8,2,16,256]{3,2,1,0:T(8,128)S(1)}, u32[]{:S(2)}, u32[]{:S(2)}) async-start(f32[8,2,16,256]{3,2,1,0:T(8,128)} %get-tuple-element.11), calls=%async_computation.1 | async-start | bytes 524288 | tf_op jit(solution)/shard_map/all_to_all | solution.py:238
  25.1 8.6 %all-to-all-done.1 = f32[8,2,16,256]{3,2,1,0:T(8,128)S(1)} async-done(((f32[8,2,16,256]{3,2,1,0:T(8,128)}), f32[8,2,16,256]{3,2,1,0:T(8,128)S(1)}, u32[]{:S(2)}, u32[]{:S(2)}) %all-to-all-start.1) | async-done | bytes 262176 | tf_op jit(solution)/shard_map/all_to_all | solution.py:238
  33.7 0.9 broadcast_in_dim.20
  34.5 3.5 %all-to-all-start.2 = ((f32[8,4,16,256]{3,2,1,0:T(8,128)}), f32[8,4,16,256]{3,2,1,0:T(8,128)S(1)}, u32[]{:S(2)}, u32[]{:S(2)}) async-start(f32[8,4,16,256]{3,2,1,0:T(8,128)} %broadcast_in_dim.20), calls=%async_computation.2 | async-start | bytes 1048576 | tf_op jit(solution)/shard_map/all_to_all | solution.py:238
  38.0 1.3 %collective-permute-start.5 = (f32[2,16,256]{2,1,0:T(8,128)S(1)}, f32[2,16,256]{2,1,0:T(8,128)S(1)}, u32[]{:S(2)}, u32[]{:S(2)}) collective-permute-start(f32[2,16,256]{2,1,0:T(8,128)S(1)} %reduce_sum.18), channel_id=1, source_target_pairs={{0,3},{4,7},{8,11},{12,15},{16,19},{20,23},{24,27},{28,31}} | collective-permute-start | bytes 98312 | tf_op jit(solution)/shard_map/ppermute | solution.py:267
  39.3 2.8 %collective-permute-start.4 = (f32[2,16,256]{2,1,0:T(8,128)S(1)}, f32[2,16,256]{2,1,0:T(8,128)S(1)}, u32[]{:S(2)}, u32[]{:S(2)}) collective-permute-start(f32[2,16,256]{2,1,0:T(8,128)S(1)} %reduce_sum.18), channel_id=1, source_target_pairs={{0,2},{4,6},{8,10},{12,14},{16,18},{20,22},{24,26},{28,30}} | collective-permute-start | bytes 98312 | tf_op jit(solution)/shard_map/ppermute | solution.py:267
  42.1 1.3 %collective-permute-start.3 = (f32[2,16,256]{2,1,0:T(8,128)S(1)}, f32[2,16,256]{2,1,0:T(8,128)S(1)}, u32[]{:S(2)}, u32[]{:S(2)}) collective-permute-start(f32[2,16,256]{2,1,0:T(8,128)S(1)} %reduce_sum.18), channel_id=1, source_target_pairs={{0,1},{4,5},{8,9},{12,13},{16,17},{20,21},{24,25},{28,29}} | collective-permute-start | bytes 98312 | tf_op jit(solution)/shard_map/ppermute | solution.py:267
  43.4 0.0 collective-permute-done.5
  43.4 0.3 collective-permute-done.4
  43.7 0.6 collective-permute-done.3
  44.3 6.7 %all-to-all-done.2.rows_c_ref = f32[8,4,16,256]{3,2,1,0:T(8,128)S(1)} async-done(((f32[8,4,16,256]{3,2,1,0:T(8,128)}), f32[8,4,16,256]{3,2,1,0:T(8,128)S(1)}, u32[]{:S(2)}, u32[]{:S(2)}) %all-to-all-start.2) | async-done | bytes 524320 | tf_op jit(solution)/shard_map/all_to_all | solution.py:238
  50.9 0.7 broadcast_in_dim.23
  51.7 3.4 %all-to-all-start.3 = ((f32[8,2,16,256]{3,2,1,0:T(8,128)}), f32[8,2,16,256]{3,2,1,0:T(8,128)S(1)}, u32[]{:S(2)}, u32[]{:S(2)}) async-start(f32[8,2,16,256]{3,2,1,0:T(8,128)} %broadcast_in_dim.23), calls=%async_computation.3 | async-start | bytes 524288 | tf_op jit(solution)/shard_map/all_to_all | solution.py:238
  55.2 3.4 %collective-permute-start.1 = (f32[8,2,16,256]{3,2,1,0:T(8,128)S(1)}, f32[8,2,16,256]{3,2,1,0:T(8,128)S(1)}, u32[]{:S(2)}, u32[]{:S(2)}) collective-permute-start(f32[8,2,16,256]{3,2,1,0:T(8,128)S(1)} %constant_dynamic-slice_fusion), channel_id=1, source_target_pairs={{0,2},{4,6},{9,11},{13,15},{18,16},{22,20},{27,25},{31,29}} | collective-permute-start | bytes 786440 | tf_op jit(solution)/shard_map/ppermute | solution.py:281
  58.6 1.3 %collective-permute-start = (f32[8,2,16,256]{3,2,1,0:T(8,128)S(1)}, f32[8,2,16,256]{3,2,1,0:T(8,128)S(1)}, u32[]{:S(2)}, u32[]{:S(2)}) collective-permute-start(f32[8,2,16,256]{3,2,1,0:T(8,128)S(1)} %constant_dynamic-slice_fusion), channel_id=1, source_target_pairs={{0,1},{4,5},{9,8},{13,12},{18,19},{22,23},{27,26},{31,30}} | collective-permute-start | bytes 786440 | tf_op jit(solution)/shard_map/ppermute | solution.py:281
  59.9 2.0 %collective-permute-start.2 = (f32[8,2,16,256]{3,2,1,0:T(8,128)S(1)}, f32[8,2,16,256]{3,2,1,0:T(8,128)}, u32[]{:S(2)}, u32[]{:S(2)}) collective-permute-start(f32[8,2,16,256]{3,2,1,0:T(8,128)S(1)} %constant_dynamic-slice_fusion), channel_id=1, source_target_pairs={{0,3},{4,7},{9,10},{13,14},{18,17},{22,21},{27,24},{31,28}} | collective-permute-start | bytes 786440 | tf_op jit(solution)/shard_map/ppermute | solution.py:281
  61.9 1.7 %all-to-all-done.3.pieces_ref = f32[8,2,16,256]{3,2,1,0:T(8,128)S(1)} async-done(((f32[8,2,16,256]{3,2,1,0:T(8,128)}), f32[8,2,16,256]{3,2,1,0:T(8,128)S(1)}, u32[]{:S(2)}, u32[]{:S(2)}) %all-to-all-start.3) | async-done | bytes 262176 | tf_op jit(solution)/shard_map/all_to_all | solution.py:238
  63.6 3.6 %all-to-all-start.4 = ((f32[8,128,256]{2,1,0:T(8,128)}), f32[8,128,256]{2,1,0:T(8,128)S(1)}, u32[]{:S(2)}, u32[]{:S(2)}) async-start(f32[8,128,256]{2,1,0:T(8,128)} %get-tuple-element.14), calls=%async_computation.4 | async-start | bytes 2097152 | tf_op jit(solution)/shard_map/all_to_all | solution.py:238
  67.2 11.2 %pivot.1 = (f32[256,256]{1,0:T(8,128)S(1)}, f32[256,256]{1,0:T(8,128)S(1)}) custom-call(f32[8,2,16,256]{3,2,1,0:T(8,128)S(1)} %all-to-all-done.3.pieces_ref), custom_call_target="tpu_custom_call" | custom-call | flops 20000000000 | bytes 1048576 | tf_op jit(solution)/shard_map/pivot/pallas_call | solution.py:292
  78.4 0.0 copy-start.1
  78.4 0.0 collective-permute-done.1
  78.4 0.0 collective-permute-done
  78.4 0.0 collective-permute-done.2
  78.4 1.1 %add_add_fusion.rows_o_ref = f32[8,2,16,256]{3,2,1,0:T(8,128)S(1)} fusion(f32[8,2,16,256]{3,2,1,0:T(8,128)} %collective-permute-done.2, f32[8,2,16,256]{3,2,1,0:T(8,128)S(1)} %collective-permute-done.1, f32[8,2,16,256]{3,2,1,0:T(8,128)S(1)} %collective-permute-done, pred[]{:T(512)S(6)} %eq.8, f32[8,4,16,256]{3,2,1,0:T(8,128)S(1)} %all-to-all-done.2.rows_c_ref, ...), kind=kLoop, calls=%fused_computation | loop fusion | flops 262144 | bytes 1310725 | tf_op jit(solution)/shard_map/add | solution.py:281
  79.5 13.0 %all-to-all-done.4.refs_0_ = f32[8,128,256]{2,1,0:T(8,128)S(1)} async-done(((f32[8,128,256]{2,1,0:T(8,128)}), f32[8,128,256]{2,1,0:T(8,128)S(1)}, u32[]{:S(2)}, u32[]{:S(2)}) %all-to-all-start.4) | async-done | bytes 1048608 | tf_op jit(solution)/shard_map/all_to_all | solution.py:238
  92.5 0.0 copy-done.1
  92.5 2.1 %finish.1 = f32[512,256]{1,0:T(8,128)} custom-call(s32[2,16]{1,0:T(2,128)S(1)} %copy-done.3, f32[512,256]{1,0:T(8,128)S(1)} %copy-done.1, f32[8,4,16,256]{3,2,1,0:T(8,128)S(1)} %all-to-all-done.2.rows_c_ref, f32[8,2,16,256]{3,2,1,0:T(8,128)S(1)} %add_add_fusion.rows_o_ref, f32[256,256]{1,0:T(8,128)S(1)} %get-tuple-element.12.upper_ref, ...), custom_call_target="tpu_custom_call" | custom-call | tf_op jit(solution)/shard_map/finish/pallas_call | solution.py:302
  (5 shorter events, 0.1 us)
Async XLA Ops:
  0.0 0.7 copy-start.3
  0.7 1.0 %copy-start = (f32[512,256]{1,0:T(8,128)S(1)}, f32[512,256]{1,0:T(8,128)}, u32[]{:S(2)}) copy-start(f32[512,256]{1,0:T(8,128)} %front_ref.3) | copy-start | bytes 1572868
  1.7 1.2 %copy-start.2 = (f32[1,128,2048]{2,1,0:T(8,128)S(1)}, f32[1,128,2048]{2,1,0:T(8,128)}, u32[]{:S(2)}) copy-start(f32[1,128,2048]{2,1,0:T(8,128)} %param.4) | copy-start | bytes 3145732
  21.6 12.0 %all-to-all-start.1 = ((f32[8,2,16,256]{3,2,1,0:T(8,128)}), f32[8,2,16,256]{3,2,1,0:T(8,128)S(1)}, u32[]{:S(2)}, u32[]{:S(2)}) async-start(f32[8,2,16,256]{3,2,1,0:T(8,128)} %get-tuple-element.11), calls=%async_computation.1 | async-start | bytes 524288 | tf_op jit(solution)/shard_map/all_to_all | solution.py:238
  34.5 16.4 %all-to-all-start.2 = ((f32[8,4,16,256]{3,2,1,0:T(8,128)}), f32[8,4,16,256]{3,2,1,0:T(8,128)S(1)}, u32[]{:S(2)}, u32[]{:S(2)}) async-start(f32[8,4,16,256]{3,2,1,0:T(8,128)} %broadcast_in_dim.20), calls=%async_computation.2 | async-start | bytes 1048576 | tf_op jit(solution)/shard_map/all_to_all | solution.py:238
  38.0 5.4 %collective-permute-start.5 = (f32[2,16,256]{2,1,0:T(8,128)S(1)}, f32[2,16,256]{2,1,0:T(8,128)S(1)}, u32[]{:S(2)}, u32[]{:S(2)}) collective-permute-start(f32[2,16,256]{2,1,0:T(8,128)S(1)} %reduce_sum.18), channel_id=1, source_target_pairs={{0,3},{4,7},{8,11},{12,15},{16,19},{20,23},{24,27},{28,31}} | collective-permute-start | bytes 98312 | tf_op jit(solution)/shard_map/ppermute | solution.py:267
  39.3 4.4 %collective-permute-start.4 = (f32[2,16,256]{2,1,0:T(8,128)S(1)}, f32[2,16,256]{2,1,0:T(8,128)S(1)}, u32[]{:S(2)}, u32[]{:S(2)}) collective-permute-start(f32[2,16,256]{2,1,0:T(8,128)S(1)} %reduce_sum.18), channel_id=1, source_target_pairs={{0,2},{4,6},{8,10},{12,14},{16,18},{20,22},{24,26},{28,30}} | collective-permute-start | bytes 98312 | tf_op jit(solution)/shard_map/ppermute | solution.py:267
  42.1 2.1 %collective-permute-start.3 = (f32[2,16,256]{2,1,0:T(8,128)S(1)}, f32[2,16,256]{2,1,0:T(8,128)S(1)}, u32[]{:S(2)}, u32[]{:S(2)}) collective-permute-start(f32[2,16,256]{2,1,0:T(8,128)S(1)} %reduce_sum.18), channel_id=1, source_target_pairs={{0,1},{4,5},{8,9},{12,13},{16,17},{20,21},{24,25},{28,29}} | collective-permute-start | bytes 98312 | tf_op jit(solution)/shard_map/ppermute | solution.py:267
  51.7 11.9 %all-to-all-start.3 = ((f32[8,2,16,256]{3,2,1,0:T(8,128)}), f32[8,2,16,256]{3,2,1,0:T(8,128)S(1)}, u32[]{:S(2)}, u32[]{:S(2)}) async-start(f32[8,2,16,256]{3,2,1,0:T(8,128)} %broadcast_in_dim.23), calls=%async_computation.3 | async-start | bytes 524288 | tf_op jit(solution)/shard_map/all_to_all | solution.py:238
  55.2 23.2 %collective-permute-start.1 = (f32[8,2,16,256]{3,2,1,0:T(8,128)S(1)}, f32[8,2,16,256]{3,2,1,0:T(8,128)S(1)}, u32[]{:S(2)}, u32[]{:S(2)}) collective-permute-start(f32[8,2,16,256]{3,2,1,0:T(8,128)S(1)} %constant_dynamic-slice_fusion), channel_id=1, source_target_pairs={{0,2},{4,6},{9,11},{13,15},{18,16},{22,20},{27,25},{31,29}} | collective-permute-start | bytes 786440 | tf_op jit(solution)/shard_map/ppermute | solution.py:281
  58.6 19.8 %collective-permute-start = (f32[8,2,16,256]{3,2,1,0:T(8,128)S(1)}, f32[8,2,16,256]{3,2,1,0:T(8,128)S(1)}, u32[]{:S(2)}, u32[]{:S(2)}) collective-permute-start(f32[8,2,16,256]{3,2,1,0:T(8,128)S(1)} %constant_dynamic-slice_fusion), channel_id=1, source_target_pairs={{0,1},{4,5},{9,8},{13,12},{18,19},{22,23},{27,26},{31,30}} | collective-permute-start | bytes 786440 | tf_op jit(solution)/shard_map/ppermute | solution.py:281
  59.9 18.5 %collective-permute-start.2 = (f32[8,2,16,256]{3,2,1,0:T(8,128)S(1)}, f32[8,2,16,256]{3,2,1,0:T(8,128)}, u32[]{:S(2)}, u32[]{:S(2)}) collective-permute-start(f32[8,2,16,256]{3,2,1,0:T(8,128)S(1)} %constant_dynamic-slice_fusion), channel_id=1, source_target_pairs={{0,3},{4,7},{9,10},{13,14},{18,17},{22,21},{27,24},{31,28}} | collective-permute-start | bytes 786440 | tf_op jit(solution)/shard_map/ppermute | solution.py:281
  63.6 28.9 %all-to-all-start.4 = ((f32[8,128,256]{2,1,0:T(8,128)}), f32[8,128,256]{2,1,0:T(8,128)S(1)}, u32[]{:S(2)}, u32[]{:S(2)}) async-start(f32[8,128,256]{2,1,0:T(8,128)} %get-tuple-element.14), calls=%async_computation.4 | async-start | bytes 2097152 | tf_op jit(solution)/shard_map/all_to_all | solution.py:238
  78.4 14.2 %copy-start.1 = (f32[512,256]{1,0:T(8,128)S(1)}, f32[512,256]{1,0:T(8,128)}, u32[]{:S(2)}) copy-start(f32[512,256]{1,0:T(8,128)} %front_ref.3) | copy-start | bytes 1572868

commit v3 on v2

--- a/solution.py
+++ b/solution.py
@@ -1,3 +1,5 @@
+import functools
+
 import jax
 import jax.numpy as jnp
 from jax import lax
@@ -99,84 +101,83 @@
     return upper, inverse
 
 
-def factor_pivot(pivot_ref, upper_ref, inverse_ref):
-    halves = pivot_ref.shape[0] // BLK
-    assert halves == 2
-    zero = jnp.zeros((BLK, BLK), jnp.float32)
-
-    def run(h, source):
-        rows = slice(h * BLK, (h + 1) * BLK)
-        upper, inverse = factor_block([source[SUB * g : SUB * (g + 1)] for g in range(BLK // SUB)])
-        for g in range(BLK // SUB):
-            at = slice(h * BLK + SUB * g, h * BLK + SUB * (g + 1))
-            upper_ref[at, rows] = upper[g]
-            inverse_ref[at, rows] = inverse[g]
-
-    run(0, pivot_ref[:BLK, :BLK])
-    first = inverse_ref[:BLK, :BLK]
-    side = dot(first, pivot_ref[:BLK, BLK:], 1, 0)
-    upper_ref[:BLK, BLK:] = side
-    upper_ref[BLK:, :BLK] = zero
-    inverse_ref[:BLK, BLK:] = zero
-    run(1, pivot_ref[BLK:, BLK:] - dot(side, side, 0, 0))
-    second = inverse_ref[BLK:, BLK:]
-    inverse_ref[BLK:, :BLK] = -dot(second, dot(side, first, 0, 0), 1, 0)
-
-
-def split_kernel(map_ref, strip_ref, front_ref, *refs):
-    top_ref, rest_ref, out_ref, inv_ref = refs
-    owners, part = top_ref.shape[0], top_ref.shape[2]
-    per = out_ref.shape[2] // BLK
+def factor_half(source, upper_ref, inverse_ref):
+    upper, inverse = factor_block([source[SUB * g : SUB * (g + 1)] for g in range(BLK // SUB)])
+    for g in range(BLK // SUB):
+        at = slice(SUB * g, SUB * (g + 1))
+        upper_ref[at, :] = upper[g]
+        inverse_ref[at, :] = inverse[g]
+
+
+def first_half_kernel(pieces_ref, upper_ref, inverse_ref, side_ref, next_ref, pivot_ref):
+    owners, blocks, part, _ = pieces_ref.shape
+    for b in range(blocks):
+        for k in range(owners):
+            at = b * BLK + part * k
+            pivot_ref[at : at + part, :] = pieces_ref[k, b]
+    factor_half(pivot_ref[:BLK, :BLK], upper_ref, inverse_ref)
+    side = dot(inverse_ref[...], pivot_ref[:BLK, BLK:], 1, 0)
+    side_ref[...] = side
+    next_ref[...] = pivot_ref[BLK:, BLK:] - dot(side, side, 0, 0)
+
+
+def second_half_kernel(first_ref, side_ref, next_ref, upper_ref, inverse_ref, second_ref):
+    factor_half(next_ref[...], upper_ref, second_ref)
+    first, second = first_ref[...], second_ref[...]
+    inverse_ref[:BLK, :BLK] = first
+    inverse_ref[:BLK, BLK:] = jnp.zeros((BLK, BLK), jnp.float32)
+    inverse_ref[BLK:, BLK:] = second
+    inverse_ref[BLK:, :BLK] = -dot(second, dot(side_ref[...], first, 0, 0), 1, 0)
+
+
+def split_kernel(map_ref, strip_ref, front_ref, sums_ref, *refs):
+    outs, inv_ref = refs[:-1], refs[-1]
+    owners, row_blocks, part, width = sums_ref.shape
+    per = width // BLK
     grp, row, col = (lax.axis_index(a) for a in ("grp", "row", "col"))
     n_row, n_col = lax.axis_size("row"), lax.axis_size("col")
     me = grp * n_row + row
     for q in range(map_ref.shape[1]):
         inv_ref[map_ref[grp, q]] = q
-    for k in range(owners):
+    mine = map_ref[grp, row * n_col + col] - col * row_blocks
+    for s in range(per):
+        at = pl.multiple_of(inv_ref[s] * BLK, BLK)
+        lanes = slice(s * BLK, (s + 1) * BLK)
+        for k in range(owners):
+            piece = strip_ref[part * k : part * (k + 1), pl.ds(at, BLK)]
+            for b in range(row_blocks):
+                rows = slice(b * BLK + part * k, b * BLK + part * (k + 1))
+                value = jnp.where(mine == b, piece, 0.0)
+                sums_ref[k, b, :, lanes] = value + jnp.where(me == 0, front_ref[rows, lanes], 0.0)
+    for d in range(owners):
         for s in range(per):
-            at = pl.multiple_of(inv_ref[k * per + s] * BLK, BLK)
-            out_ref[k, :, s * BLK : (s + 1) * BLK] = strip_ref[:, pl.ds(at, BLK)]
-    row_blocks = front_ref.shape[0] // BLK
-    tops = top_ref.shape[1]
-    mine = map_ref[grp, row * n_col + col] - col * row_blocks
-    for k in range(owners):
-        piece = out_ref[0, part * k : part * (k + 1), :]
-        for b in range(row_blocks):
-            at = b * BLK + part * k
-            value = jnp.where(mine == b, piece, 0.0)
-            value = value + jnp.where(me == 0, front_ref[at : at + part, :], 0.0)
-            if b < tops:
-                top_ref[k, b] = value
-            else:
-                rest_ref[k, b - tops] = value
-
-
-def pivot_kernel(pieces_ref, upper_ref, inverse_ref, pivot_ref):
-    owners, blocks, part, _ = pieces_ref.shape
+            at = pl.multiple_of(inv_ref[(me ^ d) * per + s] * BLK, BLK)
+            outs[d][:, s * BLK : (s + 1) * BLK] = strip_ref[:, pl.ds(at, BLK)]
+
+
+def place_rows(target_ref, pieces_ref, grp):
+    n_row, blocks, part, _ = pieces_ref.shape
     for b in range(blocks):
-        for k in range(owners):
-            at = b * BLK + part * k
-            pivot_ref[at : at + part, :] = pieces_ref[k, b]
-    factor_pivot(pivot_ref, upper_ref, inverse_ref)
-
-
-def finish_kernel(map_ref, front_ref, rows_c_ref, rows_o_ref, upper_ref, inverse_ref, *refs):
-    strips_ref, out_ref = (refs[0] if len(refs) == 2 else None), refs[-1]
+        for r in range(n_row):
+            at = pl.multiple_of(b * BLK + (grp * n_row + r) * part, SUB)
+            target_ref[pl.ds(at, part), :] = pieces_ref[r, b]
+
+
+def finish_kernel(few, map_ref, front_ref, near_ref, far_ref, upper_ref, side_ref, upper2_ref, inverse_ref, *refs):
+    parts, strips, (out_ref, rows_c_ref, rows_o_ref) = refs[: few[0]], refs[few[0] : -3], refs[-3:]
     rows, width = out_ref.shape
     n_row, n_col = lax.axis_size("row"), lax.axis_size("col")
-    col = lax.axis_index("col")
+    grp, col = lax.axis_index("grp"), lax.axis_index("col")
     me = owner_of()
     row_blocks = rows // BLK
     inv = inverse_ref[...]
-
-    def solved(ref):
-        if len(ref.shape) == 2:
-            return dot(ref[...], inv, 1, 1)
-        owners, blocks = ref.shape[:2]
-        whole = jnp.concatenate([ref[k, b] for b in range(blocks) for k in range(owners)], axis=0)
-        return dot(whole, inv, 1, 1)
-
-    left = solved(rows_c_ref)
+    if few[1]:
+        place_rows(rows_c_ref, near_ref, grp)
+        place_rows(rows_c_ref, far_ref, 1 - grp)
+    else:
+        rows_c_ref[...] = near_ref[...]
+        rows_o_ref[...] = far_ref[...]
+    left = dot(rows_c_ref[...], inv, 1, 1)
 
     @pl.when(me == 0)
     def _():
@@ -184,17 +185,29 @@
 
         @pl.when(col == 0)
         def _():
-            out_ref[:PIVOTS, :] = upper_ref[...].T
+            out_ref[:BLK, :BLK] = upper_ref[...].T
+            out_ref[:BLK, BLK:] = jnp.zeros((BLK, BLK), jnp.float32)
+            out_ref[BLK:PIVOTS, :BLK] = side_ref[...].T
+            out_ref[BLK:PIVOTS, BLK:] = upper2_ref[...].T
 
     @pl.when(me != 0)
     def _():
-        right = solved(rows_o_ref)
+        distance = (me * width // rows) ^ col
+        for e, ref in enumerate(parts):
+
+            @pl.when(distance == e)
+            def _():
+                half = ref.shape[0] // 2
+                place_rows(rows_o_ref, ref.at[:half], grp)
+                place_rows(rows_o_ref, ref.at[half:], 1 - grp)
+
+        right = dot(rows_o_ref[...], inv, 1, 1)
         out_ref[...] = front_ref[...] - dot(left, right, 1, 1)
-        if strips_ref is not None:
-            for i in range(strips_ref.shape[0]):
-                local = map_ref[i // n_row, i % n_row * n_col + col] - col * row_blocks
-                start = pl.multiple_of(local * BLK, BLK)
-                out_ref[pl.ds(start, BLK), :] += strips_ref[i]
+        for d, ref in enumerate(strips):
+            source = me ^ d
+            local = map_ref[source // n_row, source % n_row * n_col + col] - col * row_blocks
+            start = pl.multiple_of(local * BLK, BLK)
+            out_ref[pl.ds(start, BLK), :] += ref[...]
 
         @pl.when(col == 0)
         def _():
@@ -231,15 +244,17 @@
         low = c * rows // width
         sent = from_root(part, "col", c)
         rows_o = jnp.where((me >= low) & (me < low + rows // width), sent, rows_o)
-    return assembled, rows_c, rows_o, pivot.reshape(1, PIVOTS // BLK, BLK, width), []
-
-
-def swap(pieces):
-    return lax.all_to_all(pieces, OWNER, split_axis=0, concat_axis=0, tiled=True)
-
-
-def spread(piece):
-    return swap(jnp.broadcast_to(piece[None], (lax.axis_size(OWNER),) + piece.shape))
+    return assembled, rows_c, rows_o, pivot.reshape(1, PIVOTS // BLK, BLK, width), [], []
+
+
+def spread(piece, axis):
+    copies = jnp.broadcast_to(piece[None], (lax.axis_size(axis),) + piece.shape)
+    return lax.all_to_all(copies, axis, split_axis=0, concat_axis=0, tiled=True)
+
+
+def exchange(value, d):
+    perm = [(i, i ^ d) for i in range(lax.axis_size(OWNER)) if i != d]
+    return lax.ppermute(value, OWNER, perm)
 
 
 def gather_pieces(front, strip, child_map):
@@ -251,62 +266,78 @@
     part = BLK // owners
     me = owner_of()
     col = lax.axis_index("col")
-    top, rest, strips = pl.pallas_call(
+    sums, *strips = pl.pallas_call(
         split_kernel,
-        out_shape=[f32(owners, tops, part, width), f32(owners, row_blocks - tops, part, width), f32(owners, BLK, width)],
+        out_shape=[f32(owners, row_blocks, part, width)] + [f32(BLK, width)] * owners,
         in_specs=[SMEM, VMEM, VMEM],
-        out_specs=[VMEM] * 3,
+        out_specs=[VMEM] * (1 + owners),
         scratch_shapes=[pltpu.SMEM((child_map.shape[1],), jnp.int32)],
         compiler_params=PARAMS,
         name="split",
     )(child_map, strip, front)
-
-    top = jnp.sum(swap(top), axis=0)
+    strips = [strips[0]] + [exchange(strips[d], d) for d in range(1, owners)]
+
+    mine = jnp.sum(lax.all_to_all(sums, OWNER, split_axis=0, concat_axis=0, tiled=True), axis=0)
+    top = mine[:tops]
     pivot = jnp.where(col == 0, top, 0.0)
     for c in range(1, n_col):
         pivot = pivot + lax.ppermute(top, "col", [(0, c)])
-    pivot = spread(pivot)
-    rest = jnp.sum(swap(rest), axis=0)
-    rows_c = spread(jnp.concatenate([top, rest], axis=0))
-    strips = swap(strips)
-
-    root = me * width // rows
-    own_part = lax.dynamic_slice_in_dim(rows_c, me * width % rows // BLK, width // BLK, 1)
-    rows_o = jnp.where(col == root, own_part, 0.0)
+    pivot = spread(pivot, OWNER)
+    mine, pivot = lax.optimization_barrier((mine, pivot))
+    near = spread(mine, "row")
+    far = lax.ppermute(near, "grp", [(0, 1), (1, 0)])
+
+    at = me * width % rows // BLK
+    cut = lambda v: lax.dynamic_slice_in_dim(v, at, width // BLK, 1)
+    own_part = jnp.concatenate([cut(near), cut(far)], axis=0)
+    parts = [own_part]
     for e in range(1, n_col):
         perm = []
         for o in range(owners):
             c = o * width // rows
             perm.append((o * n_col + c, o * n_col + (c ^ e)))
-        rows_o = rows_o + lax.ppermute(own_part, OWNER + ("col",), perm)
-    return front, rows_c, rows_o, pivot, [strips]
+        parts.append(lax.ppermute(own_part, OWNER + ("col",), perm))
+    return front, near, far, pivot, parts, strips
 
 
 def body(front, child_blocks, child_map):
     owners = lax.axis_size(OWNER)
     rows, width = front.shape
     blocks = owners * width // BLK
-    few = BLK % (owners * 8) == 0 and child_map.shape[1] == blocks
+    few = lax.axis_size("grp") == 2 and BLK % (owners * 8) == 0 and child_map.shape[1] == blocks
     gather = gather_pieces if few else gather_wide
-    base, rows_c, rows_o, pivot, strips = gather(front, child_blocks[0], child_map)
-    upper, inverse = pl.pallas_call(
-        pivot_kernel,
-        out_shape=[f32(PIVOTS, PIVOTS)] * 2,
+    base, near, far, pivot, parts, strips = gather(front, child_blocks[0], child_map)
+    half = f32(BLK, BLK)
+    cost = pl.CostEstimate(flops=8_000_000_000, bytes_accessed=1 << 18, transcendentals=0)
+    upper, first, side, rest = pl.pallas_call(
+        first_half_kernel,
+        out_shape=[half] * 4,
         in_specs=[VMEM],
-        out_specs=[VMEM] * 2,
+        out_specs=[VMEM] * 4,
         scratch_shapes=[pltpu.VMEM((PIVOTS, PIVOTS), jnp.float32)],
         compiler_params=PARAMS,
-        cost_estimate=pl.CostEstimate(flops=20_000_000_000, bytes_accessed=1 << 20, transcendentals=0),
-        name="pivot",
+        cost_estimate=cost,
+        name="pivot_first",
     )(pivot)
+    upper2, inverse = pl.pallas_call(
+        second_half_kernel,
+        out_shape=[half, f32(PIVOTS, PIVOTS)],
+        in_specs=[VMEM] * 3,
+        out_specs=[VMEM] * 2,
+        scratch_shapes=[pltpu.VMEM((BLK, BLK), jnp.float32)],
+        compiler_params=PARAMS,
+        cost_estimate=cost,
+        name="pivot_second",
+    )(first, side, rest)
     return pl.pallas_call(
-        finish_kernel,
+        functools.partial(finish_kernel, (len(parts), few)),
         out_shape=f32(rows, width),
-        in_specs=[SMEM] + [VMEM] * (5 + len(strips)),
+        in_specs=[SMEM] + [VMEM] * (7 + len(parts) + len(strips)),
         out_specs=VMEM,
+        scratch_shapes=[pltpu.VMEM((rows, width), jnp.float32), pltpu.VMEM((width, width), jnp.float32)],
         compiler_params=PARAMS,
         name="finish",
-    )(child_map, base, rows_c, rows_o, upper, inverse, *strips)
+    )(child_map, base, near, far, upper, side, upper2, inverse, *parts, *strips)
 
 
 def solution(mesh):

time: 95.4 us -> 97.4 us (1.021)
  waiting for transfers between devices: 30.8 us -> 2.22 us
  blocking collectives: 16.8 us -> 33.6 us
  starting transfers between devices: 26 us -> 42.1 us
  other arithmetic: 1.16 us -> 0.07 us
  Pallas kernels: 15.1 us -> 14.1 us
    all_to_all x4 -> x1, waiting for transfers between devices: 30 us -> 0.01 us  [spread(): return lax.all_to_all(copies, axis, split_axis=0, concat_axis=0, tiled=True)]
    ppermute x3 -> x11, starting transfers between devices: 6.74 us -> 32.7 us  [the longest x7 24.4 us: exchange(): return lax.ppermute(value, OWNER, perm)]
    all_to_all x1 -> x2, blocking collectives: 16.8 us -> 33.6 us  [the longest x1 22.5 us: gather_pieces(): lax.all_to_all(sums, OWNER, split_axis=0, concat_axis=0, tiled=True)]
    all_to_all x4 -> x1, starting transfers between devices: 13.9 us -> 3.41 us  [spread(): return lax.all_to_all(copies, axis, split_axis=0, concat_axis=0, tiled=True)]
    add x1 -> x0, other arithmetic: 1.1 us -> none  [gather_pieces(): rows_o = rows_o + lax.ppermute(own_part, OWNER + ('col',), perm)]
    pallas_call x3 -> x4, Pallas kernels: 15.1 us -> 14.1 us  [the longest x1 5.69 us: body(): pl.pallas_call(first_half_kernel, out_shape=[half] * 4, in_specs=[VMEM],...]
  transfers between devices with their start and end apart: 10 -> 15, of which waited for: 6 -> 2; matrix products, arithmetic and copies ran while one was open for 1% -> 0% of each run, Pallas kernels for 12% -> 12%
where the time goes in v3:
time: 97.4 us; the launch traced here: 96.1 us
  starting transfers between devices  42.1 us (43%)
  blocking collectives  33.6 us (34%)
  Pallas kernels  14.1 us (14%)
  local copies, waits for them, and re-layouts  3.74 us (4%)
  waiting for transfers between devices  2.22 us (2%)
    ppermute x7, starting transfers between devices, exchange(): return lax.ppermute(value, OWNER, perm)  24.4 us
    all_to_all x1, blocking collectives, gather_pieces(): lax.all_to_all(sums, OWNER, split_axis=0, concat_axis=0, tiled=True)  22.5 us
    all_to_all x1, blocking collectives, spread(): return lax.all_to_all(copies, axis, split_axis=0, concat_axis=0, tiled=True)  11.1 us
    ppermute x3, starting transfers between devices, gather_pieces(): parts.append(lax.ppermute(own_part, OWNER + ('col',), perm))  8.21 us
    ppermute x3, starting transfers between devices, gather_pieces(): pivot = pivot + lax.ppermute(top, 'col', [(0, c)])  5.98 us
    pallas_call x1, Pallas kernels, body(): pl.pallas_call(first_half_kernel, out_shape=[half] * 4, in_specs=[VMEM],...  5.69 us
    pallas_call x1, Pallas kernels, body(): pl.pallas_call(second_half_kernel, out_shape=[half, f32(PIVOTS, PIVOTS)],...  5.42 us
    all_to_all x1, starting transfers between devices, spread(): return lax.all_to_all(copies, axis, split_axis=0, concat_axis=0, tiled=True)  3.41 us
  transfers between devices with their start and end apart: 15, of which 2 were waited for; matrix products, arithmetic and copies ran while one was open for 0% of the time, Pallas kernels for 12%

profile of v3, /device:TPU:0, one launch (start us, length us, event | category | flops | bytes accessed | tf_op | source)
XLA Modules:
  0.0 96.1 jit_solution(9622852538314952776)
XLA Ops:
  0.0 0.0 copy-start.3
  0.0 0.7 copy-done.3
  0.7 0.0 copy-start
  0.7 1.0 %copy-done = f32[512,256]{1,0:T(8,128)S(1)} copy-done((f32[512,256]{1,0:T(8,128)S(1)}, f32[512,256]{1,0:T(8,128)}, u32[]{:S(2)}) %copy-start) | copy-done | bytes 524312
  1.7 0.0 copy-start.2
  1.7 1.2 %copy-done.2 = f32[1,128,2048]{2,1,0:T(8,128)S(1)} copy-done((f32[1,128,2048]{2,1,0:T(8,128)S(1)}, f32[1,128,2048]{2,1,0:T(8,128)}, u32[]{:S(2)}) %copy-start.2) | copy-done | bytes 1048600
  2.9 0.8 split.1
  3.7 22.5 %all_to_all.15 = f32[8,4,16,256]{3,2,1,0:T(8,128)S(1)} all-to-all(f32[8,4,16,256]{3,2,1,0:T(8,128)S(1)} %get-tuple-element.22), channel_id=1, replica_groups=mesh['grp'=2,'row'=4,'col'=4] {'grp','row'}, dimensions={0} | all-to-all | bytes 1048576 | tf_op jit(solution)/shard_map/all_to_all | solution.py:280
  26.3 3.4 %collective-permute-start.1 = (f32[2,16,256]{2,1,0:T(8,128)S(1)}, f32[2,16,256]{2,1,0:T(8,128)S(1)}, u32[]{:S(2)}, u32[]{:S(2)}) collective-permute-start(f32[2,16,256]{2,1,0:T(8,128)S(1)} %slice.4), channel_id=1, source_target_pairs={{0,2},{4,6},{8,10},{12,14},{16,18},{20,22},{24,26},{28,30}} | collective-permute-start | bytes 98312 | tf_op jit(solution)/shard_map/ppermute | solution.py:284
  29.7 1.3 %collective-permute-start = (f32[2,16,256]{2,1,0:T(8,128)S(1)}, f32[2,16,256]{2,1,0:T(8,128)S(1)}, u32[]{:S(2)}, u32[]{:S(2)}) collective-permute-start(f32[2,16,256]{2,1,0:T(8,128)S(1)} %slice.4), channel_id=1, source_target_pairs={{0,1},{4,5},{8,9},{12,13},{16,17},{20,21},{24,25},{28,29}} | collective-permute-start | bytes 98312 | tf_op jit(solution)/shard_map/ppermute | solution.py:284
  31.0 1.3 %collective-permute-start.2 = (f32[2,16,256]{2,1,0:T(8,128)S(1)}, f32[2,16,256]{2,1,0:T(8,128)S(1)}, u32[]{:S(2)}, u32[]{:S(2)}) collective-permute-start(f32[2,16,256]{2,1,0:T(8,128)S(1)} %slice.4), channel_id=1, source_target_pairs={{0,3},{4,7},{8,11},{12,15},{16,19},{20,23},{24,27},{28,31}} | collective-permute-start | bytes 98312 | tf_op jit(solution)/shard_map/ppermute | solution.py:284
  32.3 0.0 collective-permute-done.1
  32.3 0.0 collective-permute-done
  32.3 1.6 %collective-permute-done.2 = f32[2,16,256]{2,1,0:T(8,128)S(1)} collective-permute-done((f32[2,16,256]{2,1,0:T(8,128)S(1)}, f32[2,16,256]{2,1,0:T(8,128)S(1)}, u32[]{:S(2)}, u32[]{:S(2)}) %collective-permute-start.2) | collective-permute-done | bytes 32800 | tf_op jit(solution)/shard_map/ppermute | solution.py:284
  33.9 11.1 %all_to_all.16.pieces_ref = f32[8,2,16,256]{3,2,1,0:T(8,128)S(1)} all-to-all(f32[8,2,16,256]{3,2,1,0:T(8,128)S(1)} %broadcast_in_dim.9), channel_id=1, replica_groups=mesh['grp'=2,'row'=4,'col'=4] {'grp','row'}, dimensions={0} | all-to-all | bytes 524288 | tf_op jit(solution)/shard_map/all_to_all | solution.py:252
  45.0 0.7 broadcast_in_dim.18
  45.8 3.4 %all-to-all-start.2 = ((f32[4,4,16,256]{3,2,1,0:T(8,128)}), f32[4,4,16,256]{3,2,1,0:T(8,128)S(1)}, u32[]{:S(2)}, u32[]{:S(2)}) async-start(f32[4,4,16,256]{3,2,1,0:T(8,128)} %broadcast_in_dim.18), calls=%async_computation.2 | async-start | bytes 524288 | tf_op jit(solution)/shard_map/all_to_all | solution.py:252
  49.2 3.9 %collective-permute-start.7 = (f32[128,256]{1,0:T(8,128)S(1)}, f32[128,256]{1,0:T(8,128)S(1)}, u32[]{:S(2)}, u32[]{:S(2)}) collective-permute-start(f32[128,256]{1,0:T(8,128)S(1)} %get-tuple-element.32), channel_id=1, source_target_pairs={{0,4},{8,12},{12,8},{16,20},{20,16},{24,28},{28,24},{1,5},{9,13},{... | collective-permute-start | bytes 393224 | tf_op jit(solution)/shard_map/ppermute | solution.py:257
  53.1 4.3 %collective-permute-start.8 = (f32[128,256]{1,0:T(8,128)S(1)}, f32[128,256]{1,0:T(8,128)S(1)}, u32[]{:S(2)}, u32[]{:S(2)}) collective-permute-start(f32[128,256]{1,0:T(8,128)S(1)} %get-tuple-element.33), channel_id=1, source_target_pairs={{0,8},{4,12},{12,4},{16,24},{20,28},{24,16},{28,20},{1,9},{5,13},{... | collective-permute-start | bytes 393224 | tf_op jit(solution)/shard_map/ppermute | solution.py:257
  57.3 1.9 %collective-permute-start.9 = (f32[128,256]{1,0:T(8,128)S(1)}, f32[128,256]{1,0:T(8,128)S(1)}, u32[]{:S(2)}, u32[]{:S(2)}) collective-permute-start(f32[128,256]{1,0:T(8,128)S(1)} %get-tuple-element.34), channel_id=1, source_target_pairs={{0,12},{4,8},{8,4},{16,28},{20,24},{24,20},{28,16},{1,13},{5,9},{9... | collective-permute-start | bytes 393224 | tf_op jit(solution)/shard_map/ppermute | solution.py:257
  59.3 2.5 %collective-permute-start.10 = (f32[128,256]{1,0:T(8,128)S(1)}, f32[128,256]{1,0:T(8,128)S(1)}, u32[]{:S(2)}, u32[]{:S(2)}) collective-permute-start(f32[128,256]{1,0:T(8,128)S(1)} %get-tuple-element.35), channel_id=1, source_target_pairs={{0,16},{4,20},{8,24},{12,28},{20,4},{24,8},{28,12},{1,17},{5,21},{... | collective-permute-start | bytes 393224 | tf_op jit(solution)/shard_map/ppermute | solution.py:257
  61.8 0.0 all-to-all-done.2.near_ref
  61.8 0.1 collective-permute-start.3
  61.9 5.7 %pivot_first.1 = (f32[128,128]{1,0:T(8,128)S(1)}, f32[128,128]{1,0:T(8,128)S(1)}, f32[128,128]{1,0:T(8,128)S(1)}, f32[128,128]{1,0:T(8,128)S(1)}) custom-call(f32[8,2,16,256]{3,2,1,0:T(8,128)S(1)} %all_to_all.16.pieces_ref), custom_call_target="tpu_custom_call" | custom-call | flops 8000000000 | bytes 262144 | tf_op jit(solution)/shard_map/pivot_first/pallas_call | solution.py:312
  67.6 0.6 collective-permute-done.3.far_ref
  68.3 3.8 %collective-permute-start.11 = (f32[128,256]{1,0:T(8,128)S(1)}, f32[128,256]{1,0:T(8,128)S(1)}, u32[]{:S(2)}, u32[]{:S(2)}) collective-permute-start(f32[128,256]{1,0:T(8,128)S(1)} %get-tuple-element.36), channel_id=1, source_target_pairs={{0,20},{4,16},{8,28},{12,24},{16,4},{24,12},{28,8},{1,21},{5,17},{... | collective-permute-start | bytes 393224 | tf_op jit(solution)/shard_map/ppermute | solution.py:257
  72.1 0.0 collective-permute-done.7.refs_5_
  72.1 5.2 %collective-permute-start.12 = (f32[128,256]{1,0:T(8,128)S(1)}, f32[128,256]{1,0:T(8,128)S(1)}, u32[]{:S(2)}, u32[]{:S(2)}) collective-permute-start(f32[128,256]{1,0:T(8,128)S(1)} %get-tuple-element.37), channel_id=1, source_target_pairs={{0,24},{4,28},{8,16},{12,20},{16,8},{20,12},{28,4},{1,25},{5,29},{... | collective-permute-start | bytes 393224 | tf_op jit(solution)/shard_map/ppermute | solution.py:257
  77.4 0.0 collective-permute-done.8.refs_6_
  77.4 2.8 %collective-permute-start.13 = (f32[128,256]{1,0:T(8,128)S(1)}, f32[128,256]{1,0:T(8,128)S(1)}, u32[]{:S(2)}, u32[]{:S(2)}) collective-permute-start(f32[128,256]{1,0:T(8,128)S(1)} %get-tuple-element.38), channel_id=1, source_target_pairs={{0,28},{4,24},{8,20},{12,16},{16,12},{20,8},{24,4},{1,29},{5,25},{... | collective-permute-start | bytes 393224 | tf_op jit(solution)/shard_map/ppermute | solution.py:257
  80.2 0.0 collective-permute-done.9.refs_7_
  80.2 4.8 %collective-permute-start.6 = (f32[8,2,16,256]{3,2,1,0:T(8,128)S(1)}, f32[8,2,16,256]{3,2,1,0:T(8,128)S(1)}, u32[]{:S(2)}, u32[]{:S(2)}) collective-permute-start(f32[8,2,16,256]{3,2,1,0:T(8,128)S(1)} %pad_maximum_fusion.refs_0_), channel_id=1, source_target_pairs={{0,3},{4,7},{9,10},{13,14},{18,17},{22,21},{27,24},{31,28}} | collective-permute-start | bytes 786440 | tf_op jit(solution)/shard_map/ppermute | solution.py:299
  85.0 0.0 collective-permute-done.10.refs_8_
  85.1 2.1 %collective-permute-start.5 = (f32[8,2,16,256]{3,2,1,0:T(8,128)S(1)}, f32[8,2,16,256]{3,2,1,0:T(8,128)S(1)}, u32[]{:S(2)}, u32[]{:S(2)}) collective-permute-start(f32[8,2,16,256]{3,2,1,0:T(8,128)S(1)} %pad_maximum_fusion.refs_0_), channel_id=1, source_target_pairs={{0,2},{4,6},{9,11},{13,15},{18,16},{22,20},{27,25},{31,29}} | collective-permute-start | bytes 786440 | tf_op jit(solution)/shard_map/ppermute | solution.py:299
  87.1 0.0 collective-permute-done.11.refs_9_
  87.1 1.3 %collective-permute-start.4 = (f32[8,2,16,256]{3,2,1,0:T(8,128)S(1)}, f32[8,2,16,256]{3,2,1,0:T(8,128)S(1)}, u32[]{:S(2)}, u32[]{:S(2)}) collective-permute-start(f32[8,2,16,256]{3,2,1,0:T(8,128)S(1)} %pad_maximum_fusion.refs_0_), channel_id=1, source_target_pairs={{0,1},{4,5},{9,8},{13,12},{18,19},{22,23},{27,26},{31,30}} | collective-permute-start | bytes 786440 | tf_op jit(solution)/shard_map/ppermute | solution.py:299
  88.5 0.0 copy-start.1
  88.5 5.4 %pivot_second.1 = (f32[128,128]{1,0:T(8,128)S(1)}, f32[256,256]{1,0:T(8,128)S(1)}) custom-call(f32[128,128]{1,0:T(8,128)S(1)} %get-tuple-element.27.first_ref, f32[128,128]{1,0:T(8,128)S(1)} %get-tuple-element.26.side_ref, f32[128,128]{1,0:T(8,128)S(1)} %get-tuple-element.28.next_ref), custom_call_target="tpu_custom_call" | custom-call | flops 8000000000 | bytes 262144 | tf_op jit(solution)/shard_map/pivot_second/pallas_call | solution.py:322
  93.9 0.0 collective-permute-done.12.refs_10_
  93.9 0.0 collective-permute-done.13.refs_11_
  93.9 0.0 collective-permute-done.6.refs_3_
  93.9 0.0 collective-permute-done.5.refs_2_
  93.9 0.0 collective-permute-done.4.refs_1_
  94.0 0.0 copy-done.1
  94.0 2.2 %finish.1 = f32[512,256]{1,0:T(8,128)} custom-call(s32[2,16]{1,0:T(2,128)S(1)} %copy-done.3, f32[512,256]{1,0:T(8,128)S(1)} %copy-done.1, f32[4,4,16,256]{3,2,1,0:T(8,128)S(1)} %all-to-all-done.2.near_ref, f32[4,4,16,256]{3,2,1,0:T(8,128)S(1)} %collective-permute-done.3.far_ref, f32[128,128]{1,0:T(8,128)S(1)} %get-tuple-element.25.upper_ref, ...), custom_call_target="tpu_custom_call" | custom-call | tf_op jit(solution)/shard_map/finish/pallas_call | solution.py:332
  (7 shorter events, 0.1 us)
Async XLA Ops:
  0.0 0.7 copy-start.3
  0.7 1.0 %copy-start = (f32[512,256]{1,0:T(8,128)S(1)}, f32[512,256]{1,0:T(8,128)}, u32[]{:S(2)}) copy-start(f32[512,256]{1,0:T(8,128)} %front_ref.3) | copy-start | bytes 1572868
  1.7 1.2 %copy-start.2 = (f32[1,128,2048]{2,1,0:T(8,128)S(1)}, f32[1,128,2048]{2,1,0:T(8,128)}, u32[]{:S(2)}) copy-start(f32[1,128,2048]{2,1,0:T(8,128)} %param.4) | copy-start | bytes 3145732
  26.3 6.0 %collective-permute-start.1 = (f32[2,16,256]{2,1,0:T(8,128)S(1)}, f32[2,16,256]{2,1,0:T(8,128)S(1)}, u32[]{:S(2)}, u32[]{:S(2)}) collective-permute-start(f32[2,16,256]{2,1,0:T(8,128)S(1)} %slice.4), channel_id=1, source_target_pairs={{0,2},{4,6},{8,10},{12,14},{16,18},{20,22},{24,26},{28,30}} | collective-permute-start | bytes 98312 | tf_op jit(solution)/shard_map/ppermute | solution.py:284
  29.7 2.6 %collective-permute-start = (f32[2,16,256]{2,1,0:T(8,128)S(1)}, f32[2,16,256]{2,1,0:T(8,128)S(1)}, u32[]{:S(2)}, u32[]{:S(2)}) collective-permute-start(f32[2,16,256]{2,1,0:T(8,128)S(1)} %slice.4), channel_id=1, source_target_pairs={{0,1},{4,5},{8,9},{12,13},{16,17},{20,21},{24,25},{28,29}} | collective-permute-start | bytes 98312 | tf_op jit(solution)/shard_map/ppermute | solution.py:284
  31.0 2.9 %collective-permute-start.2 = (f32[2,16,256]{2,1,0:T(8,128)S(1)}, f32[2,16,256]{2,1,0:T(8,128)S(1)}, u32[]{:S(2)}, u32[]{:S(2)}) collective-permute-start(f32[2,16,256]{2,1,0:T(8,128)S(1)} %slice.4), channel_id=1, source_target_pairs={{0,3},{4,7},{8,11},{12,15},{16,19},{20,23},{24,27},{28,31}} | collective-permute-start | bytes 98312 | tf_op jit(solution)/shard_map/ppermute | solution.py:284
  45.8 16.1 %all-to-all-start.2 = ((f32[4,4,16,256]{3,2,1,0:T(8,128)}), f32[4,4,16,256]{3,2,1,0:T(8,128)S(1)}, u32[]{:S(2)}, u32[]{:S(2)}) async-start(f32[4,4,16,256]{3,2,1,0:T(8,128)} %broadcast_in_dim.18), calls=%async_computation.2 | async-start | bytes 524288 | tf_op jit(solution)/shard_map/all_to_all | solution.py:252
  49.2 23.0 %collective-permute-start.7 = (f32[128,256]{1,0:T(8,128)S(1)}, f32[128,256]{1,0:T(8,128)S(1)}, u32[]{:S(2)}, u32[]{:S(2)}) collective-permute-start(f32[128,256]{1,0:T(8,128)S(1)} %get-tuple-element.32), channel_id=1, source_target_pairs={{0,4},{8,12},{12,8},{16,20},{20,16},{24,28},{28,24},{1,5},{9,13},{... | collective-permute-start | bytes 393224 | tf_op jit(solution)/shard_map/ppermute | solution.py:257
  53.1 24.3 %collective-permute-start.8 = (f32[128,256]{1,0:T(8,128)S(1)}, f32[128,256]{1,0:T(8,128)S(1)}, u32[]{:S(2)}, u32[]{:S(2)}) collective-permute-start(f32[128,256]{1,0:T(8,128)S(1)} %get-tuple-element.33), channel_id=1, source_target_pairs={{0,8},{4,12},{12,4},{16,24},{20,28},{24,16},{28,20},{1,9},{5,13},{... | collective-permute-start | bytes 393224 | tf_op jit(solution)/shard_map/ppermute | solution.py:257
  57.3 22.9 %collective-permute-start.9 = (f32[128,256]{1,0:T(8,128)S(1)}, f32[128,256]{1,0:T(8,128)S(1)}, u32[]{:S(2)}, u32[]{:S(2)}) collective-permute-start(f32[128,256]{1,0:T(8,128)S(1)} %get-tuple-element.34), channel_id=1, source_target_pairs={{0,12},{4,8},{8,4},{16,28},{20,24},{24,20},{28,16},{1,13},{5,9},{9... | collective-permute-start | bytes 393224 | tf_op jit(solution)/shard_map/ppermute | solution.py:257
  59.3 25.8 %collective-permute-start.10 = (f32[128,256]{1,0:T(8,128)S(1)}, f32[128,256]{1,0:T(8,128)S(1)}, u32[]{:S(2)}, u32[]{:S(2)}) collective-permute-start(f32[128,256]{1,0:T(8,128)S(1)} %get-tuple-element.35), channel_id=1, source_target_pairs={{0,16},{4,20},{8,24},{12,28},{20,4},{24,8},{28,12},{1,17},{5,21},{... | collective-permute-start | bytes 393224 | tf_op jit(solution)/shard_map/ppermute | solution.py:257
  61.8 6.4 %collective-permute-start.3 = (f32[4,4,16,256]{3,2,1,0:T(8,128)S(1)}, f32[4,4,16,256]{3,2,1,0:T(8,128)S(1)}, u32[]{:S(2)}, u32[]{:S(2)}) collective-permute-start(f32[4,4,16,256]{3,2,1,0:T(8,128)S(1)} %all-to-all-done.2.near_ref), channel_id=1, source_target_pairs={{0,16},{16,0},{1,17},{17,1},{2,18},{18,2},{3,19},{19,3},{4,20},{20... | collective-permute-start | bytes 786440 | tf_op jit(solution)/shard_map/ppermute | solution.py:288
  68.3 18.9 %collective-permute-start.11 = (f32[128,256]{1,0:T(8,128)S(1)}, f32[128,256]{1,0:T(8,128)S(1)}, u32[]{:S(2)}, u32[]{:S(2)}) collective-permute-start(f32[128,256]{1,0:T(8,128)S(1)} %get-tuple-element.36), channel_id=1, source_target_pairs={{0,20},{4,16},{8,28},{12,24},{16,4},{24,12},{28,8},{1,21},{5,17},{... | collective-permute-start | bytes 393224 | tf_op jit(solution)/shard_map/ppermute | solution.py:257
  72.1 21.8 %collective-permute-start.12 = (f32[128,256]{1,0:T(8,128)S(1)}, f32[128,256]{1,0:T(8,128)S(1)}, u32[]{:S(2)}, u32[]{:S(2)}) collective-permute-start(f32[128,256]{1,0:T(8,128)S(1)} %get-tuple-element.37), channel_id=1, source_target_pairs={{0,24},{4,28},{8,16},{12,20},{16,8},{20,12},{28,4},{1,25},{5,29},{... | collective-permute-start | bytes 393224 | tf_op jit(solution)/shard_map/ppermute | solution.py:257
  77.4 16.5 %collective-permute-start.13 = (f32[128,256]{1,0:T(8,128)S(1)}, f32[128,256]{1,0:T(8,128)S(1)}, u32[]{:S(2)}, u32[]{:S(2)}) collective-permute-start(f32[128,256]{1,0:T(8,128)S(1)} %get-tuple-element.38), channel_id=1, source_target_pairs={{0,28},{4,24},{8,20},{12,16},{16,12},{20,8},{24,4},{1,29},{5,25},{... | collective-permute-start | bytes 393224 | tf_op jit(solution)/shard_map/ppermute | solution.py:257
  80.2 13.7 %collective-permute-start.6 = (f32[8,2,16,256]{3,2,1,0:T(8,128)S(1)}, f32[8,2,16,256]{3,2,1,0:T(8,128)S(1)}, u32[]{:S(2)}, u32[]{:S(2)}) collective-permute-start(f32[8,2,16,256]{3,2,1,0:T(8,128)S(1)} %pad_maximum_fusion.refs_0_), channel_id=1, source_target_pairs={{0,3},{4,7},{9,10},{13,14},{18,17},{22,21},{27,24},{31,28}} | collective-permute-start | bytes 786440 | tf_op jit(solution)/shard_map/ppermute | solution.py:299
  85.1 8.9 %collective-permute-start.5 = (f32[8,2,16,256]{3,2,1,0:T(8,128)S(1)}, f32[8,2,16,256]{3,2,1,0:T(8,128)S(1)}, u32[]{:S(2)}, u32[]{:S(2)}) collective-permute-start(f32[8,2,16,256]{3,2,1,0:T(8,128)S(1)} %pad_maximum_fusion.refs_0_), channel_id=1, source_target_pairs={{0,2},{4,6},{9,11},{13,15},{18,16},{22,20},{27,25},{31,29}} | collective-permute-start | bytes 786440 | tf_op jit(solution)/shard_map/ppermute | solution.py:299
  87.1 6.8 %collective-permute-start.4 = (f32[8,2,16,256]{3,2,1,0:T(8,128)S(1)}, f32[8,2,16,256]{3,2,1,0:T(8,128)S(1)}, u32[]{:S(2)}, u32[]{:S(2)}) collective-permute-start(f32[8,2,16,256]{3,2,1,0:T(8,128)S(1)} %pad_maximum_fusion.refs_0_), channel_id=1, source_target_pairs={{0,1},{4,5},{9,8},{13,12},{18,19},{22,23},{27,26},{31,30}} | collective-permute-start | bytes 786440 | tf_op jit(solution)/shard_map/ppermute | solution.py:299
  88.5 5.5 %copy-start.1 = (f32[512,256]{1,0:T(8,128)S(1)}, f32[512,256]{1,0:T(8,128)}, u32[]{:S(2)}) copy-start(f32[512,256]{1,0:T(8,128)} %front_ref.3) | copy-start | bytes 1572868

commit v4 on v3

--- a/solution.py
+++ b/solution.py
@@ -109,50 +109,77 @@
         inverse_ref[at, :] = inverse[g]
 
 
-def first_half_kernel(pieces_ref, upper_ref, inverse_ref, side_ref, next_ref, pivot_ref):
-    owners, blocks, part, _ = pieces_ref.shape
-    for b in range(blocks):
-        for k in range(owners):
-            at = b * BLK + part * k
-            pivot_ref[at : at + part, :] = pieces_ref[k, b]
-    factor_half(pivot_ref[:BLK, :BLK], upper_ref, inverse_ref)
-    side = dot(inverse_ref[...], pivot_ref[:BLK, BLK:], 1, 0)
-    side_ref[...] = side
-    next_ref[...] = pivot_ref[BLK:, BLK:] - dot(side, side, 0, 0)
-
-
-def second_half_kernel(first_ref, side_ref, next_ref, upper_ref, inverse_ref, second_ref):
-    factor_half(next_ref[...], upper_ref, second_ref)
-    first, second = first_ref[...], second_ref[...]
-    inverse_ref[:BLK, :BLK] = first
-    inverse_ref[:BLK, BLK:] = jnp.zeros((BLK, BLK), jnp.float32)
-    inverse_ref[BLK:, BLK:] = second
-    inverse_ref[BLK:, :BLK] = -dot(second, dot(side_ref[...], first, 0, 0), 1, 0)
-
-
-def split_kernel(map_ref, strip_ref, front_ref, sums_ref, *refs):
-    outs, inv_ref = refs[:-1], refs[-1]
+def on_root(few):
+    return lax.axis_index("col") == 0 if few else lax.axis_index("col") >= 0
+
+
+def first_half_kernel(few, *refs):
+    sources, (upper_ref, inverse_ref, side_ref, next_ref, pivot_ref) = refs[:-5], refs[-5:]
+
+    @pl.when(on_root(few))
+    def _():
+        if few:
+            grp = lax.axis_index("grp")
+            tops = PIVOTS // BLK
+            place_rows(pivot_ref, sources[0].at[:, :tops], grp)
+            place_rows(pivot_ref, sources[1].at[:, :tops], 1 - grp)
+        else:
+            pivot_ref[...] = sources[0][...]
+        factor_half(pivot_ref[:BLK, :BLK], upper_ref, inverse_ref)
+        side = dot(inverse_ref[...], pivot_ref[:BLK, BLK:], 1, 0)
+        side_ref[...] = side
+        next_ref[...] = pivot_ref[BLK:, BLK:] - dot(side, side, 0, 0)
+
+
+def second_half_kernel(few, first_ref, side_ref, next_ref, upper_ref, inverse_ref, second_ref):
+    @pl.when(on_root(few))
+    def _():
+        factor_half(next_ref[...], upper_ref, second_ref)
+        first, second = first_ref[...], second_ref[...]
+        inverse_ref[:BLK, :BLK] = first
+        inverse_ref[:BLK, BLK:] = jnp.zeros((BLK, BLK), jnp.float32)
+        inverse_ref[BLK:, BLK:] = second
+        inverse_ref[BLK:, :BLK] = -dot(second, dot(side_ref[...], first, 0, 0), 1, 0)
+
+
+def split_kernel(map_ref, strip_hbm, front_hbm, sums_ref, out_ref, inv_ref, strip_ref, front_ref, sems):
     owners, row_blocks, part, width = sums_ref.shape
     per = width // BLK
     grp, row, col = (lax.axis_index(a) for a in ("grp", "row", "col"))
     n_row, n_col = lax.axis_size("row"), lax.axis_size("col")
     me = grp * n_row + row
+    get_strip = pltpu.make_async_copy(strip_hbm, strip_ref, sems.at[0])
+    get_front = pltpu.make_async_copy(front_hbm, front_ref, sems.at[1])
+    get_strip.start()
+
+    @pl.when(me == 0)
+    def _():
+        get_front.start()
+
     for q in range(map_ref.shape[1]):
         inv_ref[map_ref[grp, q]] = q
     mine = map_ref[grp, row * n_col + col] - col * row_blocks
+    get_strip.wait()
     for s in range(per):
         at = pl.multiple_of(inv_ref[s] * BLK, BLK)
         lanes = slice(s * BLK, (s + 1) * BLK)
         for k in range(owners):
             piece = strip_ref[part * k : part * (k + 1), pl.ds(at, BLK)]
             for b in range(row_blocks):
-                rows = slice(b * BLK + part * k, b * BLK + part * (k + 1))
-                value = jnp.where(mine == b, piece, 0.0)
-                sums_ref[k, b, :, lanes] = value + jnp.where(me == 0, front_ref[rows, lanes], 0.0)
-    for d in range(owners):
+                sums_ref[k, b, :, lanes] = jnp.where(mine == b, piece, 0.0)
+
+    @pl.when(me == 0)
+    def _():
+        get_front.wait()
+        for k in range(owners):
+            for b in range(row_blocks):
+                at = b * BLK + part * k
+                sums_ref[k, b] = sums_ref[k, b] + front_ref[at : at + part, :]
+
+    for k in range(owners):
         for s in range(per):
-            at = pl.multiple_of(inv_ref[(me ^ d) * per + s] * BLK, BLK)
-            outs[d][:, s * BLK : (s + 1) * BLK] = strip_ref[:, pl.ds(at, BLK)]
+            at = pl.multiple_of(inv_ref[k * per + s] * BLK, BLK)
+            out_ref[k, :, s * BLK : (s + 1) * BLK] = strip_ref[:, pl.ds(at, BLK)]
 
 
 def place_rows(target_ref, pieces_ref, grp):
@@ -163,20 +190,39 @@
             target_ref[pl.ds(at, part), :] = pieces_ref[r, b]
 
 
-def finish_kernel(few, map_ref, front_ref, near_ref, far_ref, upper_ref, side_ref, upper2_ref, inverse_ref, *refs):
-    parts, strips, (out_ref, rows_c_ref, rows_o_ref) = refs[: few[0]], refs[few[0] : -3], refs[-3:]
+def choose(refs, distance, take):
+    for ref, here in zip(refs, (distance == 0, distance == 2, distance % 2 == 1)):
+        pl.when(here)(functools.partial(take, ref))
+
+
+def finish_kernel(few, map_ref, front_ref, near_ref, far_ref, upper_ref, side_ref, upper2_ref, *refs):
+    count = 3 if few else 1
+    inverses, parts, strips = refs[:count], refs[count : 2 * count], refs[2 * count : -4]
+    out_ref, rows_c_ref, rows_o_ref, inv_ref = refs[-4:]
     rows, width = out_ref.shape
     n_row, n_col = lax.axis_size("row"), lax.axis_size("col")
     grp, col = lax.axis_index("grp"), lax.axis_index("col")
     me = owner_of()
     row_blocks = rows // BLK
-    inv = inverse_ref[...]
-    if few[1]:
+
+    def take_inverse(ref):
+        inv_ref[...] = ref[...]
+
+    def take_part(ref):
+        half = ref.shape[0] // 2
+        place_rows(rows_o_ref, ref.at[:half], grp)
+        place_rows(rows_o_ref, ref.at[half:], 1 - grp)
+
+    if few:
+        choose(inverses, col, take_inverse)
+        choose(parts, (me * width // rows) ^ col, take_part)
         place_rows(rows_c_ref, near_ref, grp)
         place_rows(rows_c_ref, far_ref, 1 - grp)
     else:
+        inv_ref[...] = inverses[0][...]
+        rows_o_ref[...] = parts[0][...]
         rows_c_ref[...] = near_ref[...]
-        rows_o_ref[...] = far_ref[...]
+    inv = inv_ref[...]
     left = dot(rows_c_ref[...], inv, 1, 1)
 
     @pl.when(me == 0)
@@ -192,22 +238,13 @@
 
     @pl.when(me != 0)
     def _():
-        distance = (me * width // rows) ^ col
-        for e, ref in enumerate(parts):
-
-            @pl.when(distance == e)
-            def _():
-                half = ref.shape[0] // 2
-                place_rows(rows_o_ref, ref.at[:half], grp)
-                place_rows(rows_o_ref, ref.at[half:], 1 - grp)
-
         right = dot(rows_o_ref[...], inv, 1, 1)
         out_ref[...] = front_ref[...] - dot(left, right, 1, 1)
-        for d, ref in enumerate(strips):
-            source = me ^ d
-            local = map_ref[source // n_row, source % n_row * n_col + col] - col * row_blocks
-            start = pl.multiple_of(local * BLK, BLK)
-            out_ref[pl.ds(start, BLK), :] += ref[...]
+        for ref in strips:
+            for i in range(ref.shape[0]):
+                local = map_ref[i // n_row, i % n_row * n_col + col] - col * row_blocks
+                start = pl.multiple_of(local * BLK, BLK)
+                out_ref[pl.ds(start, BLK), :] += ref[i]
 
         @pl.when(col == 0)
         def _():
@@ -244,7 +281,7 @@
         low = c * rows // width
         sent = from_root(part, "col", c)
         rows_o = jnp.where((me >= low) & (me < low + rows // width), sent, rows_o)
-    return assembled, rows_c, rows_o, pivot.reshape(1, PIVOTS // BLK, BLK, width), [], []
+    return assembled, (rows_c, rows_c), [rows_o], [pivot], []
 
 
 def spread(piece, axis):
@@ -252,75 +289,72 @@
     return lax.all_to_all(copies, axis, split_axis=0, concat_axis=0, tiled=True)
 
 
-def exchange(value, d):
-    perm = [(i, i ^ d) for i in range(lax.axis_size(OWNER)) if i != d]
-    return lax.ppermute(value, OWNER, perm)
+def over_col(value, roots):
+    n_col = lax.axis_size("col")
+    axes = OWNER + ("col",)
+    cross = [(o * n_col + c, o * n_col + (c ^ 2)) for o, c in enumerate(roots)]
+    over_x = lax.ppermute(value, axes, cross)
+    held = jnp.where(lax.axis_index("col") == jnp.array(roots)[owner_of()], value, over_x)
+    other = [(o * n_col + (c ^ e), o * n_col + (c ^ e ^ 1)) for o, c in enumerate(roots) for e in (0, 2)]
+    return [value, over_x, lax.ppermute(held, axes, other)]
 
 
 def gather_pieces(front, strip, child_map):
-    n_col = lax.axis_size("col")
     owners = lax.axis_size(OWNER)
     rows, width = front.shape
     row_blocks = rows // BLK
-    tops = PIVOTS // BLK
     part = BLK // owners
     me = owner_of()
-    col = lax.axis_index("col")
-    sums, *strips = pl.pallas_call(
+    any_space = pl.BlockSpec(memory_space=pl.ANY)
+    sums, strips = pl.pallas_call(
         split_kernel,
-        out_shape=[f32(owners, row_blocks, part, width)] + [f32(BLK, width)] * owners,
-        in_specs=[SMEM, VMEM, VMEM],
-        out_specs=[VMEM] * (1 + owners),
-        scratch_shapes=[pltpu.SMEM((child_map.shape[1],), jnp.int32)],
+        out_shape=[f32(owners, row_blocks, part, width), f32(owners, BLK, width)],
+        in_specs=[SMEM, any_space, any_space],
+        out_specs=[VMEM] * 2,
+        scratch_shapes=[
+            pltpu.SMEM((child_map.shape[1],), jnp.int32),
+            pltpu.VMEM(strip.shape, jnp.float32),
+            pltpu.VMEM(front.shape, jnp.float32),
+            pltpu.SemaphoreType.DMA((2,)),
+        ],
         compiler_params=PARAMS,
         name="split",
     )(child_map, strip, front)
-    strips = [strips[0]] + [exchange(strips[d], d) for d in range(1, owners)]
-
     mine = jnp.sum(lax.all_to_all(sums, OWNER, split_axis=0, concat_axis=0, tiled=True), axis=0)
-    top = mine[:tops]
-    pivot = jnp.where(col == 0, top, 0.0)
-    for c in range(1, n_col):
-        pivot = pivot + lax.ppermute(top, "col", [(0, c)])
-    pivot = spread(pivot, OWNER)
-    mine, pivot = lax.optimization_barrier((mine, pivot))
     near = spread(mine, "row")
+    strips, near = lax.optimization_barrier((strips, near))
+    strips = lax.all_to_all(strips, OWNER, split_axis=0, concat_axis=0, tiled=True)
     far = lax.ppermute(near, "grp", [(0, 1), (1, 0)])
 
     at = me * width % rows // BLK
     cut = lambda v: lax.dynamic_slice_in_dim(v, at, width // BLK, 1)
     own_part = jnp.concatenate([cut(near), cut(far)], axis=0)
-    parts = [own_part]
-    for e in range(1, n_col):
-        perm = []
-        for o in range(owners):
-            c = o * width // rows
-            perm.append((o * n_col + c, o * n_col + (c ^ e)))
-        parts.append(lax.ppermute(own_part, OWNER + ("col",), perm))
-    return front, near, far, pivot, parts, strips
+    parts = over_col(own_part, [o * width // rows for o in range(owners)])
+    return front, (near, far), parts, [near, far], [strips]
 
 
 def body(front, child_blocks, child_map):
     owners = lax.axis_size(OWNER)
     rows, width = front.shape
     blocks = owners * width // BLK
-    few = lax.axis_size("grp") == 2 and BLK % (owners * 8) == 0 and child_map.shape[1] == blocks
+    few = lax.axis_size("grp") == 2 and lax.axis_size("col") == 4
+    few = few and BLK % (owners * 8) == 0 and child_map.shape[1] == blocks
     gather = gather_pieces if few else gather_wide
-    base, near, far, pivot, parts, strips = gather(front, child_blocks[0], child_map)
+    base, panel, parts, pivot, strips = gather(front, child_blocks[0], child_map)
     half = f32(BLK, BLK)
     cost = pl.CostEstimate(flops=8_000_000_000, bytes_accessed=1 << 18, transcendentals=0)
     upper, first, side, rest = pl.pallas_call(
-        first_half_kernel,
+        functools.partial(first_half_kernel, few),
         out_shape=[half] * 4,
-        in_specs=[VMEM],
+        in_specs=[VMEM] * len(pivot),
         out_specs=[VMEM] * 4,
         scratch_shapes=[pltpu.VMEM((PIVOTS, PIVOTS), jnp.float32)],
         compiler_params=PARAMS,
         cost_estimate=cost,
         name="pivot_first",
-    )(pivot)
+    )(*pivot)
     upper2, inverse = pl.pallas_call(
-        second_half_kernel,
+        functools.partial(second_half_kernel, few),
         out_shape=[half, f32(PIVOTS, PIVOTS)],
         in_specs=[VMEM] * 3,
         out_specs=[VMEM] * 2,
@@ -329,15 +363,16 @@
         cost_estimate=cost,
         name="pivot_second",
     )(first, side, rest)
+    inverses = over_col(inverse, [0] * owners) if few else [inverse]
     return pl.pallas_call(
-        functools.partial(finish_kernel, (len(parts), few)),
+        functools.partial(finish_kernel, few),
         out_shape=f32(rows, width),
-        in_specs=[SMEM] + [VMEM] * (7 + len(parts) + len(strips)),
+        in_specs=[SMEM] + [VMEM] * (6 + len(inverses) + len(parts) + len(strips)),
         out_specs=VMEM,
-        scratch_shapes=[pltpu.VMEM((rows, width), jnp.float32), pltpu.VMEM((width, width), jnp.float32)],
+        scratch_shapes=[pltpu.VMEM((n, width), jnp.float32) for n in (rows, width, PIVOTS)],
         compiler_params=PARAMS,
         name="finish",
-    )(child_map, base, near, far, upper, side, upper2, inverse, *parts, *strips)
+    )(child_map, base, *panel, upper, side, upper2, *inverses, *parts, *strips)
 
 
 def solution(mesh):

time: 97.4 us -> 72.8 us (0.75)
  starting transfers between devices: 42.1 us -> 11.9 us
  local copies, waits for them, and re-layouts: 3.74 us -> 7.33 us
  waiting for transfers between devices: 2.22 us -> 4.03 us
  Pallas kernels: 14.1 us -> 15.3 us
    ppermute x13 -> x4, starting transfers between devices: 38.6 us -> 7.45 us  [the longest x2 4.7 us: over_col(): over_x = lax.ppermute(value, axes, cross)]
    unnamed x8 -> x18, local copies, waits for them, and re-layouts: 2.95 us -> 6.71 us
    ppermute x1, waiting for transfers between devices: 0.63 us -> 2.46 us  [gather_pieces(): far = lax.ppermute(near, 'grp', [(0, 1), (1, 0)])]
    pallas_call x1, Pallas kernels: 0.79 us -> 1.93 us  [gather_pieces(): pl.pallas_call(split_kernel, out_shape=[f32(owners, row_blocks, part, wid...]
  transfers between devices with their start and end apart: 15 -> 6, of which waited for: 2 -> 3; matrix products, arithmetic and copies ran while one was open for 0% -> 1% of each run, Pallas kernels for 12% -> 15%
where the time goes in v4:
time: 72.8 us; the launch traced here: 72.3 us
  blocking collectives  32.7 us (45%)
  Pallas kernels  15.3 us (21%)
  starting transfers between devices  11.9 us (16%)
  local copies, waits for them, and re-layouts  7.33 us (10%)
  waiting for transfers between devices  4.03 us (6%)
  between operations  0.82 us (1%)
    all_to_all x1, blocking collectives, gather_pieces(): lax.all_to_all(sums, OWNER, split_axis=0, concat_axis=0, tiled=True)  22.4 us
    all_to_all x1, blocking collectives, spread(): return lax.all_to_all(copies, axis, split_axis=0, concat_axis=0, tiled=True)  10.3 us
    unnamed x18, local copies, waits for them, and re-layouts  6.71 us
    pallas_call x1, Pallas kernels, body(): pl.pallas_call(functools.partial(first_half_kernel, few), out_shape=[half...  5.72 us
    pallas_call x1, Pallas kernels, body(): pl.pallas_call(functools.partial(second_half_kernel, few), out_shape=[hal...  5.43 us
    ppermute x2, starting transfers between devices, over_col(): over_x = lax.ppermute(value, axes, cross)  4.7 us
    all_to_all x1, starting transfers between devices, gather_pieces(): lax.all_to_all(strips, OWNER, split_axis=0, concat_axis=0, tiled=True)  3.56 us
    ppermute x2, starting transfers between devices, over_col(): return [value, over_x, lax.ppermute(held, axes, other)]  2.74 us
  transfers between devices with their start and end apart: 6, of which 3 were waited for; matrix products, arithmetic and copies ran while one was open for 1% of the time, Pallas kernels for 15%

profile of v4, /device:TPU:0, one launch (start us, length us, event | category | flops | bytes accessed | tf_op | source)
XLA Modules:
  0.0 72.3 jit_solution(12279642865913347217)
XLA Ops:
  0.0 0.0 copy-start.7
  0.0 0.7 copy-done.7
  0.7 0.0 copy-start
  0.7 1.0 %copy-done = f32[512,256]{1,0:T(8,128)S(1)} copy-done((f32[512,256]{1,0:T(8,128)S(1)}, f32[512,256]{1,0:T(8,128)}, u32[]{:S(2)}) %copy-start) | copy-done | bytes 524312
  1.7 0.0 copy-start.2
  1.7 1.2 %copy-done.2 = f32[1,128,2048]{2,1,0:T(8,128)S(1)} copy-done((f32[1,128,2048]{2,1,0:T(8,128)S(1)}, f32[1,128,2048]{2,1,0:T(8,128)}, u32[]{:S(2)}) %copy-start.2) | copy-done | bytes 1048600
  2.9 1.9 %split.1 = (f32[8,4,16,256]{3,2,1,0:T(8,128)S(1)}, f32[8,128,256]{2,1,0:T(8,128)}) custom-call(s32[2,16]{1,0:T(2,128)S(1)} %copy-done.7, f32[128,2048]{1,0:T(8,128)S(1)} %bitcast.2, f32[512,256]{1,0:T(8,128)S(1)} %copy-done), custom_call_target="tpu_custom_call" | custom-call | tf_op jit(solution)/shard_map/split/pallas_call | solution.py:309
  4.9 22.4 %all_to_all.15 = f32[8,4,16,256]{3,2,1,0:T(8,128)S(1)} all-to-all(f32[8,4,16,256]{3,2,1,0:T(8,128)S(1)} %get-tuple-element.16), channel_id=1, replica_groups=mesh['grp'=2,'row'=4,'col'=4] {'grp','row'}, dimensions={0} | all-to-all | bytes 1048576 | tf_op jit(solution)/shard_map/all_to_all | solution.py:323
  27.3 10.3 %all_to_all.16.refs_0_.near_ref = f32[4,4,16,256]{3,2,1,0:T(8,128)S(1)} all-to-all(f32[4,4,16,256]{3,2,1,0:T(8,128)S(1)} %broadcast_in_dim.2), channel_id=1, replica_groups=mesh['grp'=2,'row'=4,'col'=4] {'row'}, dimensions={0} | all-to-all | bytes 524288 | tf_op jit(solution)/shard_map/all_to_all | solution.py:289
  37.7 0.9 %collective-permute-start = (f32[4,4,16,256]{3,2,1,0:T(8,128)S(1)}, f32[4,4,16,256]{3,2,1,0:T(8,128)S(1)}, u32[]{:S(2)}, u32[]{:S(2)}) collective-permute-start(f32[4,4,16,256]{3,2,1,0:T(8,128)S(1)} %all_to_all.16.refs_0_.near_ref), channel_id=1, source_target_pairs={{0,16},{16,0},{1,17},{17,1},{2,18},{18,2},{3,19},{19,3},{4,20},{20... | collective-permute-start | bytes 786440 | tf_op jit(solution)/shard_map/ppermute | solution.py:327
  38.6 3.6 %all-to-all-start.2 = ((f32[8,128,256]{2,1,0:T(8,128)}), f32[8,128,256]{2,1,0:T(8,128)S(1)}, u32[]{:S(2)}, u32[]{:S(2)}) async-start(f32[8,128,256]{2,1,0:T(8,128)} %get-tuple-element.24), calls=%async_computation.2 | async-start | bytes 2097152 | tf_op jit(solution)/shard_map/all_to_all | solution.py:326
  42.2 2.5 %collective-permute-done.refs_1_.far_ref = f32[4,4,16,256]{3,2,1,0:T(8,128)S(1)} collective-permute-done((f32[4,4,16,256]{3,2,1,0:T(8,128)S(1)}, f32[4,4,16,256]{3,2,1,0:T(8,128)S(1)}, u32[]{:S(2)}, u32[]{:S(2)}) %collective-permute-start) | collective-permute-done | bytes 262176 | tf_op jit(solution)/shard_map/ppermute | solution.py:327
  44.7 3.4 %collective-permute-start.3 = (f32[8,2,16,256]{3,2,1,0:T(8,128)S(1)}, f32[8,2,16,256]{3,2,1,0:T(8,128)S(1)}, u32[]{:S(2)}, u32[]{:S(2)}) collective-permute-start(f32[8,2,16,256]{3,2,1,0:T(8,128)S(1)} %pad_maximum_fusion.refs_3_), channel_id=1, source_target_pairs={{0,2},{4,6},{9,11},{13,15},{18,16},{22,20},{27,25},{31,29}} | collective-permute-start | bytes 786440 | tf_op jit(solution)/shard_map/ppermute | solution.py:296
  48.1 5.7 %pivot_first.1 = (f32[128,128]{1,0:T(8,128)S(1)}, f32[128,128]{1,0:T(8,128)S(1)}, f32[128,128]{1,0:T(8,128)S(1)}, f32[128,128]{1,0:T(8,128)S(1)}) custom-call(f32[4,4,16,256]{3,2,1,0:T(8,128)S(1)} %all_to_all.16.refs_0_.near_ref, f32[4,4,16,256]{3,2,1,0:T(8,128)S(1)} %collective-permute-done.refs_1_.far_ref), custom_call_target="tpu_custom_call" | custom-call | flops 8000000000 | bytes 262144 | tf_op jit(solution)/shard_map/pivot_first/pallas_call | solution.py:346
  53.9 5.4 %pivot_second.1 = (f32[128,128]{1,0:T(8,128)S(1)}, f32[256,256]{1,0:T(8,128)S(1)}) custom-call(f32[128,128]{1,0:T(8,128)S(1)} %get-tuple-element.20.first_ref, f32[128,128]{1,0:T(8,128)S(1)} %get-tuple-element.19.side_ref, f32[128,128]{1,0:T(8,128)S(1)} %get-tuple-element.21.next_ref), custom_call_target="tpu_custom_call" | custom-call | flops 8000000000 | bytes 262144 | tf_op jit(solution)/shard_map/pivot_second/pallas_call | solution.py:356
  59.3 0.0 copy-start.5
  59.3 0.6 copy-done.5
  59.9 1.3 %collective-permute-start.1 = (f32[256,256]{1,0:T(8,128)S(1)}, f32[256,256]{1,0:T(8,128)S(1)}, u32[]{:S(2)}, u32[]{:S(2)}) collective-permute-start(f32[256,256]{1,0:T(8,128)S(1)} %get-tuple-element.23.refs_0_), channel_id=1, source_target_pairs={{0,2},{4,6},{8,10},{12,14},{16,18},{20,22},{24,26},{28,30}} | collective-permute-start | bytes 786440 | tf_op jit(solution)/shard_map/ppermute | solution.py:296
  61.2 0.0 copy-start.8
  61.2 0.6 copy-done.8
  61.9 0.6 dynamic_slice.15
  63.1 0.0 collective-permute-done.3.refs_4_
  63.2 0.0 copy-start.1
  63.2 1.4 %collective-permute-start.4 = (f32[8,2,16,256]{3,2,1,0:T(8,128)S(1)}, f32[8,2,16,256]{3,2,1,0:T(8,128)S(1)}, u32[]{:S(2)}, u32[]{:S(2)}) collective-permute-start(f32[8,2,16,256]{3,2,1,0:T(8,128)S(1)} %broadcast_select_fusion), channel_id=1, source_target_pairs={{0,1},{2,3},{4,5},{6,7},{9,8},{11,10},{13,12},{15,14},{18,19},{16,... | collective-permute-start | bytes 786440 | tf_op jit(solution)/shard_map/ppermute | solution.py:299
  64.6 0.4 collective-permute-done.1.refs_1_
  65.1 1.3 %collective-permute-start.2 = (f32[256,256]{1,0:T(8,128)S(1)}, f32[256,256]{1,0:T(8,128)S(1)}, u32[]{:S(2)}, u32[]{:S(2)}) collective-permute-start(f32[256,256]{1,0:T(8,128)S(1)} %broadcast_select_fusion.1), channel_id=1, source_target_pairs={{0,1},{2,3},{4,5},{6,7},{8,9},{10,11},{12,13},{14,15},{16,17},{18,... | collective-permute-start | bytes 786440 | tf_op jit(solution)/shard_map/ppermute | solution.py:299
  66.4 0.0 collective-permute-done.4.refs_5_
  66.4 1.1 %collective-permute-done.2.refs_2_ = f32[256,256]{1,0:T(8,128)S(1)} collective-permute-done((f32[256,256]{1,0:T(8,128)S(1)}, f32[256,256]{1,0:T(8,128)S(1)}, u32[]{:S(2)}, u32[]{:S(2)}) %collective-permute-start.2) | collective-permute-done | bytes 262176 | tf_op jit(solution)/shard_map/ppermute | solution.py:299
  67.6 0.0 copy-start.3
  67.6 0.7 copy-done.3
  68.3 0.0 all-to-all-done.2.refs_6_
  68.3 0.0 copy-done.1
  68.3 0.0 copy-start.4
  68.3 0.9 %copy-done.4 = f32[256,256]{1,0:T(8,128)S(1)} copy-done((f32[256,256]{1,0:T(8,128)S(1)}, f32[256,256]{1,0:T(8,128)}, u32[]{:S(2)}) %copy-start.4) | copy-done | bytes 262168
  69.2 0.0 copy-start.6
  69.2 0.8 %copy-done.6 = f32[128,128]{1,0:T(8,128)S(1)} copy-done((f32[128,128]{1,0:T(8,128)S(1)}, f32[128,128]{1,0:T(8,128)}, u32[]{:S(2)}) %copy-start.6) | copy-done | bytes 65560
  70.1 2.2 %finish.1 = f32[512,256]{1,0:T(8,128)} custom-call(s32[2,16]{1,0:T(2,128)S(1)} %copy-done.7, f32[512,256]{1,0:T(8,128)S(1)} %copy-done.1, f32[4,4,16,256]{3,2,1,0:T(8,128)S(1)} %all_to_all.16.refs_0_.near_ref, f32[4,4,16,256]{3,2,1,0:T(8,128)S(1)} %collective-permute-done.refs_1_.far_ref, f32[128,128]{1,0:T(8,128)S(1)} %get-tuple-element.18.upper_ref, ...), custom_call_target="tpu_custom_call" | custom-call | tf_op jit(solution)/shard_map/finish/pallas_call | solution.py:367
  (7 shorter events, 0.2 us)
Async XLA Ops:
  0.0 0.7 copy-start.7
  0.7 1.0 %copy-start = (f32[512,256]{1,0:T(8,128)S(1)}, f32[512,256]{1,0:T(8,128)}, u32[]{:S(2)}) copy-start(f32[512,256]{1,0:T(8,128)} %front_ref.1) | copy-start | bytes 1572868
  1.7 1.2 %copy-start.2 = (f32[1,128,2048]{2,1,0:T(8,128)S(1)}, f32[1,128,2048]{2,1,0:T(8,128)}, u32[]{:S(2)}) copy-start(f32[1,128,2048]{2,1,0:T(8,128)} %param.6) | copy-start | bytes 3145732
  37.7 7.0 %collective-permute-start = (f32[4,4,16,256]{3,2,1,0:T(8,128)S(1)}, f32[4,4,16,256]{3,2,1,0:T(8,128)S(1)}, u32[]{:S(2)}, u32[]{:S(2)}) collective-permute-start(f32[4,4,16,256]{3,2,1,0:T(8,128)S(1)} %all_to_all.16.refs_0_.near_ref), channel_id=1, source_target_pairs={{0,16},{16,0},{1,17},{17,1},{2,18},{18,2},{3,19},{19,3},{4,20},{20... | collective-permute-start | bytes 786440 | tf_op jit(solution)/shard_map/ppermute | solution.py:327
  38.6 29.6 %all-to-all-start.2 = ((f32[8,128,256]{2,1,0:T(8,128)}), f32[8,128,256]{2,1,0:T(8,128)S(1)}, u32[]{:S(2)}, u32[]{:S(2)}) async-start(f32[8,128,256]{2,1,0:T(8,128)} %get-tuple-element.24), calls=%async_computation.2 | async-start | bytes 2097152 | tf_op jit(solution)/shard_map/all_to_all | solution.py:326
  44.7 18.4 %collective-permute-start.3 = (f32[8,2,16,256]{3,2,1,0:T(8,128)S(1)}, f32[8,2,16,256]{3,2,1,0:T(8,128)S(1)}, u32[]{:S(2)}, u32[]{:S(2)}) collective-permute-start(f32[8,2,16,256]{3,2,1,0:T(8,128)S(1)} %pad_maximum_fusion.refs_3_), channel_id=1, source_target_pairs={{0,2},{4,6},{9,11},{13,15},{18,16},{22,20},{27,25},{31,29}} | collective-permute-start | bytes 786440 | tf_op jit(solution)/shard_map/ppermute | solution.py:296
  59.3 0.6 copy-start.5
  59.9 5.2 %collective-permute-start.1 = (f32[256,256]{1,0:T(8,128)S(1)}, f32[256,256]{1,0:T(8,128)S(1)}, u32[]{:S(2)}, u32[]{:S(2)}) collective-permute-start(f32[256,256]{1,0:T(8,128)S(1)} %get-tuple-element.23.refs_0_), channel_id=1, source_target_pairs={{0,2},{4,6},{8,10},{12,14},{16,18},{20,22},{24,26},{28,30}} | collective-permute-start | bytes 786440 | tf_op jit(solution)/shard_map/ppermute | solution.py:296
  61.2 0.7 copy-start.8
  63.2 5.1 %copy-start.1 = (f32[512,256]{1,0:T(8,128)S(1)}, f32[512,256]{1,0:T(8,128)}, u32[]{:S(2)}) copy-start(f32[512,256]{1,0:T(8,128)} %front_ref.1) | copy-start | bytes 1572868
  63.2 3.2 %collective-permute-start.4 = (f32[8,2,16,256]{3,2,1,0:T(8,128)S(1)}, f32[8,2,16,256]{3,2,1,0:T(8,128)S(1)}, u32[]{:S(2)}, u32[]{:S(2)}) collective-permute-start(f32[8,2,16,256]{3,2,1,0:T(8,128)S(1)} %broadcast_select_fusion), channel_id=1, source_target_pairs={{0,1},{2,3},{4,5},{6,7},{9,8},{11,10},{13,12},{15,14},{18,19},{16,... | collective-permute-start | bytes 786440 | tf_op jit(solution)/shard_map/ppermute | solution.py:299
  65.1 2.4 %collective-permute-start.2 = (f32[256,256]{1,0:T(8,128)S(1)}, f32[256,256]{1,0:T(8,128)S(1)}, u32[]{:S(2)}, u32[]{:S(2)}) collective-permute-start(f32[256,256]{1,0:T(8,128)S(1)} %broadcast_select_fusion.1), channel_id=1, source_target_pairs={{0,1},{2,3},{4,5},{6,7},{8,9},{10,11},{12,13},{14,15},{16,17},{18,... | collective-permute-start | bytes 786440 | tf_op jit(solution)/shard_map/ppermute | solution.py:299
  67.6 0.7 copy-start.3
  68.3 1.0 %copy-start.4 = (f32[256,256]{1,0:T(8,128)S(1)}, f32[256,256]{1,0:T(8,128)}, u32[]{:S(2)}) copy-start(f32[256,256]{1,0:T(8,128)} %copy-done.3) | copy-start | bytes 786436
  69.2 0.8 %copy-start.6 = (f32[128,128]{1,0:T(8,128)S(1)}, f32[128,128]{1,0:T(8,128)}, u32[]{:S(2)}) copy-start(f32[128,128]{1,0:T(8,128)} %copy-done.5) | copy-start | bytes 196612

commit v5 on v4

--- a/solution.py
+++ b/solution.py
@@ -38,7 +38,6 @@
     inv = [[None] * n for _ in range(n)]
     for k in range(n):
         root = lax.rsqrt(d[k][k])
-        root = root * (1.5 - 0.5 * d[k][k] * root * root)
         inv[k][k] = root
         for i in range(k + 1, n):
             low[i][k] = d[i][k] * root
@@ -195,15 +194,24 @@
         pl.when(here)(functools.partial(take, ref))
 
 
-def finish_kernel(few, map_ref, front_ref, near_ref, far_ref, upper_ref, side_ref, upper2_ref, *refs):
+def assemble_kernel(map_ref, front_ref, strips_ref, out_ref):
+    n_row, n_col = lax.axis_size("row"), lax.axis_size("col")
+    col = lax.axis_index("col")
+    row_blocks = out_ref.shape[0] // BLK
+    out_ref[...] = front_ref[...]
+    for i in range(strips_ref.shape[0]):
+        local = map_ref[i // n_row, i % n_row * n_col + col] - col * row_blocks
+        start = pl.multiple_of(local * BLK, BLK)
+        out_ref[pl.ds(start, BLK), :] += strips_ref[i]
+
+
+def finish_kernel(few, base_ref, near_ref, far_ref, upper_ref, side_ref, upper2_ref, *refs):
     count = 3 if few else 1
-    inverses, parts, strips = refs[:count], refs[count : 2 * count], refs[2 * count : -4]
+    inverses, parts = refs[:count], refs[count : 2 * count]
     out_ref, rows_c_ref, rows_o_ref, inv_ref = refs[-4:]
     rows, width = out_ref.shape
-    n_row, n_col = lax.axis_size("row"), lax.axis_size("col")
     grp, col = lax.axis_index("grp"), lax.axis_index("col")
     me = owner_of()
-    row_blocks = rows // BLK
 
     def take_inverse(ref):
         inv_ref[...] = ref[...]
@@ -239,12 +247,7 @@
     @pl.when(me != 0)
     def _():
         right = dot(rows_o_ref[...], inv, 1, 1)
-        out_ref[...] = front_ref[...] - dot(left, right, 1, 1)
-        for ref in strips:
-            for i in range(ref.shape[0]):
-                local = map_ref[i // n_row, i % n_row * n_col + col] - col * row_blocks
-                start = pl.multiple_of(local * BLK, BLK)
-                out_ref[pl.ds(start, BLK), :] += ref[i]
+        out_ref[...] = base_ref[...] - dot(left, right, 1, 1)
 
         @pl.when(col == 0)
         def _():
@@ -281,7 +284,7 @@
         low = c * rows // width
         sent = from_root(part, "col", c)
         rows_o = jnp.where((me >= low) & (me < low + rows // width), sent, rows_o)
-    return assembled, (rows_c, rows_c), [rows_o], [pivot], []
+    return assembled, (rows_c, rows_c), [pivot], rows_o
 
 
 def spread(piece, axis):
@@ -296,7 +299,7 @@
     over_x = lax.ppermute(value, axes, cross)
     held = jnp.where(lax.axis_index("col") == jnp.array(roots)[owner_of()], value, over_x)
     other = [(o * n_col + (c ^ e), o * n_col + (c ^ e ^ 1)) for o, c in enumerate(roots) for e in (0, 2)]
-    return [value, over_x, lax.ppermute(held, axes, other)]
+    return [value, over_x, lax.ppermute(held, axes, other)], held
 
 
 def gather_pieces(front, strip, child_map):
@@ -304,12 +307,11 @@
     rows, width = front.shape
     row_blocks = rows // BLK
     part = BLK // owners
-    me = owner_of()
-    any_space = pl.BlockSpec(memory_space=pl.ANY)
+    in_hbm = pl.BlockSpec(memory_space=pltpu.HBM)
     sums, strips = pl.pallas_call(
         split_kernel,
         out_shape=[f32(owners, row_blocks, part, width), f32(owners, BLK, width)],
-        in_specs=[SMEM, any_space, any_space],
+        in_specs=[SMEM, in_hbm, in_hbm],
         out_specs=[VMEM] * 2,
         scratch_shapes=[
             pltpu.SMEM((child_map.shape[1],), jnp.int32),
@@ -326,11 +328,7 @@
     strips = lax.all_to_all(strips, OWNER, split_axis=0, concat_axis=0, tiled=True)
     far = lax.ppermute(near, "grp", [(0, 1), (1, 0)])
 
-    at = me * width % rows // BLK
-    cut = lambda v: lax.dynamic_slice_in_dim(v, at, width // BLK, 1)
-    own_part = jnp.concatenate([cut(near), cut(far)], axis=0)
-    parts = over_col(own_part, [o * width // rows for o in range(owners)])
-    return front, (near, far), parts, [near, far], [strips]
+    return front, (near, far), [near, far], strips
 
 
 def body(front, child_blocks, child_map):
@@ -340,7 +338,7 @@
     few = lax.axis_size("grp") == 2 and lax.axis_size("col") == 4
     few = few and BLK % (owners * 8) == 0 and child_map.shape[1] == blocks
     gather = gather_pieces if few else gather_wide
-    base, panel, parts, pivot, strips = gather(front, child_blocks[0], child_map)
+    base, panel, pivot, last = gather(front, child_blocks[0], child_map)
     half = f32(BLK, BLK)
     cost = pl.CostEstimate(flops=8_000_000_000, bytes_accessed=1 << 18, transcendentals=0)
     upper, first, side, rest = pl.pallas_call(
@@ -353,6 +351,12 @@
         cost_estimate=cost,
         name="pivot_first",
     )(*pivot)
+    if few:
+        first, near, far = lax.optimization_barrier((first, *panel))
+        at = owner_of() * width % rows // BLK
+        cut = lambda v: lax.dynamic_slice_in_dim(v, at, width // BLK, 1)
+        own_part = jnp.concatenate([cut(near), cut(far)], axis=0)
+        parts, _ = over_col(own_part, [o * width // rows for o in range(owners)])
     upper2, inverse = pl.pallas_call(
         functools.partial(second_half_kernel, few),
         out_shape=[half, f32(PIVOTS, PIVOTS)],
@@ -363,16 +367,28 @@
         cost_estimate=cost,
         name="pivot_second",
     )(first, side, rest)
-    inverses = over_col(inverse, [0] * owners) if few else [inverse]
+    if few:
+        inverses, held = over_col(inverse, [0] * owners)
+        strips, _ = lax.optimization_barrier((last, held))
+        base = pl.pallas_call(
+            assemble_kernel,
+            out_shape=f32(rows, width),
+            in_specs=[SMEM, VMEM, VMEM],
+            out_specs=VMEM,
+            compiler_params=PARAMS,
+            name="assemble",
+        )(child_map, base, strips)
+    else:
+        inverses, parts = [inverse], [last]
     return pl.pallas_call(
         functools.partial(finish_kernel, few),
         out_shape=f32(rows, width),
-        in_specs=[SMEM] + [VMEM] * (6 + len(inverses) + len(parts) + len(strips)),
+        in_specs=[VMEM] * (6 + len(inverses) + len(parts)),
         out_specs=VMEM,
         scratch_shapes=[pltpu.VMEM((n, width), jnp.float32) for n in (rows, width, PIVOTS)],
         compiler_params=PARAMS,
         name="finish",
-    )(child_map, base, *panel, upper, side, upper2, *inverses, *parts, *strips)
+    )(base, *panel, upper, side, upper2, *inverses, *parts)
 
 
 def solution(mesh):

time: 72.8 us -> 73.2 us (level)
  the two profiles are of different devices: /device:TPU:0 before, /device:TPU:5 now
where the time goes in v5:
time: 73.2 us; the launch traced here: 72.7 us
  blocking collectives  27.7 us (38%)
  waiting for transfers between devices  19.7 us (27%)
  starting transfers between devices  11 us (15%)
  Pallas kernels  6.32 us (9%)
  local copies, waits for them, and re-layouts  5.55 us (8%)
  other arithmetic  1.55 us (2%)
  between operations  0.87 us (1%)
    all_to_all x1, blocking collectives, gather_pieces(): lax.all_to_all(sums, OWNER, split_axis=0, concat_axis=0, tiled=True)  18.9 us
    all_to_all x1, waiting for transfers between devices, gather_pieces(): lax.all_to_all(strips, OWNER, split_axis=0, concat_axis=0, tiled=True)  14.2 us
    all_to_all x1, blocking collectives, spread(): return lax.all_to_all(copies, axis, split_axis=0, concat_axis=0, tiled=True)  8.83 us
    all_to_all x1, starting transfers between devices, gather_pieces(): lax.all_to_all(strips, OWNER, split_axis=0, concat_axis=0, tiled=True)  6.15 us
    ppermute x2, waiting for transfers between devices, over_col(): return ([value, over_x, lax.ppermute(held, axes, other)], held)  5.54 us
    unnamed x22, local copies, waits for them, and re-layouts  4.93 us
    pallas_call x1, Pallas kernels, body(): pl.pallas_call(functools.partial(finish_kernel, few), out_shape=f32(rows,...  3.78 us
    ppermute x2, starting transfers between devices, over_col(): return ([value, over_x, lax.ppermute(held, axes, other)], held)  2.69 us
  transfers between devices with their start and end apart: 6, of which 3 were waited for; matrix products, arithmetic and copies ran while one was open for 3% of the time, Pallas kernels for 1%

profile of v5, /device:TPU:5, one launch (start us, length us, event | category | flops | bytes accessed | tf_op | source)
XLA Modules:
  0.0 72.7 jit_solution(3733949587667810680)
XLA Ops:
  0.0 0.0 copy-start.5
  0.0 0.7 copy-done.5
  0.7 0.0 copy-start
  0.7 1.0 %copy-done = f32[512,256]{1,0:T(8,128)S(1)} copy-done((f32[512,256]{1,0:T(8,128)S(1)}, f32[512,256]{1,0:T(8,128)}, u32[]{:S(2)}) %copy-start) | copy-done | bytes 524312
  1.7 0.0 copy-start.2
  1.7 1.2 %copy-done.2 = f32[1,128,2048]{2,1,0:T(8,128)S(1)} copy-done((f32[1,128,2048]{2,1,0:T(8,128)S(1)}, f32[1,128,2048]{2,1,0:T(8,128)}, u32[]{:S(2)}) %copy-start.2) | copy-done | bytes 1048600
  2.9 1.8 %split.1 = (f32[8,4,16,256]{3,2,1,0:T(8,128)S(1)}, f32[8,128,256]{2,1,0:T(8,128)}) custom-call(s32[2,16]{1,0:T(2,128)S(1)} %copy-done.5, f32[128,2048]{1,0:T(8,128)S(1)} %bitcast.2, f32[512,256]{1,0:T(8,128)S(1)} %copy-done), custom_call_target="tpu_custom_call" | custom-call | tf_op jit(solution)/shard_map/split/pallas_call | solution.py:311
  4.8 18.9 %all_to_all.15 = f32[8,4,16,256]{3,2,1,0:T(8,128)S(1)} all-to-all(f32[8,4,16,256]{3,2,1,0:T(8,128)S(1)} %get-tuple-element.20), channel_id=1, replica_groups=mesh['grp'=2,'row'=4,'col'=4] {'grp','row'}, dimensions={0} | all-to-all | bytes 1048576 | tf_op jit(solution)/shard_map/all_to_all | solution.py:325
  23.7 8.8 %all_to_all.16.refs_0_.near_ref = f32[4,4,16,256]{3,2,1,0:T(8,128)S(1)} all-to-all(f32[4,4,16,256]{3,2,1,0:T(8,128)S(1)} %broadcast_in_dim.2), channel_id=1, replica_groups=mesh['grp'=2,'row'=4,'col'=4] {'row'}, dimensions={0} | all-to-all | bytes 524288 | tf_op jit(solution)/shard_map/all_to_all | solution.py:292
  32.6 0.8 %collective-permute-start = (f32[4,4,16,256]{3,2,1,0:T(8,128)S(1)}, f32[4,4,16,256]{3,2,1,0:T(8,128)S(1)}, u32[]{:S(2)}, u32[]{:S(2)}) collective-permute-start(f32[4,4,16,256]{3,2,1,0:T(8,128)S(1)} %all_to_all.16.refs_0_.near_ref), channel_id=1, source_target_pairs={{0,16},{16,0},{1,17},{17,1},{2,18},{18,2},{3,19},{19,3},{4,20},{20... | collective-permute-start | bytes 786440 | tf_op jit(solution)/shard_map/ppermute | solution.py:329
  33.4 6.2 %all-to-all-start.2 = ((f32[8,128,256]{2,1,0:T(8,128)}), f32[8,128,256]{2,1,0:T(8,128)S(1)}, u32[]{:S(2)}, u32[]{:S(2)}) async-start(f32[8,128,256]{2,1,0:T(8,128)} %get-tuple-element.21), calls=%async_computation.2 | async-start | bytes 2097152 | tf_op jit(solution)/shard_map/all_to_all | solution.py:328
  39.5 0.0 collective-permute-done.refs_1_.far_ref
  39.5 0.0 copy-start.3
  39.5 0.6 copy-done.3
  40.1 0.7 collective-permute-start.1
  40.9 0.0 copy-start.6
  40.9 0.0 copy-start.8
  40.9 0.6 copy-done.6
  41.5 0.1 copy-done.8
  41.6 0.7 collective-permute-start.3
  42.3 0.0 copy-start.10
  42.3 0.6 copy-done.10
  43.0 0.6 dynamic_slice.15
  44.2 0.0 copy-start.7
  44.2 0.0 copy-start.9
  44.2 0.0 collective-permute-done.1.refs_1_
  44.2 0.7 %broadcast_select_fusion.1 = f32[256,256]{1,0:T(8,128)} fusion(f32[256,256]{1,0:T(8,128)S(1)} %get-tuple-element.27.refs_0_, f32[256,256]{1,0:T(8,128)S(1)} %collective-permute-done.1.refs_1_, pred[]{:T(512)S(6)} %eq.8), kind=kLoop, calls=%fused_computation.2 | loop fusion | flops 65536 | bytes 786433 | tf_op jit(solution)/shard_map/jit(_where)/select_n | solution.py:300
  45.0 0.0 copy-start.1
  45.0 1.4 %collective-permute-start.2 = (f32[256,256]{1,0:T(8,128)}, f32[256,256]{1,0:T(8,128)S(1)}, u32[]{:S(2)}, u32[]{:S(2)}) collective-permute-start(f32[256,256]{1,0:T(8,128)} %broadcast_select_fusion.1), channel_id=1, source_target_pairs={{0,1},{2,3},{4,5},{6,7},{8,9},{10,11},{12,13},{14,15},{16,17},{18,... | collective-permute-start | bytes 786440 | tf_op jit(solution)/shard_map/ppermute | solution.py:302
  46.4 0.0 collective-permute-done.3.refs_4_
  46.4 0.0 copy-done.7
  46.4 0.0 copy-done.9
  46.4 0.8 %broadcast_select_fusion = f32[8,2,16,256]{3,2,1,0:T(8,128)} fusion(f32[8,2,16,256]{3,2,1,0:T(8,128)S(1)} %collective-permute-done.3.refs_4_, pred[]{:T(512)S(6)} %eq.9, f32[4,2,16,256]{3,2,1,0:T(8,128)S(1)} %copy-done.7, f32[4,2,16,256]{3,2,1,0:T(8,128)S(1)} %copy-done.9), kind=kLoop, calls=%fused_computation.1 | loop fusion | flops 131072 | bytes 786433 | tf_op jit(solution)/shard_map/jit(_where)/select_n | solution.py:300
  47.2 1.3 %collective-permute-start.4 = (f32[8,2,16,256]{3,2,1,0:T(8,128)}, f32[8,2,16,256]{3,2,1,0:T(8,128)}, u32[]{:S(2)}, u32[]{:S(2)}) collective-permute-start(f32[8,2,16,256]{3,2,1,0:T(8,128)} %broadcast_select_fusion), channel_id=1, source_target_pairs={{0,1},{2,3},{4,5},{6,7},{9,8},{11,10},{13,12},{15,14},{18,19},{16,... | collective-permute-start | bytes 786440 | tf_op jit(solution)/shard_map/ppermute | solution.py:302
  48.5 14.2 %all-to-all-done.2.strips_ref = f32[8,128,256]{2,1,0:T(8,128)S(1)} async-done(((f32[8,128,256]{2,1,0:T(8,128)}), f32[8,128,256]{2,1,0:T(8,128)S(1)}, u32[]{:S(2)}, u32[]{:S(2)}) %all-to-all-start.2) | async-done | bytes 1048608 | tf_op jit(solution)/shard_map/all_to_all | solution.py:328
  62.6 0.0 copy-done.1
  62.6 0.0 copy-start.4
  62.6 0.7 assemble.1.base_ref
  63.3 0.5 collective-permute-done.2.refs_2_
  63.8 5.0 %collective-permute-done.4.refs_5_ = f32[8,2,16,256]{3,2,1,0:T(8,128)} collective-permute-done((f32[8,2,16,256]{3,2,1,0:T(8,128)}, f32[8,2,16,256]{3,2,1,0:T(8,128)}, u32[]{:S(2)}, u32[]{:S(2)}) %collective-permute-start.4) | collective-permute-done | bytes 262176 | tf_op jit(solution)/shard_map/ppermute | solution.py:302
  68.9 0.0 copy-done.4
  68.9 3.8 %finish.1 = f32[512,256]{1,0:T(8,128)} custom-call(f32[512,256]{1,0:T(8,128)S(1)} %assemble.1.base_ref, f32[4,4,16,256]{3,2,1,0:T(8,128)S(1)} %all_to_all.16.refs_0_.near_ref, f32[4,4,16,256]{3,2,1,0:T(8,128)S(1)} %collective-permute-done.refs_1_.far_ref, f32[128,128]{1,0:T(8,128)S(1)} %get-tuple-element.29.upper_ref, ...), custom_call_target="tpu_custom_call" | custom-call | tf_op jit(solution)/shard_map/finish/pallas_call | solution.py:383
  (6 shorter events, 0.1 us)
Async XLA Ops:
  0.0 0.7 copy-start.5
  0.7 1.0 %copy-start = (f32[512,256]{1,0:T(8,128)S(1)}, f32[512,256]{1,0:T(8,128)}, u32[]{:S(2)}) copy-start(f32[512,256]{1,0:T(8,128)} %front_ref.1) | copy-start | bytes 1572868
  1.7 1.2 %copy-start.2 = (f32[1,128,2048]{2,1,0:T(8,128)S(1)}, f32[1,128,2048]{2,1,0:T(8,128)}, u32[]{:S(2)}) copy-start(f32[1,128,2048]{2,1,0:T(8,128)} %param.6) | copy-start | bytes 3145732
  32.6 6.9 %collective-permute-start = (f32[4,4,16,256]{3,2,1,0:T(8,128)S(1)}, f32[4,4,16,256]{3,2,1,0:T(8,128)S(1)}, u32[]{:S(2)}, u32[]{:S(2)}) collective-permute-start(f32[4,4,16,256]{3,2,1,0:T(8,128)S(1)} %all_to_all.16.refs_0_.near_ref), channel_id=1, source_target_pairs={{0,16},{16,0},{1,17},{17,1},{2,18},{18,2},{3,19},{19,3},{4,20},{20... | collective-permute-start | bytes 786440 | tf_op jit(solution)/shard_map/ppermute | solution.py:329
  33.4 29.3 %all-to-all-start.2 = ((f32[8,128,256]{2,1,0:T(8,128)}), f32[8,128,256]{2,1,0:T(8,128)S(1)}, u32[]{:S(2)}, u32[]{:S(2)}) async-start(f32[8,128,256]{2,1,0:T(8,128)} %get-tuple-element.21), calls=%async_computation.2 | async-start | bytes 2097152 | tf_op jit(solution)/shard_map/all_to_all | solution.py:328
  39.5 0.6 copy-start.3
  40.1 4.1 %collective-permute-start.1 = (f32[256,256]{1,0:T(8,128)S(1)}, f32[256,256]{1,0:T(8,128)S(1)}, u32[]{:S(2)}, u32[]{:S(2)}) collective-permute-start(f32[256,256]{1,0:T(8,128)S(1)} %get-tuple-element.27.refs_0_), channel_id=1, source_target_pairs={{0,2},{4,6},{8,10},{12,14},{16,18},{20,22},{24,26},{28,30}} | collective-permute-start | bytes 786440 | tf_op jit(solution)/shard_map/ppermute | solution.py:299
  40.9 0.7 copy-start.6
  40.9 0.7 copy-start.8
  41.6 4.8 %collective-permute-start.3 = (f32[8,2,16,256]{3,2,1,0:T(8,128)S(1)}, f32[8,2,16,256]{3,2,1,0:T(8,128)S(1)}, u32[]{:S(2)}, u32[]{:S(2)}) collective-permute-start(f32[8,2,16,256]{3,2,1,0:T(8,128)S(1)} %pad_maximum_fusion.refs_3_), channel_id=1, source_target_pairs={{0,2},{4,6},{9,11},{13,15},{18,16},{22,20},{27,25},{31,29}} | collective-permute-start | bytes 786440 | tf_op jit(solution)/shard_map/ppermute | solution.py:299
  42.3 0.7 copy-start.10
  44.2 2.2 %copy-start.7 = (f32[4,2,16,256]{3,2,1,0:T(8,128)S(1)}, f32[4,2,16,256]{3,2,1,0:T(8,128)}, u32[]{:S(2)}) copy-start(f32[4,2,16,256]{3,2,1,0:T(8,128)} %copy-done.6) | copy-start | bytes 393220
  44.2 2.2 %copy-start.9 = (f32[4,2,16,256]{3,2,1,0:T(8,128)S(1)}, f32[4,2,16,256]{3,2,1,0:T(8,128)}, u32[]{:S(2)}) copy-start(f32[4,2,16,256]{3,2,1,0:T(8,128)} %copy-done.8) | copy-start | bytes 393220
  45.0 17.7 %copy-start.1 = (f32[512,256]{1,0:T(8,128)S(1)}, f32[512,256]{1,0:T(8,128)}, u32[]{:S(2)}) copy-start(f32[512,256]{1,0:T(8,128)} %front_ref.1) | copy-start | bytes 1572868
  45.0 18.9 %collective-permute-start.2 = (f32[256,256]{1,0:T(8,128)}, f32[256,256]{1,0:T(8,128)S(1)}, u32[]{:S(2)}, u32[]{:S(2)}) collective-permute-start(f32[256,256]{1,0:T(8,128)} %broadcast_select_fusion.1), channel_id=1, source_target_pairs={{0,1},{2,3},{4,5},{6,7},{8,9},{10,11},{12,13},{14,15},{16,17},{18,... | collective-permute-start | bytes 786440 | tf_op jit(solution)/shard_map/ppermute | solution.py:302
  47.2 21.7 %collective-permute-start.4 = (f32[8,2,16,256]{3,2,1,0:T(8,128)}, f32[8,2,16,256]{3,2,1,0:T(8,128)}, u32[]{:S(2)}, u32[]{:S(2)}) collective-permute-start(f32[8,2,16,256]{3,2,1,0:T(8,128)} %broadcast_select_fusion), channel_id=1, source_target_pairs={{0,1},{2,3},{4,5},{6,7},{9,8},{11,10},{13,12},{15,14},{18,19},{16,... | collective-permute-start | bytes 786440 | tf_op jit(solution)/shard_map/ppermute | solution.py:302
  62.6 6.2 %copy-start.4 = (f32[128,128]{1,0:T(8,128)S(1)}, f32[128,128]{1,0:T(8,128)}, u32[]{:S(2)}) copy-start(f32[128,128]{1,0:T(8,128)} %copy-done.3) | copy-start | bytes 196612

commit v6 on v5

--- a/solution.py
+++ b/solution.py
@@ -141,24 +141,15 @@
         inverse_ref[BLK:, :BLK] = -dot(second, dot(side_ref[...], first, 0, 0), 1, 0)
 
 
-def split_kernel(map_ref, strip_hbm, front_hbm, sums_ref, out_ref, inv_ref, strip_ref, front_ref, sems):
+def split_kernel(map_ref, strip_ref, front_ref, sums_ref, out_ref, inv_ref):
     owners, row_blocks, part, width = sums_ref.shape
     per = width // BLK
     grp, row, col = (lax.axis_index(a) for a in ("grp", "row", "col"))
     n_row, n_col = lax.axis_size("row"), lax.axis_size("col")
     me = grp * n_row + row
-    get_strip = pltpu.make_async_copy(strip_hbm, strip_ref, sems.at[0])
-    get_front = pltpu.make_async_copy(front_hbm, front_ref, sems.at[1])
-    get_strip.start()
-
-    @pl.when(me == 0)
-    def _():
-        get_front.start()
-
     for q in range(map_ref.shape[1]):
         inv_ref[map_ref[grp, q]] = q
     mine = map_ref[grp, row * n_col + col] - col * row_blocks
-    get_strip.wait()
     for s in range(per):
         at = pl.multiple_of(inv_ref[s] * BLK, BLK)
         lanes = slice(s * BLK, (s + 1) * BLK)
@@ -169,7 +160,6 @@
 
     @pl.when(me == 0)
     def _():
-        get_front.wait()
         for k in range(owners):
             for b in range(row_blocks):
                 at = b * BLK + part * k
@@ -182,10 +172,11 @@
 
 
 def place_rows(target_ref, pieces_ref, grp):
+    row = lax.axis_index("row")
     n_row, blocks, part, _ = pieces_ref.shape
     for b in range(blocks):
         for r in range(n_row):
-            at = pl.multiple_of(b * BLK + (grp * n_row + r) * part, SUB)
+            at = pl.multiple_of(b * BLK + (grp * n_row + (row ^ r)) * part, SUB)
             target_ref[pl.ds(at, part), :] = pieces_ref[r, b]
 
 
@@ -287,11 +278,6 @@
     return assembled, (rows_c, rows_c), [pivot], rows_o
 
 
-def spread(piece, axis):
-    copies = jnp.broadcast_to(piece[None], (lax.axis_size(axis),) + piece.shape)
-    return lax.all_to_all(copies, axis, split_axis=0, concat_axis=0, tiled=True)
-
-
 def over_col(value, roots):
     n_col = lax.axis_size("col")
     axes = OWNER + ("col",)
@@ -307,24 +293,20 @@
     rows, width = front.shape
     row_blocks = rows // BLK
     part = BLK // owners
-    in_hbm = pl.BlockSpec(memory_space=pltpu.HBM)
     sums, strips = pl.pallas_call(
         split_kernel,
         out_shape=[f32(owners, row_blocks, part, width), f32(owners, BLK, width)],
-        in_specs=[SMEM, in_hbm, in_hbm],
+        in_specs=[SMEM, VMEM, VMEM],
         out_specs=[VMEM] * 2,
-        scratch_shapes=[
-            pltpu.SMEM((child_map.shape[1],), jnp.int32),
-            pltpu.VMEM(strip.shape, jnp.float32),
-            pltpu.VMEM(front.shape, jnp.float32),
-            pltpu.SemaphoreType.DMA((2,)),
-        ],
+        scratch_shapes=[pltpu.SMEM((child_map.shape[1],), jnp.int32)],
         compiler_params=PARAMS,
         name="split",
     )(child_map, strip, front)
     mine = jnp.sum(lax.all_to_all(sums, OWNER, split_axis=0, concat_axis=0, tiled=True), axis=0)
-    near = spread(mine, "row")
-    strips, near = lax.optimization_barrier((strips, near))
+    strips, mine = lax.optimization_barrier((strips, mine))
+    n_row = lax.axis_size("row")
+    others = [lax.ppermute(mine, "row", [(i, i ^ d) for i in range(n_row)]) for d in range(1, n_row)]
+    near = jnp.stack([mine] + others)
     strips = lax.all_to_all(strips, OWNER, split_axis=0, concat_axis=0, tiled=True)
     far = lax.ppermute(near, "grp", [(0, 1), (1, 0)])
 
@@ -335,7 +317,7 @@
     owners = lax.axis_size(OWNER)
     rows, width = front.shape
     blocks = owners * width // BLK
-    few = lax.axis_size("grp") == 2 and lax.axis_size("col") == 4
+    few = lax.axis_size("grp") == 2 and lax.axis_size("row") == 4 and lax.axis_size("col") == 4
     few = few and BLK % (owners * 8) == 0 and child_map.shape[1] == blocks
     gather = gather_pieces if few else gather_wide
     base, panel, pivot, last = gather(front, child_blocks[0], child_map)

time: 73.2 us -> 72.8 us (level)
  blocking collectives: 27.7 us -> 18.9 us
  waiting for transfers between devices: 19.7 us -> 26.7 us
  starting transfers between devices: 11 us -> 12.6 us
    all_to_all x1 -> x0, blocking collectives: 8.83 us -> none  [spread(): return lax.all_to_all(copies, axis, split_axis=0, concat_axis=0, tiled=True)]
    ppermute x0 -> x3, waiting for transfers between devices: none -> 5.27 us  [gather_pieces(): lax.ppermute(mine, 'row', [(i, i ^ d) for i in range(n_row)])]
    ppermute x0 -> x3, starting transfers between devices: none -> 3.61 us  [gather_pieces(): lax.ppermute(mine, 'row', [(i, i ^ d) for i in range(n_row)])]
    ppermute x1, waiting for transfers between devices: 0.01 us -> 2.05 us  [gather_pieces(): far = lax.ppermute(near, 'grp', [(0, 1), (1, 0)])]
    all_to_all x1, waiting for transfers between devices: 14.2 us -> 12.9 us  [gather_pieces(): lax.all_to_all(strips, OWNER, split_axis=0, concat_axis=0, tiled=True)]
    all_to_all x1, starting transfers between devices: 6.15 us -> 4.93 us  [gather_pieces(): lax.all_to_all(strips, OWNER, split_axis=0, concat_axis=0, tiled=True)]
    ppermute x2, waiting for transfers between devices: 5.54 us -> 6.45 us  [over_col(): return ([value, over_x, lax.ppermute(held, axes, other)], held)]
  transfers between devices with their start and end apart: 6 -> 9, of which waited for: 3 -> 6; matrix products, arithmetic and copies ran while one was open for 3% -> 3% of each run, Pallas kernels for 1% -> 1%
where the time goes in v6:
time: 72.8 us; the launch traced here: 72.3 us
  waiting for transfers between devices  26.7 us (37%)
  blocking collectives  18.9 us (26%)
  starting transfers between devices  12.6 us (17%)
  Pallas kernels  6.21 us (9%)
  local copies, waits for them, and re-layouts  5.53 us (8%)
  other arithmetic  1.55 us (2%)
  between operations  0.86 us (1%)
    all_to_all x1, blocking collectives, gather_pieces(): lax.all_to_all(sums, OWNER, split_axis=0, concat_axis=0, tiled=True)  18.9 us
    all_to_all x1, waiting for transfers between devices, gather_pieces(): lax.all_to_all(strips, OWNER, split_axis=0, concat_axis=0, tiled=True)  12.9 us
    ppermute x2, waiting for transfers between devices, over_col(): return ([value, over_x, lax.ppermute(held, axes, other)], held)  6.45 us
    ppermute x3, waiting for transfers between devices, gather_pieces(): lax.ppermute(mine, 'row', [(i, i ^ d) for i in range(n_row)])  5.27 us
    all_to_all x1, starting transfers between devices, gather_pieces(): lax.all_to_all(strips, OWNER, split_axis=0, concat_axis=0, tiled=True)  4.93 us
    unnamed x22, local copies, waits for them, and re-layouts  4.92 us
    pallas_call x1, Pallas kernels, body(): pl.pallas_call(functools.partial(finish_kernel, few), out_shape=f32(rows,...  3.74 us
    ppermute x3, starting transfers between devices, gather_pieces(): lax.ppermute(mine, 'row', [(i, i ^ d) for i in range(n_row)])  3.61 us
  transfers between devices with their start and end apart: 9, of which 6 were waited for; matrix products, arithmetic and copies ran while one was open for 3% of the time, Pallas kernels for 1%

profile of v6, /device:TPU:5, one launch (start us, length us, event | category | flops | bytes accessed | tf_op | source)
XLA Modules:
  0.0 72.3 jit_solution(5940092574064042695)
XLA Ops:
  0.0 0.0 copy-start.5
  0.0 0.7 copy-done.5
  0.7 0.0 copy-start
  0.7 1.0 %copy-done = f32[512,256]{1,0:T(8,128)S(1)} copy-done((f32[512,256]{1,0:T(8,128)S(1)}, f32[512,256]{1,0:T(8,128)}, u32[]{:S(2)}) %copy-start) | copy-done | bytes 524312
  1.7 0.0 copy-start.2
  1.7 1.2 %copy-done.2 = f32[1,128,2048]{2,1,0:T(8,128)S(1)} copy-done((f32[1,128,2048]{2,1,0:T(8,128)S(1)}, f32[1,128,2048]{2,1,0:T(8,128)}, u32[]{:S(2)}) %copy-start.2) | copy-done | bytes 1048600
  2.9 1.8 %split.1 = (f32[8,4,16,256]{3,2,1,0:T(8,128)S(1)}, f32[8,128,256]{2,1,0:T(8,128)}) custom-call(s32[2,16]{1,0:T(2,128)S(1)} %copy-done.5, f32[128,2048]{1,0:T(8,128)S(1)} %bitcast.6, f32[512,256]{1,0:T(8,128)S(1)} %copy-done), custom_call_target="tpu_custom_call" | custom-call | tf_op jit(solution)/shard_map/split/pallas_call | solution.py:296
  4.7 18.9 %all_to_all.10 = f32[8,4,16,256]{3,2,1,0:T(8,128)S(1)} all-to-all(f32[8,4,16,256]{3,2,1,0:T(8,128)S(1)} %get-tuple-element.20), channel_id=1, replica_groups=mesh['grp'=2,'row'=4,'col'=4] {'grp','row'}, dimensions={0} | all-to-all | bytes 1048576 | tf_op jit(solution)/shard_map/all_to_all | solution.py:305
  23.6 1.3 %collective-permute-start.2 = (f32[4,16,256]{2,1,0:T(8,128)S(1)}, f32[4,16,256]{2,1,0:T(8,128)S(1)}, u32[]{:S(2)}, u32[]{:S(2)}) collective-permute-start(f32[4,16,256]{2,1,0:T(8,128)S(1)} %reduce_sum.9), channel_id=1, source_target_pairs={{0,12},{4,8},{8,4},{12,0},{1,13},{5,9},{9,5},{13,1},{2,14},{6,10},... | collective-permute-start | bytes 196616 | tf_op jit(solution)/shard_map/ppermute | solution.py:308
  24.9 0.6 collective-permute-start.1
  25.5 1.8 %collective-permute-start = (f32[4,16,256]{2,1,0:T(8,128)S(1)}, f32[4,16,256]{2,1,0:T(8,128)S(1)}, u32[]{:S(2)}, u32[]{:S(2)}) collective-permute-start(f32[4,16,256]{2,1,0:T(8,128)S(1)} %reduce_sum.9), channel_id=1, source_target_pairs={{0,4},{4,0},{8,12},{12,8},{1,5},{5,1},{9,13},{13,9},{2,6},{6,2},{1... | collective-permute-start | bytes 196616 | tf_op jit(solution)/shard_map/ppermute | solution.py:308
  27.2 1.5 %collective-permute-done.2 = f32[4,16,256]{2,1,0:T(8,128)S(1)} collective-permute-done((f32[4,16,256]{2,1,0:T(8,128)S(1)}, f32[4,16,256]{2,1,0:T(8,128)S(1)}, u32[]{:S(2)}, u32[]{:S(2)}) %collective-permute-start.2) | collective-permute-done | bytes 65568 | tf_op jit(solution)/shard_map/ppermute | solution.py:308
  28.8 3.7 %collective-permute-done.1 = f32[4,16,256]{2,1,0:T(8,128)S(1)} collective-permute-done((f32[4,16,256]{2,1,0:T(8,128)S(1)}, f32[4,16,256]{2,1,0:T(8,128)S(1)}, u32[]{:S(2)}, u32[]{:S(2)}) %collective-permute-start.1) | collective-permute-done | bytes 65568 | tf_op jit(solution)/shard_map/ppermute | solution.py:308
  32.5 0.0 collective-permute-done
  32.5 0.1 collective-permute-start.3
  32.6 4.9 %all-to-all-start.1 = ((f32[8,128,256]{2,1,0:T(8,128)}), f32[8,128,256]{2,1,0:T(8,128)S(1)}, u32[]{:S(2)}, u32[]{:S(2)}) async-start(f32[8,128,256]{2,1,0:T(8,128)} %get-tuple-element.21), calls=%async_computation.1 | async-start | bytes 2097152 | tf_op jit(solution)/shard_map/all_to_all | solution.py:310
  37.5 2.1 %collective-permute-done.3.refs_1_.far_ref = f32[4,4,16,256]{3,2,1,0:T(8,128)S(1)} collective-permute-done((f32[4,4,16,256]{3,2,1,0:T(8,128)S(1)}, f32[4,4,16,256]{3,2,1,0:T(8,128)S(1)}, u32[]{:S(2)}, u32[]{:S(2)}) %collective-permute-start.3) | collective-permute-done | bytes 262176 | tf_op jit(solution)/shard_map/ppermute | solution.py:311
  39.6 0.0 copy-start.3
  39.6 0.6 copy-done.3
  40.2 0.7 collective-permute-start.4
  41.0 0.0 copy-start.6
  41.0 0.0 copy-start.8
  41.0 0.6 copy-done.6
  41.6 0.0 copy-done.8
  41.7 0.7 collective-permute-start.6
  42.4 0.0 copy-start.10
  42.4 0.6 copy-done.10
  43.0 0.6 dynamic_slice.15
  44.3 0.0 copy-start.7
  44.3 0.0 copy-start.9
  44.3 0.0 collective-permute-done.4.refs_1_
  44.3 0.7 %broadcast_select_fusion.1 = f32[256,256]{1,0:T(8,128)} fusion(f32[256,256]{1,0:T(8,128)S(1)} %get-tuple-element.27.refs_0_, f32[256,256]{1,0:T(8,128)S(1)} %collective-permute-done.4.refs_1_, pred[]{:T(512)S(6)} %eq.8), kind=kLoop, calls=%fused_computation.3 | loop fusion | flops 65536 | bytes 786433 | tf_op jit(solution)/shard_map/jit(_where)/select_n | solution.py:286
  45.1 0.0 copy-start.1
  45.1 1.4 %collective-permute-start.5 = (f32[256,256]{1,0:T(8,128)}, f32[256,256]{1,0:T(8,128)S(1)}, u32[]{:S(2)}, u32[]{:S(2)}) collective-permute-start(f32[256,256]{1,0:T(8,128)} %broadcast_select_fusion.1), channel_id=1, source_target_pairs={{0,1},{2,3},{4,5},{6,7},{8,9},{10,11},{12,13},{14,15},{16,17},{18,... | collective-permute-start | bytes 786440 | tf_op jit(solution)/shard_map/ppermute | solution.py:288
  46.5 0.0 collective-permute-done.6.refs_4_
  46.5 0.0 copy-done.7
  46.5 0.0 copy-done.9
  46.5 0.7 %broadcast_select_fusion = f32[8,2,16,256]{3,2,1,0:T(8,128)} fusion(f32[8,2,16,256]{3,2,1,0:T(8,128)S(1)} %collective-permute-done.6.refs_4_, pred[]{:T(512)S(6)} %eq.9, f32[4,2,16,256]{3,2,1,0:T(8,128)S(1)} %copy-done.7, f32[4,2,16,256]{3,2,1,0:T(8,128)S(1)} %copy-done.9), kind=kLoop, calls=%fused_computation.2 | loop fusion | flops 131072 | bytes 786433 | tf_op jit(solution)/shard_map/jit(_where)/select_n | solution.py:286
  47.2 1.3 %collective-permute-start.7 = (f32[8,2,16,256]{3,2,1,0:T(8,128)}, f32[8,2,16,256]{3,2,1,0:T(8,128)}, u32[]{:S(2)}, u32[]{:S(2)}) collective-permute-start(f32[8,2,16,256]{3,2,1,0:T(8,128)} %broadcast_select_fusion), channel_id=1, source_target_pairs={{0,1},{2,3},{4,5},{6,7},{9,8},{11,10},{13,12},{15,14},{18,19},{16,... | collective-permute-start | bytes 786440 | tf_op jit(solution)/shard_map/ppermute | solution.py:288
  48.5 12.9 %all-to-all-done.1.strips_ref = f32[8,128,256]{2,1,0:T(8,128)S(1)} async-done(((f32[8,128,256]{2,1,0:T(8,128)}), f32[8,128,256]{2,1,0:T(8,128)S(1)}, u32[]{:S(2)}, u32[]{:S(2)}) %all-to-all-start.1) | async-done | bytes 1048608 | tf_op jit(solution)/shard_map/all_to_all | solution.py:310
  61.4 0.0 copy-done.1
  61.4 0.0 copy-start.4
  61.4 0.7 assemble.1.base_ref
  62.1 1.4 %collective-permute-done.5.refs_2_ = f32[256,256]{1,0:T(8,128)S(1)} collective-permute-done((f32[256,256]{1,0:T(8,128)}, f32[256,256]{1,0:T(8,128)S(1)}, u32[]{:S(2)}, u32[]{:S(2)}) %collective-permute-start.5) | collective-permute-done | bytes 262176 | tf_op jit(solution)/shard_map/ppermute | solution.py:288
  63.6 5.0 %collective-permute-done.7.refs_5_ = f32[8,2,16,256]{3,2,1,0:T(8,128)} collective-permute-done((f32[8,2,16,256]{3,2,1,0:T(8,128)}, f32[8,2,16,256]{3,2,1,0:T(8,128)}, u32[]{:S(2)}, u32[]{:S(2)}) %collective-permute-start.7) | collective-permute-done | bytes 262176 | tf_op jit(solution)/shard_map/ppermute | solution.py:288
  68.6 0.0 copy-done.4
  68.6 3.7 %finish.1 = f32[512,256]{1,0:T(8,128)} custom-call(f32[512,256]{1,0:T(8,128)S(1)} %assemble.1.base_ref, f32[4,4,16,256]{3,2,1,0:T(8,128)S(1)} %pad_maximum_fusion.refs_0_.near_ref, f32[4,4,16,256]{3,2,1,0:T(8,128)S(1)} %collective-permute-done.3.refs_1_.far_ref, f32[128,128]{1,0:T(8,128)S(1)} %get-tuple-element.29.upper_ref, ...), custom_call_target="tpu_custom_call" | custom-call | tf_op jit(solution)/shard_map/finish/pallas_call | solution.py:365
  (6 shorter events, 0.1 us)
Async XLA Ops:
  0.0 0.7 copy-start.5
  0.7 1.0 %copy-start = (f32[512,256]{1,0:T(8,128)S(1)}, f32[512,256]{1,0:T(8,128)}, u32[]{:S(2)}) copy-start(f32[512,256]{1,0:T(8,128)} %front_ref.3) | copy-start | bytes 1572868
  1.7 1.2 %copy-start.2 = (f32[1,128,2048]{2,1,0:T(8,128)S(1)}, f32[1,128,2048]{2,1,0:T(8,128)}, u32[]{:S(2)}) copy-start(f32[1,128,2048]{2,1,0:T(8,128)} %param.6) | copy-start | bytes 3145732
  23.6 5.1 %collective-permute-start.2 = (f32[4,16,256]{2,1,0:T(8,128)S(1)}, f32[4,16,256]{2,1,0:T(8,128)S(1)}, u32[]{:S(2)}, u32[]{:S(2)}) collective-permute-start(f32[4,16,256]{2,1,0:T(8,128)S(1)} %reduce_sum.9), channel_id=1, source_target_pairs={{0,12},{4,8},{8,4},{12,0},{1,13},{5,9},{9,5},{13,1},{2,14},{6,10},... | collective-permute-start | bytes 196616 | tf_op jit(solution)/shard_map/ppermute | solution.py:308
  24.9 7.6 %collective-permute-start.1 = (f32[4,16,256]{2,1,0:T(8,128)S(1)}, f32[4,16,256]{2,1,0:T(8,128)S(1)}, u32[]{:S(2)}, u32[]{:S(2)}) collective-permute-start(f32[4,16,256]{2,1,0:T(8,128)S(1)} %reduce_sum.9), channel_id=1, source_target_pairs={{0,8},{4,12},{8,0},{12,4},{1,9},{5,13},{9,1},{13,5},{2,10},{6,14},... | collective-permute-start | bytes 196616 | tf_op jit(solution)/shard_map/ppermute | solution.py:308
  25.5 7.0 %collective-permute-start = (f32[4,16,256]{2,1,0:T(8,128)S(1)}, f32[4,16,256]{2,1,0:T(8,128)S(1)}, u32[]{:S(2)}, u32[]{:S(2)}) collective-permute-start(f32[4,16,256]{2,1,0:T(8,128)S(1)} %reduce_sum.9), channel_id=1, source_target_pairs={{0,4},{4,0},{8,12},{12,8},{1,5},{5,1},{9,13},{13,9},{2,6},{6,2},{1... | collective-permute-start | bytes 196616 | tf_op jit(solution)/shard_map/ppermute | solution.py:308
  32.5 7.1 %collective-permute-start.3 = (f32[4,4,16,256]{3,2,1,0:T(8,128)S(1)}, f32[4,4,16,256]{3,2,1,0:T(8,128)S(1)}, u32[]{:S(2)}, u32[]{:S(2)}) collective-permute-start(f32[4,4,16,256]{3,2,1,0:T(8,128)S(1)} %pad_maximum_fusion.refs_0_.near_ref), channel_id=1, source_target_pairs={{0,16},{16,0},{1,17},{17,1},{2,18},{18,2},{3,19},{19,3},{4,20},{20... | collective-permute-start | bytes 786440 | tf_op jit(solution)/shard_map/ppermute | solution.py:311
  32.6 28.8 %all-to-all-start.1 = ((f32[8,128,256]{2,1,0:T(8,128)}), f32[8,128,256]{2,1,0:T(8,128)S(1)}, u32[]{:S(2)}, u32[]{:S(2)}) async-start(f32[8,128,256]{2,1,0:T(8,128)} %get-tuple-element.21), calls=%async_computation.1 | async-start | bytes 2097152 | tf_op jit(solution)/shard_map/all_to_all | solution.py:310
  39.6 0.6 copy-start.3
  40.2 4.1 %collective-permute-start.4 = (f32[256,256]{1,0:T(8,128)S(1)}, f32[256,256]{1,0:T(8,128)S(1)}, u32[]{:S(2)}, u32[]{:S(2)}) collective-permute-start(f32[256,256]{1,0:T(8,128)S(1)} %get-tuple-element.27.refs_0_), channel_id=1, source_target_pairs={{0,2},{4,6},{8,10},{12,14},{16,18},{20,22},{24,26},{28,30}} | collective-permute-start | bytes 786440 | tf_op jit(solution)/shard_map/ppermute | solution.py:285
  41.0 0.7 copy-start.6
  41.0 0.7 copy-start.8
  41.7 4.8 %collective-permute-start.6 = (f32[8,2,16,256]{3,2,1,0:T(8,128)S(1)}, f32[8,2,16,256]{3,2,1,0:T(8,128)S(1)}, u32[]{:S(2)}, u32[]{:S(2)}) collective-permute-start(f32[8,2,16,256]{3,2,1,0:T(8,128)S(1)} %pad_maximum_fusion.1.refs_3_), channel_id=1, source_target_pairs={{0,2},{4,6},{9,11},{13,15},{18,16},{22,20},{27,25},{31,29}} | collective-permute-start | bytes 786440 | tf_op jit(solution)/shard_map/ppermute | solution.py:285
  42.4 0.7 copy-start.10
  44.3 2.2 %copy-start.7 = (f32[4,2,16,256]{3,2,1,0:T(8,128)S(1)}, f32[4,2,16,256]{3,2,1,0:T(8,128)}, u32[]{:S(2)}) copy-start(f32[4,2,16,256]{3,2,1,0:T(8,128)} %copy-done.6) | copy-start | bytes 393220
  44.3 2.2 %copy-start.9 = (f32[4,2,16,256]{3,2,1,0:T(8,128)S(1)}, f32[4,2,16,256]{3,2,1,0:T(8,128)}, u32[]{:S(2)}) copy-start(f32[4,2,16,256]{3,2,1,0:T(8,128)} %copy-done.8) | copy-start | bytes 393220
  45.1 16.4 %copy-start.1 = (f32[512,256]{1,0:T(8,128)S(1)}, f32[512,256]{1,0:T(8,128)}, u32[]{:S(2)}) copy-start(f32[512,256]{1,0:T(8,128)} %front_ref.3) | copy-start | bytes 1572868
  45.1 18.5 %collective-permute-start.5 = (f32[256,256]{1,0:T(8,128)}, f32[256,256]{1,0:T(8,128)S(1)}, u32[]{:S(2)}, u32[]{:S(2)}) collective-permute-start(f32[256,256]{1,0:T(8,128)} %broadcast_select_fusion.1), channel_id=1, source_target_pairs={{0,1},{2,3},{4,5},{6,7},{8,9},{10,11},{12,13},{14,15},{16,17},{18,... | collective-permute-start | bytes 786440 | tf_op jit(solution)/shard_map/ppermute | solution.py:288
  47.2 21.3 %collective-permute-start.7 = (f32[8,2,16,256]{3,2,1,0:T(8,128)}, f32[8,2,16,256]{3,2,1,0:T(8,128)}, u32[]{:S(2)}, u32[]{:S(2)}) collective-permute-start(f32[8,2,16,256]{3,2,1,0:T(8,128)} %broadcast_select_fusion), channel_id=1, source_target_pairs={{0,1},{2,3},{4,5},{6,7},{9,8},{11,10},{13,12},{15,14},{18,19},{16,... | collective-permute-start | bytes 786440 | tf_op jit(solution)/shard_map/ppermute | solution.py:288
  61.4 7.2 %copy-start.4 = (f32[128,128]{1,0:T(8,128)S(1)}, f32[128,128]{1,0:T(8,128)}, u32[]{:S(2)}) copy-start(f32[128,128]{1,0:T(8,128)} %copy-done.3) | copy-start | bytes 196612

commit v7 on v6

--- a/solution.py
+++ b/solution.py
@@ -141,34 +141,28 @@
         inverse_ref[BLK:, :BLK] = -dot(second, dot(side_ref[...], first, 0, 0), 1, 0)
 
 
-def split_kernel(map_ref, strip_ref, front_ref, sums_ref, out_ref, inv_ref):
-    owners, row_blocks, part, width = sums_ref.shape
+def split_kernel(map_ref, strip_ref, panel_ref, out_ref, inv_ref):
+    owners, part, width = panel_ref.shape
     per = width // BLK
-    grp, row, col = (lax.axis_index(a) for a in ("grp", "row", "col"))
-    n_row, n_col = lax.axis_size("row"), lax.axis_size("col")
-    me = grp * n_row + row
+    grp = lax.axis_index("grp")
     for q in range(map_ref.shape[1]):
         inv_ref[map_ref[grp, q]] = q
-    mine = map_ref[grp, row * n_col + col] - col * row_blocks
-    for s in range(per):
-        at = pl.multiple_of(inv_ref[s] * BLK, BLK)
-        lanes = slice(s * BLK, (s + 1) * BLK)
-        for k in range(owners):
-            piece = strip_ref[part * k : part * (k + 1), pl.ds(at, BLK)]
-            for b in range(row_blocks):
-                sums_ref[k, b, :, lanes] = jnp.where(mine == b, piece, 0.0)
-
-    @pl.when(me == 0)
-    def _():
-        for k in range(owners):
-            for b in range(row_blocks):
-                at = b * BLK + part * k
-                sums_ref[k, b] = sums_ref[k, b] + front_ref[at : at + part, :]
-
     for k in range(owners):
         for s in range(per):
             at = pl.multiple_of(inv_ref[k * per + s] * BLK, BLK)
             out_ref[k, :, s * BLK : (s + 1) * BLK] = strip_ref[:, pl.ds(at, BLK)]
+    for k in range(owners):
+        panel_ref[k] = out_ref[0, part * k : part * (k + 1), :]
+
+
+def sum_panel_kernel(map_ref, low_ref, high_ref, pieces_ref, out_ref):
+    n_row, n_col = lax.axis_size("row"), lax.axis_size("col")
+    grp, col = lax.axis_index("grp"), lax.axis_index("col")
+    blocks = out_ref.shape[0]
+    out_ref[...] = jnp.where(grp == 0, low_ref[...], high_ref[...])
+    for i in range(pieces_ref.shape[0]):
+        local = map_ref[i // n_row, i % n_row * n_col + col] - col * blocks
+        out_ref[local] = out_ref[local] + pieces_ref[i]
 
 
 def place_rows(target_ref, pieces_ref, grp):
@@ -293,18 +287,32 @@
     rows, width = front.shape
     row_blocks = rows // BLK
     part = BLK // owners
-    sums, strips = pl.pallas_call(
+    n_row = lax.axis_size("row")
+    cut = front.reshape(row_blocks, owners // n_row, n_row, part, width)
+    got = jnp.where(owner_of() == 0, cut[:, :, 0], 0.0)
+    for r in range(1, n_row):
+        got = got + lax.ppermute(cut[:, :, r], OWNER, [(0, r)])
+    low = got[:, 0]
+    high = lax.ppermute(got[:, 1], OWNER, [(r, n_row + r) for r in range(n_row)])
+    panel, strips = pl.pallas_call(
         split_kernel,
-        out_shape=[f32(owners, row_blocks, part, width), f32(owners, BLK, width)],
-        in_specs=[SMEM, VMEM, VMEM],
+        out_shape=[f32(owners, part, width), f32(owners, BLK, width)],
+        in_specs=[SMEM, VMEM],
         out_specs=[VMEM] * 2,
         scratch_shapes=[pltpu.SMEM((child_map.shape[1],), jnp.int32)],
         compiler_params=PARAMS,
         name="split",
-    )(child_map, strip, front)
-    mine = jnp.sum(lax.all_to_all(sums, OWNER, split_axis=0, concat_axis=0, tiled=True), axis=0)
+    )(child_map, strip)
+    pieces = lax.all_to_all(panel, OWNER, split_axis=0, concat_axis=0, tiled=True)
+    mine = pl.pallas_call(
+        sum_panel_kernel,
+        out_shape=f32(row_blocks, part, width),
+        in_specs=[SMEM, VMEM, VMEM, VMEM],
+        out_specs=VMEM,
+        compiler_params=PARAMS,
+        name="sum_panel",
+    )(child_map, low, high, pieces)
     strips, mine = lax.optimization_barrier((strips, mine))
-    n_row = lax.axis_size("row")
     others = [lax.ppermute(mine, "row", [(i, i ^ d) for i in range(n_row)]) for d in range(1, n_row)]
     near = jnp.stack([mine] + others)
     strips = lax.all_to_all(strips, OWNER, split_axis=0, concat_axis=0, tiled=True)

time: 72.8 us -> 69.4 us (0.953)
  blocking collectives: 18.9 us -> 0 us
  starting transfers between devices: 12.6 us -> 25.3 us
  waiting for transfers between devices: 26.7 us -> 30.5 us
  local copies, waits for them, and re-layouts: 5.53 us -> 3.85 us
    all_to_all x1 -> x0, blocking collectives: 18.9 us -> none  [gather_pieces(): lax.all_to_all(sums, OWNER, split_axis=0, concat_axis=0, tiled=True)]
    all_to_all x0 -> x1, starting transfers between devices: none -> 9.34 us  [gather_pieces(): lax.all_to_all(panel, OWNER, split_axis=0, concat_axis=0, tiled=True)]
    ppermute x0 -> x4, waiting for transfers between devices: none -> 4.02 us  [the longest x1 4.02 us: gather_pieces(): lax.ppermute(got[:, 1], OWNER, [(r, n_row + r) for r in range(n_row)])]
    ppermute x0 -> x4, starting transfers between devices: none -> 3.3 us  [the longest x3 2.01 us: gather_pieces(): got = got + lax.ppermute(cut[:, :, r], OWNER, [(0, r)])]
    unnamed x22 -> x23, local copies, waits for them, and re-layouts: 4.92 us -> 2.01 us
    ppermute x2, waiting for transfers between devices: 6.45 us -> 8.25 us  [over_col(): return ([value, over_x, lax.ppermute(held, axes, other)], held)]
    ppermute x1, waiting for transfers between devices: 2.05 us -> 0.57 us  [gather_pieces(): far = lax.ppermute(near, 'grp', [(0, 1), (1, 0)])]
    ppermute x1, starting transfers between devices: 0.07 us -> 1.38 us  [gather_pieces(): far = lax.ppermute(near, 'grp', [(0, 1), (1, 0)])]
  transfers between devices with their start and end apart: 9 -> 14, of which waited for: 6 -> 7; matrix products, arithmetic and copies ran while one was open for 3% -> 3% of each run, Pallas kernels for 1% -> 4%
where the time goes in v7:
time: 69.4 us; the launch traced here: 68.9 us
  waiting for transfers between devices  30.5 us (44%)
  starting transfers between devices  25.3 us (36%)
  Pallas kernels  6.77 us (10%)
  local copies, waits for them, and re-layouts  3.85 us (6%)
  other arithmetic  1.57 us (2%)
  between operations  0.95 us (1%)
    all_to_all x1, waiting for transfers between devices, gather_pieces(): lax.all_to_all(strips, OWNER, split_axis=0, concat_axis=0, tiled=True)  13 us
    all_to_all x1, starting transfers between devices, gather_pieces(): lax.all_to_all(panel, OWNER, split_axis=0, concat_axis=0, tiled=True)  9.34 us
    ppermute x2, waiting for transfers between devices, over_col(): return ([value, over_x, lax.ppermute(held, axes, other)], held)  8.25 us
    ppermute x3, waiting for transfers between devices, gather_pieces(): lax.ppermute(mine, 'row', [(i, i ^ d) for i in range(n_row)])  4.61 us
    ppermute x1, waiting for transfers between devices, gather_pieces(): lax.ppermute(got[:, 1], OWNER, [(r, n_row + r) for r in range(n_row)])  4.02 us
    pallas_call x1, Pallas kernels, body(): pl.pallas_call(functools.partial(finish_kernel, few), out_shape=f32(rows,...  3.74 us
    all_to_all x1, starting transfers between devices, gather_pieces(): lax.all_to_all(strips, OWNER, split_axis=0, concat_axis=0, tiled=True)  3.63 us
    ppermute x3, starting transfers between devices, gather_pieces(): lax.ppermute(mine, 'row', [(i, i ^ d) for i in range(n_row)])  3.61 us
  transfers between devices with their start and end apart: 14, of which 7 were waited for; matrix products, arithmetic and copies ran while one was open for 3% of the time, Pallas kernels for 4%

profile of v7, /device:TPU:5, one launch (start us, length us, event | category | flops | bytes accessed | tf_op | source)
XLA Modules:
  0.0 68.9 jit_solution(17090003042172812767)
XLA Ops:
  0.0 0.0 copy-start.1
  0.0 1.2 %fusion.4 = (f32[4,2,1,16,256]{4,3,2,1,0:T(8,128)S(1)}, f32[4,2,1,16,256]{4,3,2,1,0:T(8,128)S(1)}, f32[4,2,1,16,256]{4,3,2,1,0:T(8,128)S(1)}, f32[4,2,1,16,256]{4,3,2,1,0:T(8,128)S(1)}) fusion(f32[4,2,4,16,256]{4,3,2,1,0:T(8,128)} %bitcast.28), kind=kLoop, calls=%fused_computation.16 | loop fusion | bytes 1048576 | tf_op jit(solution)/shard_map/slice | solution.py:292
  1.2 0.7 collective-permute-start.2
  1.9 0.7 collective-permute-start.1
  2.6 0.0 copy-start.4
  2.6 0.7 collective-permute-start
  3.3 0.0 copy-done.1
  3.3 0.0 copy-done.4
  3.3 1.7 %split.1 = (f32[8,16,256]{2,1,0:T(8,128)}, f32[8,128,256]{2,1,0:T(8,128)}) custom-call(s32[2,16]{1,0:T(2,128)S(1)} %copy-done.4, f32[128,2048]{1,0:T(8,128)S(1)} %bitcast.29), custom_call_target="tpu_custom_call" | custom-call | tf_op jit(solution)/shard_map/split/pallas_call | solution.py:297
  5.1 9.3 %all-to-all-start = ((f32[8,16,256]{2,1,0:T(8,128)}), f32[8,16,256]{2,1,0:T(8,128)S(1)}, u32[]{:S(2)}, u32[]{:S(2)}) async-start(f32[8,16,256]{2,1,0:T(8,128)} %get-tuple-element.20), calls=%async_computation | async-start | bytes 262144 | tf_op jit(solution)/shard_map/all_to_all | solution.py:306
  14.4 0.0 collective-permute-done.2
  14.4 0.0 collective-permute-done.1
  14.4 0.0 collective-permute-done
  14.5 1.3 %collective-permute-start.3 = (f32[4,16,256]{2,1,0:T(8,128)S(1)}, f32[4,16,256]{2,1,0:T(8,128)S(1)}, u32[]{:S(2)}, u32[]{:S(2)}) collective-permute-start(f32[4,16,256]{2,1,0:T(8,128)S(1)} %get-tuple-element.37), channel_id=1, source_target_pairs={{0,16},{4,20},{8,24},{12,28},{1,17},{5,21},{9,25},{13,29},{2,18},{... | collective-permute-start | bytes 196616 | tf_op jit(solution)/shard_map/ppermute | solution.py:296
  15.8 4.0 %collective-permute-done.3.high_ref = f32[4,16,256]{2,1,0:T(8,128)S(1)} collective-permute-done((f32[4,16,256]{2,1,0:T(8,128)S(1)}, f32[4,16,256]{2,1,0:T(8,128)S(1)}, u32[]{:S(2)}, u32[]{:S(2)}) %collective-permute-start.3) | collective-permute-done | bytes 65568 | tf_op jit(solution)/shard_map/ppermute | solution.py:296
  19.8 0.0 all-to-all-done.pieces_ref
  19.8 0.6 sum_panel.1
  20.4 2.8 %collective-permute-start.6 = (f32[4,16,256]{2,1,0:T(8,128)S(1)}, f32[4,16,256]{2,1,0:T(8,128)S(1)}, u32[]{:S(2)}, u32[]{:S(2)}) collective-permute-start(f32[4,16,256]{2,1,0:T(8,128)S(1)} %sum_panel.1), channel_id=1, source_target_pairs={{0,12},{4,8},{8,4},{12,0},{1,13},{5,9},{9,5},{13,1},{2,14},{6,10},... | collective-permute-start | bytes 196616 | tf_op jit(solution)/shard_map/ppermute | solution.py:316
  23.2 0.0 collective-permute-start.5
  23.2 0.8 %collective-permute-start.4 = (f32[4,16,256]{2,1,0:T(8,128)S(1)}, f32[4,16,256]{2,1,0:T(8,128)S(1)}, u32[]{:S(2)}, u32[]{:S(2)}) collective-permute-start(f32[4,16,256]{2,1,0:T(8,128)S(1)} %sum_panel.1), channel_id=1, source_target_pairs={{0,4},{4,0},{8,12},{12,8},{1,5},{5,1},{9,13},{13,9},{2,6},{6,2},{1... | collective-permute-start | bytes 196616 | tf_op jit(solution)/shard_map/ppermute | solution.py:316
  24.0 1.4 %collective-permute-done.6 = f32[4,16,256]{2,1,0:T(8,128)S(1)} collective-permute-done((f32[4,16,256]{2,1,0:T(8,128)S(1)}, f32[4,16,256]{2,1,0:T(8,128)S(1)}, u32[]{:S(2)}, u32[]{:S(2)}) %collective-permute-start.6) | collective-permute-done | bytes 65568 | tf_op jit(solution)/shard_map/ppermute | solution.py:316
  25.4 3.2 %collective-permute-done.5 = f32[4,16,256]{2,1,0:T(8,128)S(1)} collective-permute-done((f32[4,16,256]{2,1,0:T(8,128)S(1)}, f32[4,16,256]{2,1,0:T(8,128)S(1)}, u32[]{:S(2)}, u32[]{:S(2)}) %collective-permute-start.5) | collective-permute-done | bytes 65568 | tf_op jit(solution)/shard_map/ppermute | solution.py:316
  28.6 0.0 collective-permute-done.4
  28.7 1.4 %collective-permute-start.7 = (f32[4,4,16,256]{3,2,1,0:T(8,128)S(1)}, f32[4,4,16,256]{3,2,1,0:T(8,128)S(1)}, u32[]{:S(2)}, u32[]{:S(2)}) collective-permute-start(f32[4,4,16,256]{3,2,1,0:T(8,128)S(1)} %pad_maximum_fusion.refs_0_.near_ref), channel_id=1, source_target_pairs={{0,16},{16,0},{1,17},{17,1},{2,18},{18,2},{3,19},{19,3},{4,20},{20... | collective-permute-start | bytes 786440 | tf_op jit(solution)/shard_map/ppermute | solution.py:319
  30.0 3.6 %all-to-all-start.1 = ((f32[8,128,256]{2,1,0:T(8,128)}), f32[8,128,256]{2,1,0:T(8,128)S(1)}, u32[]{:S(2)}, u32[]{:S(2)}) async-start(f32[8,128,256]{2,1,0:T(8,128)} %get-tuple-element.21), calls=%async_computation.1 | async-start | bytes 2097152 | tf_op jit(solution)/shard_map/all_to_all | solution.py:318
  33.7 0.6 collective-permute-done.7.refs_1_.far_ref
  34.3 0.0 copy-start.2
  34.3 0.6 copy-done.2
  34.9 0.7 collective-permute-start.8
  35.6 0.0 copy-start.5
  35.6 0.0 copy-start.7
  35.6 0.6 copy-done.5
  36.3 0.1 copy-done.7
  36.3 0.7 collective-permute-start.10
  37.0 0.0 copy-start.9
  37.0 0.6 copy-done.9
  37.7 0.6 dynamic_slice.15
  38.9 0.0 copy-start.6
  38.9 0.0 copy-start.8
  38.9 0.0 collective-permute-done.8.refs_1_
  39.0 0.7 %broadcast_select_fusion.1 = f32[256,256]{1,0:T(8,128)} fusion(f32[256,256]{1,0:T(8,128)S(1)} %get-tuple-element.27.refs_0_, f32[256,256]{1,0:T(8,128)S(1)} %collective-permute-done.8.refs_1_, pred[]{:T(512)S(6)} %eq.12), kind=kLoop, calls=%fused_computation.11 | loop fusion | flops 65536 | bytes 786433 | tf_op jit(solution)/shard_map/jit(_where)/select_n | solution.py:280
  39.7 0.0 copy-start
  39.7 1.4 %collective-permute-start.9 = (f32[256,256]{1,0:T(8,128)}, f32[256,256]{1,0:T(8,128)S(1)}, u32[]{:S(2)}, u32[]{:S(2)}) collective-permute-start(f32[256,256]{1,0:T(8,128)} %broadcast_select_fusion.1), channel_id=1, source_target_pairs={{0,1},{2,3},{4,5},{6,7},{8,9},{10,11},{12,13},{14,15},{16,17},{18,... | collective-permute-start | bytes 786440 | tf_op jit(solution)/shard_map/ppermute | solution.py:282
  41.1 0.0 collective-permute-done.10.refs_4_
  41.1 0.0 copy-done.6
  41.1 0.0 copy-done.8
  41.2 0.8 %broadcast_select_fusion = f32[8,2,16,256]{3,2,1,0:T(8,128)} fusion(f32[8,2,16,256]{3,2,1,0:T(8,128)S(1)} %collective-permute-done.10.refs_4_, pred[]{:T(512)S(6)} %eq.13, f32[4,2,16,256]{3,2,1,0:T(8,128)S(1)} %copy-done.6, f32[4,2,16,256]{3,2,1,0:T(8,128)S(1)} %copy-done.8), kind=kLoop, calls=%fused_computation.10 | loop fusion | flops 131072 | bytes 786433 | tf_op jit(solution)/shard_map/jit(_where)/select_n | solution.py:280
  41.9 1.3 %collective-permute-start.11 = (f32[8,2,16,256]{3,2,1,0:T(8,128)}, f32[8,2,16,256]{3,2,1,0:T(8,128)}, u32[]{:S(2)}, u32[]{:S(2)}) collective-permute-start(f32[8,2,16,256]{3,2,1,0:T(8,128)} %broadcast_select_fusion), channel_id=1, source_target_pairs={{0,1},{2,3},{4,5},{6,7},{9,8},{11,10},{13,12},{15,14},{18,19},{16,... | collective-permute-start | bytes 786440 | tf_op jit(solution)/shard_map/ppermute | solution.py:282
  43.2 13.0 %all-to-all-done.1.strips_ref = f32[8,128,256]{2,1,0:T(8,128)S(1)} async-done(((f32[8,128,256]{2,1,0:T(8,128)}), f32[8,128,256]{2,1,0:T(8,128)S(1)}, u32[]{:S(2)}, u32[]{:S(2)}) %all-to-all-start.1) | async-done | bytes 1048608 | tf_op jit(solution)/shard_map/all_to_all | solution.py:318
  56.2 0.0 copy-done
  56.2 0.0 copy-start.3
  56.2 0.7 %assemble.1.base_ref = f32[512,256]{1,0:T(8,128)S(1)} custom-call(s32[2,16]{1,0:T(2,128)S(1)} %copy-done.4, f32[512,256]{1,0:T(8,128)S(1)} %copy-done, f32[8,128,256]{2,1,0:T(8,128)S(1)} %all-to-all-done.1.strips_ref), custom_call_target="tpu_custom_call" | custom-call | tf_op jit(solution)/shard_map/assemble/pallas_call | solution.py:363
  56.9 3.2 %collective-permute-done.9.refs_2_ = f32[256,256]{1,0:T(8,128)S(1)} collective-permute-done((f32[256,256]{1,0:T(8,128)}, f32[256,256]{1,0:T(8,128)S(1)}, u32[]{:S(2)}, u32[]{:S(2)}) %collective-permute-start.9) | collective-permute-done | bytes 262176 | tf_op jit(solution)/shard_map/ppermute | solution.py:282
  60.1 5.0 %collective-permute-done.11.refs_5_ = f32[8,2,16,256]{3,2,1,0:T(8,128)} collective-permute-done((f32[8,2,16,256]{3,2,1,0:T(8,128)}, f32[8,2,16,256]{3,2,1,0:T(8,128)}, u32[]{:S(2)}, u32[]{:S(2)}) %collective-permute-start.11) | collective-permute-done | bytes 262176 | tf_op jit(solution)/shard_map/ppermute | solution.py:282
  65.2 0.0 copy-done.3
  65.2 3.7 %finish.1 = f32[512,256]{1,0:T(8,128)} custom-call(f32[512,256]{1,0:T(8,128)S(1)} %assemble.1.base_ref, f32[4,4,16,256]{3,2,1,0:T(8,128)S(1)} %pad_maximum_fusion.refs_0_.near_ref, f32[4,4,16,256]{3,2,1,0:T(8,128)S(1)} %collective-permute-done.7.refs_1_.far_ref, f32[128,128]{1,0:T(8,128)S(1)} %get-tuple-element.29.upper_ref, ...), custom_call_target="tpu_custom_call" | custom-call | tf_op jit(solution)/shard_map/finish/pallas_call | solution.py:373
  (10 shorter events, 0.1 us)
Async XLA Ops:
  0.0 3.3 %copy-start.1 = (f32[1,128,2048]{2,1,0:T(8,128)S(1)}, f32[1,128,2048]{2,1,0:T(8,128)}, u32[]{:S(2)}) copy-start(f32[1,128,2048]{2,1,0:T(8,128)} %param.6) | copy-start | bytes 3145732
  1.2 13.2 %collective-permute-start.2 = (f32[4,2,16,256]{3,2,0,1:T(8,128)S(1)}, f32[4,2,16,256]{3,2,0,1:T(8,128)S(1)}, u32[]{:S(2)}, u32[]{:S(2)}) collective-permute-start(f32[4,2,16,256]{3,2,0,1:T(8,128)S(1)} %bitcast.31), channel_id=1, source_target_pairs={{0,12},{1,13},{2,14},{3,15}} | collective-permute-start | bytes 393224 | tf_op jit(solution)/shard_map/ppermute | solution.py:294
  1.9 12.5 %collective-permute-start.1 = (f32[4,2,16,256]{3,2,0,1:T(8,128)S(1)}, f32[4,2,16,256]{3,2,0,1:T(8,128)S(1)}, u32[]{:S(2)}, u32[]{:S(2)}) collective-permute-start(f32[4,2,16,256]{3,2,0,1:T(8,128)S(1)} %bitcast.32), channel_id=1, source_target_pairs={{0,8},{1,9},{2,10},{3,11}} | collective-permute-start | bytes 393224 | tf_op jit(solution)/shard_map/ppermute | solution.py:294
  2.6 0.7 %copy-start.4 = (s32[2,16]{1,0:T(2,128)S(1)}, s32[2,16]{1,0:T(2,128)}, u32[]{:S(2)}) copy-start(s32[2,16]{1,0:T(2,128)} %map_ref.5) | copy-start | bytes 388
  2.6 11.8 %collective-permute-start = (f32[4,2,16,256]{3,2,0,1:T(8,128)S(1)}, f32[4,2,16,256]{3,2,0,1:T(8,128)S(1)}, u32[]{:S(2)}, u32[]{:S(2)}) collective-permute-start(f32[4,2,16,256]{3,2,0,1:T(8,128)S(1)} %bitcast.33), channel_id=1, source_target_pairs={{0,4},{1,5},{2,6},{3,7}} | collective-permute-start | bytes 393224 | tf_op jit(solution)/shard_map/ppermute | solution.py:294
  5.1 14.7 %all-to-all-start = ((f32[8,16,256]{2,1,0:T(8,128)}), f32[8,16,256]{2,1,0:T(8,128)S(1)}, u32[]{:S(2)}, u32[]{:S(2)}) async-start(f32[8,16,256]{2,1,0:T(8,128)} %get-tuple-element.20), calls=%async_computation | async-start | bytes 262144 | tf_op jit(solution)/shard_map/all_to_all | solution.py:306
  14.5 5.3 %collective-permute-start.3 = (f32[4,16,256]{2,1,0:T(8,128)S(1)}, f32[4,16,256]{2,1,0:T(8,128)S(1)}, u32[]{:S(2)}, u32[]{:S(2)}) collective-permute-start(f32[4,16,256]{2,1,0:T(8,128)S(1)} %get-tuple-element.37), channel_id=1, source_target_pairs={{0,16},{4,20},{8,24},{12,28},{1,17},{5,21},{9,25},{13,29},{2,18},{... | collective-permute-start | bytes 196616 | tf_op jit(solution)/shard_map/ppermute | solution.py:296
  20.4 5.0 %collective-permute-start.6 = (f32[4,16,256]{2,1,0:T(8,128)S(1)}, f32[4,16,256]{2,1,0:T(8,128)S(1)}, u32[]{:S(2)}, u32[]{:S(2)}) collective-permute-start(f32[4,16,256]{2,1,0:T(8,128)S(1)} %sum_panel.1), channel_id=1, source_target_pairs={{0,12},{4,8},{8,4},{12,0},{1,13},{5,9},{9,5},{13,1},{2,14},{6,10},... | collective-permute-start | bytes 196616 | tf_op jit(solution)/shard_map/ppermute | solution.py:316
  23.2 5.5 %collective-permute-start.5 = (f32[4,16,256]{2,1,0:T(8,128)S(1)}, f32[4,16,256]{2,1,0:T(8,128)S(1)}, u32[]{:S(2)}, u32[]{:S(2)}) collective-permute-start(f32[4,16,256]{2,1,0:T(8,128)S(1)} %sum_panel.1), channel_id=1, source_target_pairs={{0,8},{4,12},{8,0},{12,4},{1,9},{5,13},{9,1},{13,5},{2,10},{6,14},... | collective-permute-start | bytes 196616 | tf_op jit(solution)/shard_map/ppermute | solution.py:316
  23.2 5.5 %collective-permute-start.4 = (f32[4,16,256]{2,1,0:T(8,128)S(1)}, f32[4,16,256]{2,1,0:T(8,128)S(1)}, u32[]{:S(2)}, u32[]{:S(2)}) collective-permute-start(f32[4,16,256]{2,1,0:T(8,128)S(1)} %sum_panel.1), channel_id=1, source_target_pairs={{0,4},{4,0},{8,12},{12,8},{1,5},{5,1},{9,13},{13,9},{2,6},{6,2},{1... | collective-permute-start | bytes 196616 | tf_op jit(solution)/shard_map/ppermute | solution.py:316
  28.7 5.6 %collective-permute-start.7 = (f32[4,4,16,256]{3,2,1,0:T(8,128)S(1)}, f32[4,4,16,256]{3,2,1,0:T(8,128)S(1)}, u32[]{:S(2)}, u32[]{:S(2)}) collective-permute-start(f32[4,4,16,256]{3,2,1,0:T(8,128)S(1)} %pad_maximum_fusion.refs_0_.near_ref), channel_id=1, source_target_pairs={{0,16},{16,0},{1,17},{17,1},{2,18},{18,2},{3,19},{19,3},{4,20},{20... | collective-permute-start | bytes 786440 | tf_op jit(solution)/shard_map/ppermute | solution.py:319
  30.0 26.2 %all-to-all-start.1 = ((f32[8,128,256]{2,1,0:T(8,128)}), f32[8,128,256]{2,1,0:T(8,128)S(1)}, u32[]{:S(2)}, u32[]{:S(2)}) async-start(f32[8,128,256]{2,1,0:T(8,128)} %get-tuple-element.21), calls=%async_computation.1 | async-start | bytes 2097152 | tf_op jit(solution)/shard_map/all_to_all | solution.py:318
  34.3 0.6 copy-start.2
  34.9 4.1 %collective-permute-start.8 = (f32[256,256]{1,0:T(8,128)S(1)}, f32[256,256]{1,0:T(8,128)S(1)}, u32[]{:S(2)}, u32[]{:S(2)}) collective-permute-start(f32[256,256]{1,0:T(8,128)S(1)} %get-tuple-element.27.refs_0_), channel_id=1, source_target_pairs={{0,2},{4,6},{8,10},{12,14},{16,18},{20,22},{24,26},{28,30}} | collective-permute-start | bytes 786440 | tf_op jit(solution)/shard_map/ppermute | solution.py:279
  35.6 0.6 copy-start.5
  35.6 0.7 %copy-start.7 = (f32[4,2,16,256]{3,2,1,0:T(8,128)}, f32[4,2,16,256]{3,2,1,0:T(8,128)S(1)}, u32[]{:S(2)}) copy-start(f32[4,2,16,256]{3,2,1,0:T(8,128)S(1)} %get-tuple-element.40) | copy-start | bytes 393220
  36.3 4.8 %collective-permute-start.10 = (f32[8,2,16,256]{3,2,1,0:T(8,128)S(1)}, f32[8,2,16,256]{3,2,1,0:T(8,128)S(1)}, u32[]{:S(2)}, u32[]{:S(2)}) collective-permute-start(f32[8,2,16,256]{3,2,1,0:T(8,128)S(1)} %pad_maximum_fusion.1.refs_3_), channel_id=1, source_target_pairs={{0,2},{4,6},{9,11},{13,15},{18,16},{22,20},{27,25},{31,29}} | collective-permute-start | bytes 786440 | tf_op jit(solution)/shard_map/ppermute | solution.py:279
  37.0 0.7 copy-start.9
  38.9 2.2 %copy-start.6 = (f32[4,2,16,256]{3,2,1,0:T(8,128)S(1)}, f32[4,2,16,256]{3,2,1,0:T(8,128)}, u32[]{:S(2)}) copy-start(f32[4,2,16,256]{3,2,1,0:T(8,128)} %copy-done.5) | copy-start | bytes 393220
  38.9 2.2 %copy-start.8 = (f32[4,2,16,256]{3,2,1,0:T(8,128)S(1)}, f32[4,2,16,256]{3,2,1,0:T(8,128)}, u32[]{:S(2)}) copy-start(f32[4,2,16,256]{3,2,1,0:T(8,128)} %copy-done.7) | copy-start | bytes 393220
  39.7 16.5 %copy-start = (f32[512,256]{1,0:T(8,128)S(1)}, f32[512,256]{1,0:T(8,128)}, u32[]{:S(2)}) copy-start(f32[512,256]{1,0:T(8,128)} %front_ref.1) | copy-start | bytes 1572868
  39.7 20.4 %collective-permute-start.9 = (f32[256,256]{1,0:T(8,128)}, f32[256,256]{1,0:T(8,128)S(1)}, u32[]{:S(2)}, u32[]{:S(2)}) collective-permute-start(f32[256,256]{1,0:T(8,128)} %broadcast_select_fusion.1), channel_id=1, source_target_pairs={{0,1},{2,3},{4,5},{6,7},{8,9},{10,11},{12,13},{14,15},{16,17},{18,... | collective-permute-start | bytes 786440 | tf_op jit(solution)/shard_map/ppermute | solution.py:282
  41.9 23.3 %collective-permute-start.11 = (f32[8,2,16,256]{3,2,1,0:T(8,128)}, f32[8,2,16,256]{3,2,1,0:T(8,128)}, u32[]{:S(2)}, u32[]{:S(2)}) collective-permute-start(f32[8,2,16,256]{3,2,1,0:T(8,128)} %broadcast_select_fusion), channel_id=1, source_target_pairs={{0,1},{2,3},{4,5},{6,7},{9,8},{11,10},{13,12},{15,14},{18,19},{16,... | collective-permute-start | bytes 786440 | tf_op jit(solution)/shard_map/ppermute | solution.py:282
  56.2 9.0 %copy-start.3 = (f32[128,128]{1,0:T(8,128)S(1)}, f32[128,128]{1,0:T(8,128)}, u32[]{:S(2)}) copy-start(f32[128,128]{1,0:T(8,128)} %copy-done.2) | copy-start | bytes 196612

commit v8 on v7

--- a/solution.py
+++ b/solution.py
@@ -121,7 +121,7 @@
             grp = lax.axis_index("grp")
             tops = PIVOTS // BLK
             place_rows(pivot_ref, sources[0].at[:, :tops], grp)
-            place_rows(pivot_ref, sources[1].at[:, :tops], 1 - grp)
+            place_rows(pivot_ref, sources[1], 1 - grp)
         else:
             pivot_ref[...] = sources[0][...]
         factor_half(pivot_ref[:BLK, :BLK], upper_ref, inverse_ref)
@@ -165,12 +165,12 @@
         out_ref[local] = out_ref[local] + pieces_ref[i]
 
 
-def place_rows(target_ref, pieces_ref, grp):
+def place_rows(target_ref, pieces_ref, grp, first=0):
     row = lax.axis_index("row")
     n_row, blocks, part, _ = pieces_ref.shape
     for b in range(blocks):
         for r in range(n_row):
-            at = pl.multiple_of(b * BLK + (grp * n_row + (row ^ r)) * part, SUB)
+            at = pl.multiple_of((first + b) * BLK + (grp * n_row + (row ^ r)) * part, SUB)
             target_ref[pl.ds(at, part), :] = pieces_ref[r, b]
 
 
@@ -190,8 +190,9 @@
         out_ref[pl.ds(start, BLK), :] += strips_ref[i]
 
 
-def finish_kernel(few, base_ref, near_ref, far_ref, upper_ref, side_ref, upper2_ref, *refs):
+def finish_kernel(few, base_ref, *refs):
     count = 3 if few else 1
+    panel, (upper_ref, side_ref, upper2_ref), refs = refs[:count], refs[count : count + 3], refs[count + 3 :]
     inverses, parts = refs[:count], refs[count : 2 * count]
     out_ref, rows_c_ref, rows_o_ref, inv_ref = refs[-4:]
     rows, width = out_ref.shape
@@ -209,12 +210,14 @@
     if few:
         choose(inverses, col, take_inverse)
         choose(parts, (me * width // rows) ^ col, take_part)
+        near_ref, far_top_ref, far_rest_ref = panel
         place_rows(rows_c_ref, near_ref, grp)
-        place_rows(rows_c_ref, far_ref, 1 - grp)
+        place_rows(rows_c_ref, far_top_ref, 1 - grp)
+        place_rows(rows_c_ref, far_rest_ref, 1 - grp, far_top_ref.shape[1])
     else:
         inv_ref[...] = inverses[0][...]
         rows_o_ref[...] = parts[0][...]
-        rows_c_ref[...] = near_ref[...]
+        rows_c_ref[...] = panel[0][...]
     inv = inv_ref[...]
     left = dot(rows_c_ref[...], inv, 1, 1)
 
@@ -269,15 +272,15 @@
         low = c * rows // width
         sent = from_root(part, "col", c)
         rows_o = jnp.where((me >= low) & (me < low + rows // width), sent, rows_o)
-    return assembled, (rows_c, rows_c), [pivot], rows_o
-
-
-def over_col(value, roots):
+    return assembled, [rows_c], [pivot], rows_o
+
+
+def over_col(value, roots, root):
     n_col = lax.axis_size("col")
     axes = OWNER + ("col",)
     cross = [(o * n_col + c, o * n_col + (c ^ 2)) for o, c in enumerate(roots)]
     over_x = lax.ppermute(value, axes, cross)
-    held = jnp.where(lax.axis_index("col") == jnp.array(roots)[owner_of()], value, over_x)
+    held = jnp.where(lax.axis_index("col") == root, value, over_x)
     other = [(o * n_col + (c ^ e), o * n_col + (c ^ e ^ 1)) for o, c in enumerate(roots) for e in (0, 2)]
     return [value, over_x, lax.ppermute(held, axes, other)], held
 
@@ -316,9 +319,8 @@
     others = [lax.ppermute(mine, "row", [(i, i ^ d) for i in range(n_row)]) for d in range(1, n_row)]
     near = jnp.stack([mine] + others)
     strips = lax.all_to_all(strips, OWNER, split_axis=0, concat_axis=0, tiled=True)
-    far = lax.ppermute(near, "grp", [(0, 1), (1, 0)])
-
-    return front, (near, far), [near, far], strips
+    far_top = lax.ppermute(near[:, : PIVOTS // BLK], "grp", [(0, 1), (1, 0)])
+    return front, [near], [near, far_top], strips
 
 
 def body(front, child_blocks, child_map):
@@ -327,6 +329,7 @@
     blocks = owners * width // BLK
     few = lax.axis_size("grp") == 2 and lax.axis_size("row") == 4 and lax.axis_size("col") == 4
     few = few and BLK % (owners * 8) == 0 and child_map.shape[1] == blocks
+    few = few and rows == 2 * width and width == PIVOTS
     gather = gather_pieces if few else gather_wide
     base, panel, pivot, last = gather(front, child_blocks[0], child_map)
     half = f32(BLK, BLK)
@@ -342,11 +345,17 @@
         name="pivot_first",
     )(*pivot)
     if few:
-        first, near, far = lax.optimization_barrier((first, *panel))
+        tops = PIVOTS // BLK
+        near, far_top = pivot
+        first, later = lax.optimization_barrier((first, near[:, tops:]))
+        far_rest = lax.ppermute(later, "grp", [(0, 1), (1, 0)])
+        panel = [near, far_top, far_rest]
+        root = owner_of() * width // rows
         at = owner_of() * width % rows // BLK
-        cut = lambda v: lax.dynamic_slice_in_dim(v, at, width // BLK, 1)
-        own_part = jnp.concatenate([cut(near), cut(far)], axis=0)
-        parts, _ = over_col(own_part, [o * width // rows for o in range(owners)])
+        cut_near = lax.dynamic_slice_in_dim(near, at, width // BLK, 1)
+        cut_far = jnp.where(at == 0, far_top, far_rest)
+        own_part = jnp.concatenate([cut_near, cut_far], axis=0)
+        parts, _ = over_col(own_part, [o * width // rows for o in range(owners)], root)
     upper2, inverse = pl.pallas_call(
         functools.partial(second_half_kernel, few),
         out_shape=[half, f32(PIVOTS, PIVOTS)],
@@ -358,7 +367,7 @@
         name="pivot_second",
     )(first, side, rest)
     if few:
-        inverses, held = over_col(inverse, [0] * owners)
+        inverses, held = over_col(inverse, [0] * owners, 0)
         strips, _ = lax.optimization_barrier((last, held))
         base = pl.pallas_call(
             assemble_kernel,
@@ -373,7 +382,7 @@
     return pl.pallas_call(
         functools.partial(finish_kernel, few),
         out_shape=f32(rows, width),
-        in_specs=[VMEM] * (6 + len(inverses) + len(parts)),
+        in_specs=[VMEM] * (4 + len(panel) + len(inverses) + len(parts)),
         out_specs=VMEM,
         scratch_shapes=[pltpu.VMEM((n, width), jnp.float32) for n in (rows, width, PIVOTS)],
         compiler_params=PARAMS,

time: 69.4 us -> 66.9 us (0.964)
  the two profiles are of different devices: /device:TPU:5 before, /device:TPU:27 now
where the time goes in v8:
time: 66.9 us; the launch traced here: 66.4 us
  starting transfers between devices  33.2 us (50%)
  waiting for transfers between devices  22.6 us (34%)
  Pallas kernels  6.76 us (10%)
  local copies, waits for them, and re-layouts  2.02 us (3%)
  other arithmetic  1.58 us (2%)
    ppermute x1, waiting for transfers between devices, body(): far_rest = lax.ppermute(later, 'grp', [(0, 1), (1, 0)])  11.9 us
    all_to_all x1, starting transfers between devices, gather_pieces(): lax.all_to_all(panel, OWNER, split_axis=0, concat_axis=0, tiled=True)  8.43 us
    all_to_all x1, starting transfers between devices, gather_pieces(): lax.all_to_all(strips, OWNER, split_axis=0, concat_axis=0, tiled=True)  5.99 us
    ppermute x2, starting transfers between devices, over_col(): return ([value, over_x, lax.ppermute(held, axes, other)], held)  5.73 us
    ppermute x2, waiting for transfers between devices, over_col(): over_x = lax.ppermute(value, axes, cross)  5.26 us
    ppermute x3, waiting for transfers between devices, gather_pieces(): lax.ppermute(mine, 'row', [(i, i ^ d) for i in range(n_row)])  4.02 us
    pallas_call x1, Pallas kernels, body(): pl.pallas_call(functools.partial(finish_kernel, few), out_shape=f32(rows,...  3.74 us
    ppermute x3, starting transfers between devices, gather_pieces(): lax.ppermute(mine, 'row', [(i, i ^ d) for i in range(n_row)])  3.61 us
  transfers between devices with their start and end apart: 15, of which 6 were waited for; matrix products, arithmetic and copies ran while one was open for 2% of the time, Pallas kernels for 4%

profile of v8, /device:TPU:27, one launch (start us, length us, event | category | flops | bytes accessed | tf_op | source)
XLA Modules:
  0.0 66.4 jit_solution(8622062028358828856)
XLA Ops:
  0.0 0.0 copy-start.1
  0.0 1.2 %fusion.4 = (f32[4,2,1,16,256]{4,3,2,1,0:T(8,128)S(1)}, f32[4,2,1,16,256]{4,3,2,1,0:T(8,128)S(1)}, f32[4,2,1,16,256]{4,3,2,1,0:T(8,128)S(1)}, f32[4,2,1,16,256]{4,3,2,1,0:T(8,128)S(1)}) fusion(f32[4,2,4,16,256]{4,3,2,1,0:T(8,128)} %bitcast.27), kind=kLoop, calls=%fused_computation.16 | loop fusion | bytes 1048576 | tf_op jit(solution)/shard_map/slice | solution.py:295
  1.2 1.3 %collective-permute-start.2 = (f32[4,2,16,256]{3,2,0,1:T(8,128)S(1)}, f32[4,2,16,256]{3,2,0,1:T(8,128)S(1)}, u32[]{:S(2)}, u32[]{:S(2)}) collective-permute-start(f32[4,2,16,256]{3,2,0,1:T(8,128)S(1)} %bitcast.30), channel_id=1, source_target_pairs={{0,12},{1,13},{2,14},{3,15}} | collective-permute-start | bytes 393224 | tf_op jit(solution)/shard_map/ppermute | solution.py:297
  2.6 0.7 %collective-permute-start.1 = (f32[4,2,16,256]{3,2,0,1:T(8,128)S(1)}, f32[4,2,16,256]{3,2,0,1:T(8,128)S(1)}, u32[]{:S(2)}, u32[]{:S(2)}) collective-permute-start(f32[4,2,16,256]{3,2,0,1:T(8,128)S(1)} %bitcast.31), channel_id=1, source_target_pairs={{0,8},{1,9},{2,10},{3,11}} | collective-permute-start | bytes 393224 | tf_op jit(solution)/shard_map/ppermute | solution.py:297
  3.3 0.0 copy-start.4
  3.3 0.7 %collective-permute-start = (f32[4,2,16,256]{3,2,0,1:T(8,128)S(1)}, f32[4,2,16,256]{3,2,0,1:T(8,128)S(1)}, u32[]{:S(2)}, u32[]{:S(2)}) collective-permute-start(f32[4,2,16,256]{3,2,0,1:T(8,128)S(1)} %bitcast.32), channel_id=1, source_target_pairs={{0,4},{1,5},{2,6},{3,7}} | collective-permute-start | bytes 393224 | tf_op jit(solution)/shard_map/ppermute | solution.py:297
  3.9 0.0 copy-done.1
  4.0 0.0 copy-done.4
  4.0 1.7 %split.1 = (f32[8,16,256]{2,1,0:T(8,128)}, f32[8,128,256]{2,1,0:T(8,128)}) custom-call(s32[2,16]{1,0:T(2,128)S(1)} %copy-done.4, f32[128,2048]{1,0:T(8,128)S(1)} %bitcast.28), custom_call_target="tpu_custom_call" | custom-call | tf_op jit(solution)/shard_map/split/pallas_call | solution.py:300
  5.7 8.4 %all-to-all-start = ((f32[8,16,256]{2,1,0:T(8,128)}), f32[8,16,256]{2,1,0:T(8,128)S(1)}, u32[]{:S(2)}, u32[]{:S(2)}) async-start(f32[8,16,256]{2,1,0:T(8,128)} %get-tuple-element.19), calls=%async_computation | async-start | bytes 262144 | tf_op jit(solution)/shard_map/all_to_all | solution.py:309
  14.1 0.0 collective-permute-done.2
  14.1 0.0 collective-permute-done.1
  14.1 0.0 collective-permute-done
  14.2 3.1 %collective-permute-start.3 = (f32[4,16,256]{2,1,0:T(8,128)S(1)}, f32[4,16,256]{2,1,0:T(8,128)S(1)}, u32[]{:S(2)}, u32[]{:S(2)}) collective-permute-start(f32[4,16,256]{2,1,0:T(8,128)S(1)} %get-tuple-element.38), channel_id=1, source_target_pairs={{0,16},{4,20},{8,24},{12,28},{1,17},{5,21},{9,25},{13,29},{2,18},{... | collective-permute-start | bytes 196616 | tf_op jit(solution)/shard_map/ppermute | solution.py:299
  17.3 1.3 %collective-permute-done.3.high_ref = f32[4,16,256]{2,1,0:T(8,128)S(1)} collective-permute-done((f32[4,16,256]{2,1,0:T(8,128)S(1)}, f32[4,16,256]{2,1,0:T(8,128)S(1)}, u32[]{:S(2)}, u32[]{:S(2)}) %collective-permute-start.3) | collective-permute-done | bytes 65568 | tf_op jit(solution)/shard_map/ppermute | solution.py:299
  18.6 0.0 all-to-all-done.pieces_ref
  18.7 0.6 sum_panel.1
  19.3 2.0 %collective-permute-start.6 = (f32[4,16,256]{2,1,0:T(8,128)S(1)}, f32[4,16,256]{2,1,0:T(8,128)S(1)}, u32[]{:S(2)}, u32[]{:S(2)}) collective-permute-start(f32[4,16,256]{2,1,0:T(8,128)S(1)} %sum_panel.1), channel_id=1, source_target_pairs={{0,12},{4,8},{8,4},{12,0},{1,13},{5,9},{9,5},{13,1},{2,14},{6,10},... | collective-permute-start | bytes 196616 | tf_op jit(solution)/shard_map/ppermute | solution.py:319
  21.2 0.0 collective-permute-start.5
  21.3 1.6 %collective-permute-start.4 = (f32[4,16,256]{2,1,0:T(8,128)S(1)}, f32[4,16,256]{2,1,0:T(8,128)S(1)}, u32[]{:S(2)}, u32[]{:S(2)}) collective-permute-start(f32[4,16,256]{2,1,0:T(8,128)S(1)} %sum_panel.1), channel_id=1, source_target_pairs={{0,4},{4,0},{8,12},{12,8},{1,5},{5,1},{9,13},{13,9},{2,6},{6,2},{1... | collective-permute-start | bytes 196616 | tf_op jit(solution)/shard_map/ppermute | solution.py:319
  22.9 1.4 %collective-permute-done.6 = f32[4,16,256]{2,1,0:T(8,128)S(1)} collective-permute-done((f32[4,16,256]{2,1,0:T(8,128)S(1)}, f32[4,16,256]{2,1,0:T(8,128)S(1)}, u32[]{:S(2)}, u32[]{:S(2)}) %collective-permute-start.6) | collective-permute-done | bytes 65568 | tf_op jit(solution)/shard_map/ppermute | solution.py:319
  24.3 2.6 %collective-permute-done.5 = f32[4,16,256]{2,1,0:T(8,128)S(1)} collective-permute-done((f32[4,16,256]{2,1,0:T(8,128)S(1)}, f32[4,16,256]{2,1,0:T(8,128)S(1)}, u32[]{:S(2)}, u32[]{:S(2)}) %collective-permute-start.5) | collective-permute-done | bytes 65568 | tf_op jit(solution)/shard_map/ppermute | solution.py:319
  26.9 0.0 collective-permute-done.4
  27.0 0.0 copy-start.7
  27.0 0.5 collective-permute-start.7
  27.5 6.0 %all-to-all-start.1 = ((f32[8,128,256]{2,1,0:T(8,128)}), f32[8,128,256]{2,1,0:T(8,128)S(1)}, u32[]{:S(2)}, u32[]{:S(2)}) async-start(f32[8,128,256]{2,1,0:T(8,128)} %get-tuple-element.20), calls=%async_computation.1 | async-start | bytes 2097152 | tf_op jit(solution)/shard_map/all_to_all | solution.py:321
  33.4 0.0 collective-permute-done.7.refs_1_
  33.4 1.2 %collective-permute-start.9 = (f32[4,2,16,256]{3,2,1,0:T(8,128)S(1)}, f32[4,2,16,256]{3,2,1,0:T(8,128)S(1)}, u32[]{:S(2)}, u32[]{:S(2)}) collective-permute-start(f32[4,2,16,256]{3,2,1,0:T(8,128)S(1)} %get-tuple-element.28), channel_id=1, source_target_pairs={{0,16},{16,0},{1,17},{17,1},{2,18},{18,2},{3,19},{19,3},{4,20},{20... | collective-permute-start | bytes 393224 | tf_op jit(solution)/shard_map/ppermute | solution.py:351
  34.7 0.0 copy-start.2
  34.7 0.7 %collective-permute-start.8 = (f32[256,256]{1,0:T(8,128)S(1)}, f32[256,256]{1,0:T(8,128)S(1)}, u32[]{:S(2)}, u32[]{:S(2)}) collective-permute-start(f32[256,256]{1,0:T(8,128)S(1)} %get-tuple-element.26.refs_6_), channel_id=1, source_target_pairs={{0,2},{4,6},{8,10},{12,14},{16,18},{20,22},{24,26},{28,30}} | collective-permute-start | bytes 786440 | tf_op jit(solution)/shard_map/ppermute | solution.py:282
  35.3 11.9 %collective-permute-done.9.refs_2_ = f32[4,2,16,256]{3,2,1,0:T(8,128)S(1)} collective-permute-done((f32[4,2,16,256]{3,2,1,0:T(8,128)S(1)}, f32[4,2,16,256]{3,2,1,0:T(8,128)S(1)}, u32[]{:S(2)}, u32[]{:S(2)}) %collective-permute-start.9) | collective-permute-done | bytes 131104 | tf_op jit(solution)/shard_map/ppermute | solution.py:351
  47.3 0.0 copy-done.2
  47.3 0.0 copy-start.5
  47.3 0.0 copy-done.7
  47.3 0.6 copy-done.5
  47.9 1.3 %collective-permute-start.11 = (f32[8,2,16,256]{3,2,1,0:T(8,128)S(1)}, f32[8,2,16,256]{3,2,1,0:T(8,128)S(1)}, u32[]{:S(2)}, u32[]{:S(2)}) collective-permute-start(f32[8,2,16,256]{3,2,1,0:T(8,128)S(1)} %pad_maximum_fusion.1.refs_9_), channel_id=1, source_target_pairs={{0,2},{4,6},{9,11},{13,15},{18,16},{22,20},{27,25},{31,29}} | collective-permute-start | bytes 786440 | tf_op jit(solution)/shard_map/ppermute | solution.py:282
  49.3 0.0 copy-start.6
  49.3 0.0 copy-start.8
  49.3 0.0 collective-permute-done.8.refs_7_
  49.3 0.7 %broadcast_select_fusion.1 = f32[256,256]{1,0:T(8,128)} fusion(f32[256,256]{1,0:T(8,128)S(1)} %get-tuple-element.26.refs_6_, f32[256,256]{1,0:T(8,128)S(1)} %collective-permute-done.8.refs_7_, pred[]{:T(512)S(6)} %eq.15), kind=kLoop, calls=%fused_computation.11 | loop fusion | flops 65536 | bytes 786433 | tf_op jit(solution)/shard_map/jit(_where)/select_n | solution.py:283
  50.0 0.0 copy-start
  50.0 1.4 %collective-permute-start.10 = (f32[256,256]{1,0:T(8,128)}, f32[256,256]{1,0:T(8,128)S(1)}, u32[]{:S(2)}, u32[]{:S(2)}) collective-permute-start(f32[256,256]{1,0:T(8,128)} %broadcast_select_fusion.1), channel_id=1, source_target_pairs={{0,1},{2,3},{4,5},{6,7},{8,9},{10,11},{12,13},{14,15},{16,17},{18,... | collective-permute-start | bytes 786440 | tf_op jit(solution)/shard_map/ppermute | solution.py:285
  51.4 5.3 %collective-permute-done.11.refs_10_ = f32[8,2,16,256]{3,2,1,0:T(8,128)S(1)} collective-permute-done((f32[8,2,16,256]{3,2,1,0:T(8,128)S(1)}, f32[8,2,16,256]{3,2,1,0:T(8,128)S(1)}, u32[]{:S(2)}, u32[]{:S(2)}) %collective-permute-start.11) | collective-permute-done | bytes 262176 | tf_op jit(solution)/shard_map/ppermute | solution.py:282
  56.7 0.0 copy-done.6
  56.7 0.0 copy-done.8
  56.7 0.8 %broadcast_select_fusion = f32[8,2,16,256]{3,2,1,0:T(8,128)} fusion(f32[8,2,16,256]{3,2,1,0:T(8,128)S(1)} %collective-permute-done.11.refs_10_, pred[]{:T(512)S(6)} %eq.17, f32[4,2,16,256]{3,2,1,0:T(8,128)S(1)} %copy-done.6, f32[4,2,16,256]{3,2,1,0:T(8,128)S(1)} %copy-done.8), kind=kLoop, calls=%fused_computation.10 | loop fusion | flops 131072 | bytes 786433 | tf_op jit(solution)/shard_map/jit(_where)/select_n | solution.py:283
  57.5 4.3 %collective-permute-start.12 = (f32[8,2,16,256]{3,2,1,0:T(8,128)}, f32[8,2,16,256]{3,2,1,0:T(8,128)}, u32[]{:S(2)}, u32[]{:S(2)}) collective-permute-start(f32[8,2,16,256]{3,2,1,0:T(8,128)} %broadcast_select_fusion), channel_id=1, source_target_pairs={{0,1},{2,3},{4,5},{6,7},{9,8},{11,10},{13,12},{15,14},{18,19},{16,... | collective-permute-start | bytes 786440 | tf_op jit(solution)/shard_map/ppermute | solution.py:285
  61.8 0.0 all-to-all-done.1.strips_ref
  61.8 0.0 copy-done
  61.8 0.0 copy-start.3
  61.8 0.7 %assemble.1.base_ref = f32[512,256]{1,0:T(8,128)S(1)} custom-call(s32[2,16]{1,0:T(2,128)S(1)} %copy-done.4, f32[512,256]{1,0:T(8,128)S(1)} %copy-done, f32[8,128,256]{2,1,0:T(8,128)S(1)} %all-to-all-done.1.strips_ref), custom_call_target="tpu_custom_call" | custom-call | tf_op jit(solution)/shard_map/assemble/pallas_call | solution.py:372
  62.5 0.0 collective-permute-done.10.refs_8_
  62.5 0.1 collective-permute-done.12.refs_11_
  62.6 0.1 copy-done.3
  62.6 3.7 %finish.1 = f32[512,256]{1,0:T(8,128)} custom-call(f32[512,256]{1,0:T(8,128)S(1)} %assemble.1.base_ref, f32[4,4,16,256]{3,2,1,0:T(8,128)S(1)} %pad_maximum_fusion.refs_0_, f32[4,2,16,256]{3,2,1,0:T(8,128)S(1)} %collective-permute-done.7.refs_1_, f32[4,2,16,256]{3,2,1,0:T(8,128)S(1)} %collective-permute-done.9.refs_2_, ...), custom_call_target="tpu_custom_call" | custom-call | tf_op jit(solution)/shard_map/finish/pallas_call | solution.py:382
  (11 shorter events, 0.2 us)
Async XLA Ops:
  0.0 3.9 %copy-start.1 = (f32[1,128,2048]{2,1,0:T(8,128)S(1)}, f32[1,128,2048]{2,1,0:T(8,128)}, u32[]{:S(2)}) copy-start(f32[1,128,2048]{2,1,0:T(8,128)} %param.4) | copy-start | bytes 3145732
  1.2 12.9 %collective-permute-start.2 = (f32[4,2,16,256]{3,2,0,1:T(8,128)S(1)}, f32[4,2,16,256]{3,2,0,1:T(8,128)S(1)}, u32[]{:S(2)}, u32[]{:S(2)}) collective-permute-start(f32[4,2,16,256]{3,2,0,1:T(8,128)S(1)} %bitcast.30), channel_id=1, source_target_pairs={{0,12},{1,13},{2,14},{3,15}} | collective-permute-start | bytes 393224 | tf_op jit(solution)/shard_map/ppermute | solution.py:297
  2.6 11.6 %collective-permute-start.1 = (f32[4,2,16,256]{3,2,0,1:T(8,128)S(1)}, f32[4,2,16,256]{3,2,0,1:T(8,128)S(1)}, u32[]{:S(2)}, u32[]{:S(2)}) collective-permute-start(f32[4,2,16,256]{3,2,0,1:T(8,128)S(1)} %bitcast.31), channel_id=1, source_target_pairs={{0,8},{1,9},{2,10},{3,11}} | collective-permute-start | bytes 393224 | tf_op jit(solution)/shard_map/ppermute | solution.py:297
  3.3 0.7 %copy-start.4 = (s32[2,16]{1,0:T(2,128)S(1)}, s32[2,16]{1,0:T(2,128)}, u32[]{:S(2)}) copy-start(s32[2,16]{1,0:T(2,128)} %map_ref.5) | copy-start | bytes 388
  3.3 10.9 %collective-permute-start = (f32[4,2,16,256]{3,2,0,1:T(8,128)S(1)}, f32[4,2,16,256]{3,2,0,1:T(8,128)S(1)}, u32[]{:S(2)}, u32[]{:S(2)}) collective-permute-start(f32[4,2,16,256]{3,2,0,1:T(8,128)S(1)} %bitcast.32), channel_id=1, source_target_pairs={{0,4},{1,5},{2,6},{3,7}} | collective-permute-start | bytes 393224 | tf_op jit(solution)/shard_map/ppermute | solution.py:297
  5.7 13.0 %all-to-all-start = ((f32[8,16,256]{2,1,0:T(8,128)}), f32[8,16,256]{2,1,0:T(8,128)S(1)}, u32[]{:S(2)}, u32[]{:S(2)}) async-start(f32[8,16,256]{2,1,0:T(8,128)} %get-tuple-element.19), calls=%async_computation | async-start | bytes 262144 | tf_op jit(solution)/shard_map/all_to_all | solution.py:309
  14.2 4.4 %collective-permute-start.3 = (f32[4,16,256]{2,1,0:T(8,128)S(1)}, f32[4,16,256]{2,1,0:T(8,128)S(1)}, u32[]{:S(2)}, u32[]{:S(2)}) collective-permute-start(f32[4,16,256]{2,1,0:T(8,128)S(1)} %get-tuple-element.38), channel_id=1, source_target_pairs={{0,16},{4,20},{8,24},{12,28},{1,17},{5,21},{9,25},{13,29},{2,18},{... | collective-permute-start | bytes 196616 | tf_op jit(solution)/shard_map/ppermute | solution.py:299
  19.3 5.0 %collective-permute-start.6 = (f32[4,16,256]{2,1,0:T(8,128)S(1)}, f32[4,16,256]{2,1,0:T(8,128)S(1)}, u32[]{:S(2)}, u32[]{:S(2)}) collective-permute-start(f32[4,16,256]{2,1,0:T(8,128)S(1)} %sum_panel.1), channel_id=1, source_target_pairs={{0,12},{4,8},{8,4},{12,0},{1,13},{5,9},{9,5},{13,1},{2,14},{6,10},... | collective-permute-start | bytes 196616 | tf_op jit(solution)/shard_map/ppermute | solution.py:319
  21.2 5.6 %collective-permute-start.5 = (f32[4,16,256]{2,1,0:T(8,128)S(1)}, f32[4,16,256]{2,1,0:T(8,128)S(1)}, u32[]{:S(2)}, u32[]{:S(2)}) collective-permute-start(f32[4,16,256]{2,1,0:T(8,128)S(1)} %sum_panel.1), channel_id=1, source_target_pairs={{0,8},{4,12},{8,0},{12,4},{1,9},{5,13},{9,1},{13,5},{2,10},{6,14},... | collective-permute-start | bytes 196616 | tf_op jit(solution)/shard_map/ppermute | solution.py:319
  21.3 5.6 %collective-permute-start.4 = (f32[4,16,256]{2,1,0:T(8,128)S(1)}, f32[4,16,256]{2,1,0:T(8,128)S(1)}, u32[]{:S(2)}, u32[]{:S(2)}) collective-permute-start(f32[4,16,256]{2,1,0:T(8,128)S(1)} %sum_panel.1), channel_id=1, source_target_pairs={{0,4},{4,0},{8,12},{12,8},{1,5},{5,1},{9,13},{13,9},{2,6},{6,2},{1... | collective-permute-start | bytes 196616 | tf_op jit(solution)/shard_map/ppermute | solution.py:319
  27.0 20.3 %copy-start.7 = (f32[4,2,16,256]{3,2,1,0:T(8,128)}, f32[4,2,16,256]{3,2,1,0:T(8,128)S(1)}, u32[]{:S(2)}) copy-start(f32[4,2,16,256]{3,2,1,0:T(8,128)S(1)} %get-tuple-element.35) | copy-start | bytes 393220
  27.0 6.5 %collective-permute-start.7 = (f32[4,2,16,256]{3,2,1,0:T(8,128)S(1)}, f32[4,2,16,256]{3,2,1,0:T(8,128)S(1)}, u32[]{:S(2)}, u32[]{:S(2)}) collective-permute-start(f32[4,2,16,256]{3,2,1,0:T(8,128)S(1)} %get-tuple-element.37), channel_id=1, source_target_pairs={{0,16},{16,0},{1,17},{17,1},{2,18},{18,2},{3,19},{19,3},{4,20},{20... | collective-permute-start | bytes 393224 | tf_op jit(solution)/shard_map/ppermute | solution.py:322
  27.5 34.3 %all-to-all-start.1 = ((f32[8,128,256]{2,1,0:T(8,128)}), f32[8,128,256]{2,1,0:T(8,128)S(1)}, u32[]{:S(2)}, u32[]{:S(2)}) async-start(f32[8,128,256]{2,1,0:T(8,128)} %get-tuple-element.20), calls=%async_computation.1 | async-start | bytes 2097152 | tf_op jit(solution)/shard_map/all_to_all | solution.py:321
  33.4 13.8 %collective-permute-start.9 = (f32[4,2,16,256]{3,2,1,0:T(8,128)S(1)}, f32[4,2,16,256]{3,2,1,0:T(8,128)S(1)}, u32[]{:S(2)}, u32[]{:S(2)}) collective-permute-start(f32[4,2,16,256]{3,2,1,0:T(8,128)S(1)} %get-tuple-element.28), channel_id=1, source_target_pairs={{0,16},{16,0},{1,17},{17,1},{2,18},{18,2},{3,19},{19,3},{4,20},{20... | collective-permute-start | bytes 393224 | tf_op jit(solution)/shard_map/ppermute | solution.py:351
  34.7 12.6 %copy-start.2 = (f32[128,128]{1,0:T(8,128)}, f32[128,128]{1,0:T(8,128)S(1)}, u32[]{:S(2)}) copy-start(f32[128,128]{1,0:T(8,128)S(1)} %get-tuple-element.30.refs_5_) | copy-start | bytes 196612
  34.7 14.6 %collective-permute-start.8 = (f32[256,256]{1,0:T(8,128)S(1)}, f32[256,256]{1,0:T(8,128)S(1)}, u32[]{:S(2)}, u32[]{:S(2)}) collective-permute-start(f32[256,256]{1,0:T(8,128)S(1)} %get-tuple-element.26.refs_6_), channel_id=1, source_target_pairs={{0,2},{4,6},{8,10},{12,14},{16,18},{20,22},{24,26},{28,30}} | collective-permute-start | bytes 786440 | tf_op jit(solution)/shard_map/ppermute | solution.py:282
  47.3 0.7 copy-start.5
  47.9 8.8 %collective-permute-start.11 = (f32[8,2,16,256]{3,2,1,0:T(8,128)S(1)}, f32[8,2,16,256]{3,2,1,0:T(8,128)S(1)}, u32[]{:S(2)}, u32[]{:S(2)}) collective-permute-start(f32[8,2,16,256]{3,2,1,0:T(8,128)S(1)} %pad_maximum_fusion.1.refs_9_), channel_id=1, source_target_pairs={{0,2},{4,6},{9,11},{13,15},{18,16},{22,20},{27,25},{31,29}} | collective-permute-start | bytes 786440 | tf_op jit(solution)/shard_map/ppermute | solution.py:282
  49.3 7.5 %copy-start.6 = (f32[4,2,16,256]{3,2,1,0:T(8,128)S(1)}, f32[4,2,16,256]{3,2,1,0:T(8,128)}, u32[]{:S(2)}) copy-start(f32[4,2,16,256]{3,2,1,0:T(8,128)} %copy-done.5) | copy-start | bytes 393220
  49.3 7.4 %copy-start.8 = (f32[4,2,16,256]{3,2,1,0:T(8,128)S(1)}, f32[4,2,16,256]{3,2,1,0:T(8,128)}, u32[]{:S(2)}) copy-start(f32[4,2,16,256]{3,2,1,0:T(8,128)} %copy-done.7) | copy-start | bytes 393220
  50.0 11.8 %copy-start = (f32[512,256]{1,0:T(8,128)S(1)}, f32[512,256]{1,0:T(8,128)}, u32[]{:S(2)}) copy-start(f32[512,256]{1,0:T(8,128)} %front_ref.1) | copy-start | bytes 1572868
  50.0 12.5 %collective-permute-start.10 = (f32[256,256]{1,0:T(8,128)}, f32[256,256]{1,0:T(8,128)S(1)}, u32[]{:S(2)}, u32[]{:S(2)}) collective-permute-start(f32[256,256]{1,0:T(8,128)} %broadcast_select_fusion.1), channel_id=1, source_target_pairs={{0,1},{2,3},{4,5},{6,7},{8,9},{10,11},{12,13},{14,15},{16,17},{18,... | collective-permute-start | bytes 786440 | tf_op jit(solution)/shard_map/ppermute | solution.py:285
  57.5 5.1 %collective-permute-start.12 = (f32[8,2,16,256]{3,2,1,0:T(8,128)}, f32[8,2,16,256]{3,2,1,0:T(8,128)}, u32[]{:S(2)}, u32[]{:S(2)}) collective-permute-start(f32[8,2,16,256]{3,2,1,0:T(8,128)} %broadcast_select_fusion), channel_id=1, source_target_pairs={{0,1},{2,3},{4,5},{6,7},{9,8},{11,10},{13,12},{15,14},{18,19},{16,... | collective-permute-start | bytes 786440 | tf_op jit(solution)/shard_map/ppermute | solution.py:285
  61.8 0.8 %copy-start.3 = (f32[128,128]{1,0:T(8,128)S(1)}, f32[128,128]{1,0:T(8,128)}, u32[]{:S(2)}) copy-start(f32[128,128]{1,0:T(8,128)} %copy-done.2) | copy-start | bytes 196612

commit v9 on v8

--- a/solution.py
+++ b/solution.py
@@ -83,20 +83,20 @@
         if b + 1 == count:
             break
         inside = (lane >= base) & (lane < base + SUB)
-        nxt = groups[b + 1]
-        after = [spread_col(nxt, base + k) for k in range(SUB)]
-        nxt = jnp.where(inside, 0.0, nxt)
-        for i in range(SUB):
-            low = after[0] * inv[i][0]
-            for k in range(1, i + 1):
-                low = low + after[k] * inv[i][k]
-            nxt = nxt - low * spread_row(kept, i)
-        groups[b + 1] = nxt
-        if b + 2 < count:
-            change = dot(done[:, base + 2 * SUB :], kept, 0, 0)
-            for j in range(b + 2, count):
-                at = SUB * (j - b - 2)
-                groups[j] = jnp.where(inside, 0.0, groups[j]) - change[at : at + SUB]
+        for j in range(b + 1, min(b + 3, count)):
+            nxt = groups[j]
+            after = [spread_col(nxt, base + k) for k in range(SUB)]
+            nxt = jnp.where(inside, 0.0, nxt)
+            for i in range(SUB):
+                low = after[0] * inv[i][0]
+                for k in range(1, i + 1):
+                    low = low + after[k] * inv[i][k]
+                nxt = nxt - low * spread_row(kept, i)
+            groups[j] = nxt
+        if b + 3 < count:
+            change = dot(done, kept, 0, 0)
+            for j in range(b + 3, count):
+                groups[j] = jnp.where(inside, 0.0, groups[j]) - change[SUB * j : SUB * (j + 1)]
     return upper, inverse
 
 
@@ -175,8 +175,8 @@
 
 
 def choose(refs, distance, take):
-    for ref, here in zip(refs, (distance == 0, distance == 2, distance % 2 == 1)):
-        pl.when(here)(functools.partial(take, ref))
+    for e, ref in enumerate(refs):
+        pl.when(distance == e)(functools.partial(take, ref))
 
 
 def assemble_kernel(map_ref, front_ref, strips_ref, out_ref):
@@ -193,6 +193,7 @@
 def finish_kernel(few, base_ref, *refs):
     count = 3 if few else 1
     panel, (upper_ref, side_ref, upper2_ref), refs = refs[:count], refs[count : count + 3], refs[count + 3 :]
+    count = lax.axis_size("col") if few else 1
     inverses, parts = refs[:count], refs[count : 2 * count]
     out_ref, rows_c_ref, rows_o_ref, inv_ref = refs[-4:]
     rows, width = out_ref.shape
@@ -275,14 +276,13 @@
     return assembled, [rows_c], [pivot], rows_o
 
 
-def over_col(value, roots, root):
+def over_col(value, roots):
     n_col = lax.axis_size("col")
     axes = OWNER + ("col",)
-    cross = [(o * n_col + c, o * n_col + (c ^ 2)) for o, c in enumerate(roots)]
-    over_x = lax.ppermute(value, axes, cross)
-    held = jnp.where(lax.axis_index("col") == root, value, over_x)
-    other = [(o * n_col + (c ^ e), o * n_col + (c ^ e ^ 1)) for o, c in enumerate(roots) for e in (0, 2)]
-    return [value, over_x, lax.ppermute(held, axes, other)], held
+    pairs = lambda e, f: [(o * n_col + (c ^ e), o * n_col + (c ^ f)) for o, c in enumerate(roots)]
+    over_x = lax.ppermute(value, axes, pairs(0, 2))
+    beside = lax.ppermute(value, axes, pairs(0, 1))
+    return [value, beside, over_x, lax.ppermute(over_x, axes, pairs(2, 3))], over_x
 
 
 def gather_pieces(front, strip, child_map):
@@ -350,12 +350,11 @@
         first, later = lax.optimization_barrier((first, near[:, tops:]))
         far_rest = lax.ppermute(later, "grp", [(0, 1), (1, 0)])
         panel = [near, far_top, far_rest]
-        root = owner_of() * width // rows
         at = owner_of() * width % rows // BLK
         cut_near = lax.dynamic_slice_in_dim(near, at, width // BLK, 1)
         cut_far = jnp.where(at == 0, far_top, far_rest)
         own_part = jnp.concatenate([cut_near, cut_far], axis=0)
-        parts, _ = over_col(own_part, [o * width // rows for o in range(owners)], root)
+        parts, _ = over_col(own_part, [o * width // rows for o in range(owners)])
     upper2, inverse = pl.pallas_call(
         functools.partial(second_half_kernel, few),
         out_shape=[half, f32(PIVOTS, PIVOTS)],
@@ -367,7 +366,7 @@
         name="pivot_second",
     )(first, side, rest)
     if few:
-        inverses, held = over_col(inverse, [0] * owners, 0)
+        inverses, held = over_col(inverse, [0] * owners)
         strips, _ = lax.optimization_barrier((last, held))
         base = pl.pallas_call(
             assemble_kernel,

time: 66.9 us -> 66 us (0.987)
  the two profiles are of different devices: /device:TPU:27 before, /device:TPU:0 now
where the time goes in v9:
time: 66 us; the launch traced here: 65.5 us
  starting transfers between devices  36.1 us (55%)
  Pallas kernels  15.4 us (23%)
  waiting for transfers between devices  12.2 us (18%)
  local copies, waits for them, and re-layouts  1.41 us (2%)
    ppermute x3, starting transfers between devices, gather_pieces(): got = got + lax.ppermute(cut[:, :, r], OWNER, [(0, r)])  9.56 us
    pallas_call x1, Pallas kernels, body(): pl.pallas_call(functools.partial(first_half_kernel, few), out_shape=[half...  4.96 us
    pallas_call x1, Pallas kernels, body(): pl.pallas_call(functools.partial(second_half_kernel, few), out_shape=[hal...  4.66 us
    ppermute x3, starting transfers between devices, gather_pieces(): lax.ppermute(mine, 'row', [(i, i ^ d) for i in range(n_row)])  4.45 us
    all_to_all x1, waiting for transfers between devices, gather_pieces(): lax.all_to_all(strips, OWNER, split_axis=0, concat_axis=0, tiled=True)  3.75 us
    all_to_all x1, starting transfers between devices, gather_pieces(): lax.all_to_all(strips, OWNER, split_axis=0, concat_axis=0, tiled=True)  3.56 us
    ppermute x3, waiting for transfers between devices, gather_pieces(): lax.ppermute(mine, 'row', [(i, i ^ d) for i in range(n_row)])  3.38 us
    all_to_all x1, starting transfers between devices, gather_pieces(): lax.all_to_all(panel, OWNER, split_axis=0, concat_axis=0, tiled=True)  3.37 us
  transfers between devices with their start and end apart: 17, of which 7 were waited for; matrix products, arithmetic and copies ran while one was open for 0% of the time, Pallas kernels for 18%

profile of v9, /device:TPU:0, one launch (start us, length us, event | category | flops | bytes accessed | tf_op | source)
XLA Modules:
  0.0 65.5 jit_solution(6522448309140129312)
XLA Ops:
  0.0 0.0 copy-start.1
  0.0 1.2 %fusion.4 = (f32[4,2,1,16,256]{4,3,2,1,0:T(8,128)S(1)}, f32[4,2,1,16,256]{4,3,2,1,0:T(8,128)S(1)}, f32[4,2,1,16,256]{4,3,2,1,0:T(8,128)S(1)}, f32[4,2,1,16,256]{4,3,2,1,0:T(8,128)S(1)}) fusion(f32[4,2,4,16,256]{4,3,2,1,0:T(8,128)} %bitcast.27), kind=kLoop, calls=%fused_computation.14 | loop fusion | bytes 1048576 | tf_op jit(solution)/shard_map/slice | solution.py:295
  1.2 7.0 %collective-permute-start.2 = (f32[4,2,16,256]{3,2,0,1:T(8,128)S(1)}, f32[4,2,16,256]{3,2,0,1:T(8,128)S(1)}, u32[]{:S(2)}, u32[]{:S(2)}) collective-permute-start(f32[4,2,16,256]{3,2,0,1:T(8,128)S(1)} %bitcast.30), channel_id=1, source_target_pairs={{0,12},{1,13},{2,14},{3,15}} | collective-permute-start | bytes 393224 | tf_op jit(solution)/shard_map/ppermute | solution.py:297
  8.2 1.3 %collective-permute-start = (f32[4,2,16,256]{3,2,0,1:T(8,128)S(1)}, f32[4,2,16,256]{3,2,0,1:T(8,128)S(1)}, u32[]{:S(2)}, u32[]{:S(2)}) collective-permute-start(f32[4,2,16,256]{3,2,0,1:T(8,128)S(1)} %bitcast.31), channel_id=1, source_target_pairs={{0,4},{1,5},{2,6},{3,7}} | collective-permute-start | bytes 393224 | tf_op jit(solution)/shard_map/ppermute | solution.py:297
  9.6 0.0 copy-start.4
  9.6 1.3 %collective-permute-start.1 = (f32[4,2,16,256]{3,2,0,1:T(8,128)S(1)}, f32[4,2,16,256]{3,2,0,1:T(8,128)S(1)}, u32[]{:S(2)}, u32[]{:S(2)}) collective-permute-start(f32[4,2,16,256]{3,2,0,1:T(8,128)S(1)} %bitcast.32), channel_id=1, source_target_pairs={{0,8},{1,9},{2,10},{3,11}} | collective-permute-start | bytes 393224 | tf_op jit(solution)/shard_map/ppermute | solution.py:297
  10.9 0.0 copy-done.1
  10.9 0.0 copy-done.4
  10.9 1.7 %split.1 = (f32[8,16,256]{2,1,0:T(8,128)}, f32[8,128,256]{2,1,0:T(8,128)}) custom-call(s32[2,16]{1,0:T(2,128)S(1)} %copy-done.4, f32[128,2048]{1,0:T(8,128)S(1)} %bitcast.28), custom_call_target="tpu_custom_call" | custom-call | tf_op jit(solution)/shard_map/split/pallas_call | solution.py:300
  12.6 3.4 %all-to-all-start = ((f32[8,16,256]{2,1,0:T(8,128)}), f32[8,16,256]{2,1,0:T(8,128)S(1)}, u32[]{:S(2)}, u32[]{:S(2)}) async-start(f32[8,16,256]{2,1,0:T(8,128)} %get-tuple-element.19), calls=%async_computation | async-start | bytes 262144 | tf_op jit(solution)/shard_map/all_to_all | solution.py:309
  16.0 0.0 collective-permute-done.2
  16.0 0.0 collective-permute-done
  16.0 0.9 %collective-permute-done.1 = f32[4,2,16,256]{3,2,0,1:T(8,128)S(1)} collective-permute-done((f32[4,2,16,256]{3,2,0,1:T(8,128)S(1)}, f32[4,2,16,256]{3,2,0,1:T(8,128)S(1)}, u32[]{:S(2)}, u32[]{:S(2)}) %collective-permute-start.1) | collective-permute-done | bytes 131104 | tf_op jit(solution)/shard_map/ppermute | solution.py:297
  17.0 2.9 %collective-permute-start.3 = (f32[4,16,256]{2,1,0:T(8,128)S(1)}, f32[4,16,256]{2,1,0:T(8,128)S(1)}, u32[]{:S(2)}, u32[]{:S(2)}) collective-permute-start(f32[4,16,256]{2,1,0:T(8,128)S(1)} %get-tuple-element.38), channel_id=1, source_target_pairs={{0,16},{4,20},{8,24},{12,28},{1,17},{5,21},{9,25},{13,29},{2,18},{... | collective-permute-start | bytes 196616 | tf_op jit(solution)/shard_map/ppermute | solution.py:299
  19.9 2.0 %collective-permute-done.3.high_ref = f32[4,16,256]{2,1,0:T(8,128)S(1)} collective-permute-done((f32[4,16,256]{2,1,0:T(8,128)S(1)}, f32[4,16,256]{2,1,0:T(8,128)S(1)}, u32[]{:S(2)}, u32[]{:S(2)}) %collective-permute-start.3) | collective-permute-done | bytes 65568 | tf_op jit(solution)/shard_map/ppermute | solution.py:299
  21.9 1.5 %all-to-all-done.pieces_ref = f32[8,16,256]{2,1,0:T(8,128)S(1)} async-done(((f32[8,16,256]{2,1,0:T(8,128)}), f32[8,16,256]{2,1,0:T(8,128)S(1)}, u32[]{:S(2)}, u32[]{:S(2)}) %all-to-all-start) | async-done | bytes 131104 | tf_op jit(solution)/shard_map/all_to_all | solution.py:309
  23.5 0.6 sum_panel.1
  24.1 1.7 %collective-permute-start.6 = (f32[4,16,256]{2,1,0:T(8,128)S(1)}, f32[4,16,256]{2,1,0:T(8,128)S(1)}, u32[]{:S(2)}, u32[]{:S(2)}) collective-permute-start(f32[4,16,256]{2,1,0:T(8,128)S(1)} %sum_panel.1), channel_id=1, source_target_pairs={{0,12},{4,8},{8,4},{12,0},{1,13},{5,9},{9,5},{13,1},{2,14},{6,10},... | collective-permute-start | bytes 196616 | tf_op jit(solution)/shard_map/ppermute | solution.py:319
  25.8 0.0 collective-permute-start.5
  25.8 2.7 %collective-permute-start.4 = (f32[4,16,256]{2,1,0:T(8,128)S(1)}, f32[4,16,256]{2,1,0:T(8,128)S(1)}, u32[]{:S(2)}, u32[]{:S(2)}) collective-permute-start(f32[4,16,256]{2,1,0:T(8,128)S(1)} %sum_panel.1), channel_id=1, source_target_pairs={{0,4},{4,0},{8,12},{12,8},{1,5},{5,1},{9,13},{13,9},{2,6},{6,2},{1... | collective-permute-start | bytes 196616 | tf_op jit(solution)/shard_map/ppermute | solution.py:319
  28.5 1.8 %collective-permute-done.6 = f32[4,16,256]{2,1,0:T(8,128)S(1)} collective-permute-done((f32[4,16,256]{2,1,0:T(8,128)S(1)}, f32[4,16,256]{2,1,0:T(8,128)S(1)}, u32[]{:S(2)}, u32[]{:S(2)}) %collective-permute-start.6) | collective-permute-done | bytes 65568 | tf_op jit(solution)/shard_map/ppermute | solution.py:319
  30.3 1.6 %collective-permute-done.5 = f32[4,16,256]{2,1,0:T(8,128)S(1)} collective-permute-done((f32[4,16,256]{2,1,0:T(8,128)S(1)}, f32[4,16,256]{2,1,0:T(8,128)S(1)}, u32[]{:S(2)}, u32[]{:S(2)}) %collective-permute-start.5) | collective-permute-done | bytes 65568 | tf_op jit(solution)/shard_map/ppermute | solution.py:319
  31.9 0.0 collective-permute-done.4
  32.0 1.5 %collective-permute-start.7 = (f32[4,2,16,256]{3,2,1,0:T(8,128)S(1)}, f32[4,2,16,256]{3,2,1,0:T(8,128)S(1)}, u32[]{:S(2)}, u32[]{:S(2)}) collective-permute-start(f32[4,2,16,256]{3,2,1,0:T(8,128)S(1)} %get-tuple-element.37), channel_id=1, source_target_pairs={{0,16},{16,0},{1,17},{17,1},{2,18},{18,2},{3,19},{19,3},{4,20},{20... | collective-permute-start | bytes 393224 | tf_op jit(solution)/shard_map/ppermute | solution.py:322
  33.4 3.6 %all-to-all-start.1 = ((f32[8,128,256]{2,1,0:T(8,128)}), f32[8,128,256]{2,1,0:T(8,128)S(1)}, u32[]{:S(2)}, u32[]{:S(2)}) async-start(f32[8,128,256]{2,1,0:T(8,128)} %get-tuple-element.20), calls=%async_computation.1 | async-start | bytes 2097152 | tf_op jit(solution)/shard_map/all_to_all | solution.py:321
  37.0 0.0 collective-permute-done.7.refs_1_
  37.0 5.0 %pivot_first.1 = (f32[128,128]{1,0:T(8,128)S(1)}, f32[128,128]{1,0:T(8,128)S(1)}, f32[128,128]{1,0:T(8,128)S(1)}, f32[128,128]{1,0:T(8,128)S(1)}) custom-call(f32[4,4,16,256]{3,2,1,0:T(8,128)S(1)} %pad_maximum_fusion.refs_0_, f32[4,2,16,256]{3,2,1,0:T(8,128)S(1)} %collective-permute-done.7.refs_1_), custom_call_target="tpu_custom_call" | custom-call | flops 8000000000 | bytes 262144 | tf_op jit(solution)/shard_map/pivot_first/pallas_call | solution.py:337
  42.0 2.0 %collective-permute-start.9 = (f32[4,2,16,256]{3,2,1,0:T(8,128)S(1)}, f32[4,2,16,256]{3,2,1,0:T(8,128)S(1)}, u32[]{:S(2)}, u32[]{:S(2)}) collective-permute-start(f32[4,2,16,256]{3,2,1,0:T(8,128)S(1)} %get-tuple-element.28), channel_id=1, source_target_pairs={{0,16},{16,0},{1,17},{17,1},{2,18},{18,2},{3,19},{19,3},{4,20},{20... | collective-permute-start | bytes 393224 | tf_op jit(solution)/shard_map/ppermute | solution.py:351
  44.0 4.7 %pivot_second.1 = (f32[128,128]{1,0:T(8,128)S(1)}, f32[256,256]{1,0:T(8,128)S(1)}) custom-call(f32[128,128]{1,0:T(8,128)S(1)} %get-tuple-element.23.first_ref, f32[128,128]{1,0:T(8,128)S(1)} %get-tuple-element.24.side_ref.refs_4_, f32[128,128]{1,0:T(8,128)S(1)} %get-tuple-element.25.next_ref), custom_call_target="tpu_custom_call" | custom-call | flops 8000000000 | bytes 262144 | tf_op jit(solution)/shard_map/pivot_second/pallas_call | solution.py:358
  48.6 0.0 copy-start.2
  48.6 0.0 copy-start
  48.7 1.4 %collective-permute-start.8 = (f32[256,256]{1,0:T(8,128)S(1)}, f32[256,256]{1,0:T(8,128)S(1)}, u32[]{:S(2)}, u32[]{:S(2)}) collective-permute-start(f32[256,256]{1,0:T(8,128)S(1)} %get-tuple-element.26.refs_6_), channel_id=1, source_target_pairs={{0,2},{4,6},{8,10},{12,14},{16,18},{20,22},{24,26},{28,30}} | collective-permute-start | bytes 786440 | tf_op jit(solution)/shard_map/ppermute | solution.py:283
  50.1 0.0 collective-permute-done.9.refs_2_
  50.1 0.0 copy-done.2
  50.2 1.3 %collective-permute-start.13 = (f32[8,2,16,256]{3,2,1,0:T(8,128)S(1)}, f32[8,2,16,256]{3,2,1,0:T(8,128)S(1)}, u32[]{:S(2)}, u32[]{:S(2)}) collective-permute-start(f32[8,2,16,256]{3,2,1,0:T(8,128)S(1)} %pad_maximum_fusion.1.refs_10_), channel_id=1, source_target_pairs={{0,2},{4,6},{9,11},{13,15},{18,16},{22,20},{27,25},{31,29}} | collective-permute-start | bytes 786440 | tf_op jit(solution)/shard_map/ppermute | solution.py:283
  51.5 1.3 %collective-permute-start.10 = (f32[256,256]{1,0:T(8,128)S(1)}, f32[256,256]{1,0:T(8,128)S(1)}, u32[]{:S(2)}, u32[]{:S(2)}) collective-permute-start(f32[256,256]{1,0:T(8,128)S(1)} %get-tuple-element.26.refs_6_), channel_id=1, source_target_pairs={{0,1},{4,5},{8,9},{12,13},{16,17},{20,21},{24,25},{28,29}} | collective-permute-start | bytes 786440 | tf_op jit(solution)/shard_map/ppermute | solution.py:284
  52.8 2.0 %collective-permute-start.12 = (f32[8,2,16,256]{3,2,1,0:T(8,128)S(1)}, f32[8,2,16,256]{3,2,1,0:T(8,128)}, u32[]{:S(2)}, u32[]{:S(2)}) collective-permute-start(f32[8,2,16,256]{3,2,1,0:T(8,128)S(1)} %pad_maximum_fusion.1.refs_10_), channel_id=1, source_target_pairs={{0,1},{4,5},{9,8},{13,12},{18,19},{22,23},{27,26},{31,30}} | collective-permute-start | bytes 786440 | tf_op jit(solution)/shard_map/ppermute | solution.py:284
  54.8 0.0 collective-permute-done.8.refs_8_
  54.8 1.4 %collective-permute-start.11 = (f32[256,256]{1,0:T(8,128)S(1)}, f32[256,256]{1,0:T(8,128)}, u32[]{:S(2)}, u32[]{:S(2)}) collective-permute-start(f32[256,256]{1,0:T(8,128)S(1)} %collective-permute-done.8.refs_8_), channel_id=1, source_target_pairs={{2,3},{6,7},{10,11},{14,15},{18,19},{22,23},{26,27},{30,31}} | collective-permute-start | bytes 786440 | tf_op jit(solution)/shard_map/ppermute | solution.py:285
  56.2 0.6 collective-permute-done.13.refs_12_
  56.8 1.4 %collective-permute-start.14 = (f32[8,2,16,256]{3,2,1,0:T(8,128)S(1)}, f32[8,2,16,256]{3,2,1,0:T(8,128)}, u32[]{:S(2)}, u32[]{:S(2)}) collective-permute-start(f32[8,2,16,256]{3,2,1,0:T(8,128)S(1)} %collective-permute-done.13.refs_12_), channel_id=1, source_target_pairs={{2,3},{6,7},{11,10},{15,14},{16,17},{20,21},{25,24},{29,28}} | collective-permute-start | bytes 786440 | tf_op jit(solution)/shard_map/ppermute | solution.py:285
  58.2 3.8 %all-to-all-done.1.strips_ref = f32[8,128,256]{2,1,0:T(8,128)S(1)} async-done(((f32[8,128,256]{2,1,0:T(8,128)}), f32[8,128,256]{2,1,0:T(8,128)S(1)}, u32[]{:S(2)}, u32[]{:S(2)}) %all-to-all-start.1) | async-done | bytes 1048608 | tf_op jit(solution)/shard_map/all_to_all | solution.py:321
  61.9 0.0 copy-done
  61.9 0.0 copy-start.3
  61.9 0.7 %assemble.1.base_ref = f32[512,256]{1,0:T(8,128)S(1)} custom-call(s32[2,16]{1,0:T(2,128)S(1)} %copy-done.4, f32[512,256]{1,0:T(8,128)S(1)} %copy-done, f32[8,128,256]{2,1,0:T(8,128)S(1)} %all-to-all-done.1.strips_ref), custom_call_target="tpu_custom_call" | custom-call | tf_op jit(solution)/shard_map/assemble/pallas_call | solution.py:371
  62.6 0.0 collective-permute-done.10.refs_7_
  62.6 0.0 collective-permute-done.12.refs_11_
  62.6 0.0 collective-permute-done.11.refs_9_
  62.6 0.0 collective-permute-done.14.refs_13_
  62.7 0.1 copy-done.3
  62.8 2.8 %finish.1 = f32[512,256]{1,0:T(8,128)} custom-call(f32[512,256]{1,0:T(8,128)S(1)} %assemble.1.base_ref, f32[4,4,16,256]{3,2,1,0:T(8,128)S(1)} %pad_maximum_fusion.refs_0_, f32[4,2,16,256]{3,2,1,0:T(8,128)S(1)} %collective-permute-done.7.refs_1_, f32[4,2,16,256]{3,2,1,0:T(8,128)S(1)} %collective-permute-done.9.refs_2_, ...), custom_call_target="tpu_custom_call" | custom-call | tf_op jit(solution)/shard_map/finish/pallas_call | solution.py:381
  (9 shorter events, 0.2 us)
Async XLA Ops:
  0.0 10.9 %copy-start.1 = (f32[1,128,2048]{2,1,0:T(8,128)S(1)}, f32[1,128,2048]{2,1,0:T(8,128)}, u32[]{:S(2)}) copy-start(f32[1,128,2048]{2,1,0:T(8,128)} %param.4) | copy-start | bytes 3145732
  1.2 14.8 %collective-permute-start.2 = (f32[4,2,16,256]{3,2,0,1:T(8,128)S(1)}, f32[4,2,16,256]{3,2,0,1:T(8,128)S(1)}, u32[]{:S(2)}, u32[]{:S(2)}) collective-permute-start(f32[4,2,16,256]{3,2,0,1:T(8,128)S(1)} %bitcast.30), channel_id=1, source_target_pairs={{0,12},{1,13},{2,14},{3,15}} | collective-permute-start | bytes 393224 | tf_op jit(solution)/shard_map/ppermute | solution.py:297
  8.2 7.8 %collective-permute-start = (f32[4,2,16,256]{3,2,0,1:T(8,128)S(1)}, f32[4,2,16,256]{3,2,0,1:T(8,128)S(1)}, u32[]{:S(2)}, u32[]{:S(2)}) collective-permute-start(f32[4,2,16,256]{3,2,0,1:T(8,128)S(1)} %bitcast.31), channel_id=1, source_target_pairs={{0,4},{1,5},{2,6},{3,7}} | collective-permute-start | bytes 393224 | tf_op jit(solution)/shard_map/ppermute | solution.py:297
  9.6 1.3 %copy-start.4 = (s32[2,16]{1,0:T(2,128)S(1)}, s32[2,16]{1,0:T(2,128)}, u32[]{:S(2)}) copy-start(s32[2,16]{1,0:T(2,128)} %map_ref.5) | copy-start | bytes 388
  9.6 7.4 %collective-permute-start.1 = (f32[4,2,16,256]{3,2,0,1:T(8,128)S(1)}, f32[4,2,16,256]{3,2,0,1:T(8,128)S(1)}, u32[]{:S(2)}, u32[]{:S(2)}) collective-permute-start(f32[4,2,16,256]{3,2,0,1:T(8,128)S(1)} %bitcast.32), channel_id=1, source_target_pairs={{0,8},{1,9},{2,10},{3,11}} | collective-permute-start | bytes 393224 | tf_op jit(solution)/shard_map/ppermute | solution.py:297
  12.6 10.8 %all-to-all-start = ((f32[8,16,256]{2,1,0:T(8,128)}), f32[8,16,256]{2,1,0:T(8,128)S(1)}, u32[]{:S(2)}, u32[]{:S(2)}) async-start(f32[8,16,256]{2,1,0:T(8,128)} %get-tuple-element.19), calls=%async_computation | async-start | bytes 262144 | tf_op jit(solution)/shard_map/all_to_all | solution.py:309
  17.0 4.9 %collective-permute-start.3 = (f32[4,16,256]{2,1,0:T(8,128)S(1)}, f32[4,16,256]{2,1,0:T(8,128)S(1)}, u32[]{:S(2)}, u32[]{:S(2)}) collective-permute-start(f32[4,16,256]{2,1,0:T(8,128)S(1)} %get-tuple-element.38), channel_id=1, source_target_pairs={{0,16},{4,20},{8,24},{12,28},{1,17},{5,21},{9,25},{13,29},{2,18},{... | collective-permute-start | bytes 196616 | tf_op jit(solution)/shard_map/ppermute | solution.py:299
  24.1 6.3 %collective-permute-start.6 = (f32[4,16,256]{2,1,0:T(8,128)S(1)}, f32[4,16,256]{2,1,0:T(8,128)S(1)}, u32[]{:S(2)}, u32[]{:S(2)}) collective-permute-start(f32[4,16,256]{2,1,0:T(8,128)S(1)} %sum_panel.1), channel_id=1, source_target_pairs={{0,12},{4,8},{8,4},{12,0},{1,13},{5,9},{9,5},{13,1},{2,14},{6,10},... | collective-permute-start | bytes 196616 | tf_op jit(solution)/shard_map/ppermute | solution.py:319
  25.8 6.1 %collective-permute-start.5 = (f32[4,16,256]{2,1,0:T(8,128)S(1)}, f32[4,16,256]{2,1,0:T(8,128)S(1)}, u32[]{:S(2)}, u32[]{:S(2)}) collective-permute-start(f32[4,16,256]{2,1,0:T(8,128)S(1)} %sum_panel.1), channel_id=1, source_target_pairs={{0,8},{4,12},{8,0},{12,4},{1,9},{5,13},{9,1},{13,5},{2,10},{6,14},... | collective-permute-start | bytes 196616 | tf_op jit(solution)/shard_map/ppermute | solution.py:319
  25.8 6.1 %collective-permute-start.4 = (f32[4,16,256]{2,1,0:T(8,128)S(1)}, f32[4,16,256]{2,1,0:T(8,128)S(1)}, u32[]{:S(2)}, u32[]{:S(2)}) collective-permute-start(f32[4,16,256]{2,1,0:T(8,128)S(1)} %sum_panel.1), channel_id=1, source_target_pairs={{0,4},{4,0},{8,12},{12,8},{1,5},{5,1},{9,13},{13,9},{2,6},{6,2},{1... | collective-permute-start | bytes 196616 | tf_op jit(solution)/shard_map/ppermute | solution.py:319
  32.0 5.0 %collective-permute-start.7 = (f32[4,2,16,256]{3,2,1,0:T(8,128)S(1)}, f32[4,2,16,256]{3,2,1,0:T(8,128)S(1)}, u32[]{:S(2)}, u32[]{:S(2)}) collective-permute-start(f32[4,2,16,256]{3,2,1,0:T(8,128)S(1)} %get-tuple-element.37), channel_id=1, source_target_pairs={{0,16},{16,0},{1,17},{17,1},{2,18},{18,2},{3,19},{19,3},{4,20},{20... | collective-permute-start | bytes 393224 | tf_op jit(solution)/shard_map/ppermute | solution.py:322
  33.4 28.5 %all-to-all-start.1 = ((f32[8,128,256]{2,1,0:T(8,128)}), f32[8,128,256]{2,1,0:T(8,128)S(1)}, u32[]{:S(2)}, u32[]{:S(2)}) async-start(f32[8,128,256]{2,1,0:T(8,128)} %get-tuple-element.20), calls=%async_computation.1 | async-start | bytes 2097152 | tf_op jit(solution)/shard_map/all_to_all | solution.py:321
  42.0 8.1 %collective-permute-start.9 = (f32[4,2,16,256]{3,2,1,0:T(8,128)S(1)}, f32[4,2,16,256]{3,2,1,0:T(8,128)S(1)}, u32[]{:S(2)}, u32[]{:S(2)}) collective-permute-start(f32[4,2,16,256]{3,2,1,0:T(8,128)S(1)} %get-tuple-element.28), channel_id=1, source_target_pairs={{0,16},{16,0},{1,17},{17,1},{2,18},{18,2},{3,19},{19,3},{4,20},{20... | collective-permute-start | bytes 393224 | tf_op jit(solution)/shard_map/ppermute | solution.py:351
  48.6 1.5 %copy-start.2 = (f32[128,128]{1,0:T(8,128)}, f32[128,128]{1,0:T(8,128)S(1)}, u32[]{:S(2)}) copy-start(f32[128,128]{1,0:T(8,128)S(1)} %get-tuple-element.30.refs_5_) | copy-start | bytes 196612
  48.6 13.3 %copy-start = (f32[512,256]{1,0:T(8,128)S(1)}, f32[512,256]{1,0:T(8,128)}, u32[]{:S(2)}) copy-start(f32[512,256]{1,0:T(8,128)} %front_ref.1) | copy-start | bytes 1572868
  48.7 6.2 %collective-permute-start.8 = (f32[256,256]{1,0:T(8,128)S(1)}, f32[256,256]{1,0:T(8,128)S(1)}, u32[]{:S(2)}, u32[]{:S(2)}) collective-permute-start(f32[256,256]{1,0:T(8,128)S(1)} %get-tuple-element.26.refs_6_), channel_id=1, source_target_pairs={{0,2},{4,6},{8,10},{12,14},{16,18},{20,22},{24,26},{28,30}} | collective-permute-start | bytes 786440 | tf_op jit(solution)/shard_map/ppermute | solution.py:283
  50.2 6.6 %collective-permute-start.13 = (f32[8,2,16,256]{3,2,1,0:T(8,128)S(1)}, f32[8,2,16,256]{3,2,1,0:T(8,128)S(1)}, u32[]{:S(2)}, u32[]{:S(2)}) collective-permute-start(f32[8,2,16,256]{3,2,1,0:T(8,128)S(1)} %pad_maximum_fusion.1.refs_10_), channel_id=1, source_target_pairs={{0,2},{4,6},{9,11},{13,15},{18,16},{22,20},{27,25},{31,29}} | collective-permute-start | bytes 786440 | tf_op jit(solution)/shard_map/ppermute | solution.py:283
  51.5 11.1 %collective-permute-start.10 = (f32[256,256]{1,0:T(8,128)S(1)}, f32[256,256]{1,0:T(8,128)S(1)}, u32[]{:S(2)}, u32[]{:S(2)}) collective-permute-start(f32[256,256]{1,0:T(8,128)S(1)} %get-tuple-element.26.refs_6_), channel_id=1, source_target_pairs={{0,1},{4,5},{8,9},{12,13},{16,17},{20,21},{24,25},{28,29}} | collective-permute-start | bytes 786440 | tf_op jit(solution)/shard_map/ppermute | solution.py:284
  52.8 9.8 %collective-permute-start.12 = (f32[8,2,16,256]{3,2,1,0:T(8,128)S(1)}, f32[8,2,16,256]{3,2,1,0:T(8,128)}, u32[]{:S(2)}, u32[]{:S(2)}) collective-permute-start(f32[8,2,16,256]{3,2,1,0:T(8,128)S(1)} %pad_maximum_fusion.1.refs_10_), channel_id=1, source_target_pairs={{0,1},{4,5},{9,8},{13,12},{18,19},{22,23},{27,26},{31,30}} | collective-permute-start | bytes 786440 | tf_op jit(solution)/shard_map/ppermute | solution.py:284
  54.8 7.8 %collective-permute-start.11 = (f32[256,256]{1,0:T(8,128)S(1)}, f32[256,256]{1,0:T(8,128)}, u32[]{:S(2)}, u32[]{:S(2)}) collective-permute-start(f32[256,256]{1,0:T(8,128)S(1)} %collective-permute-done.8.refs_8_), channel_id=1, source_target_pairs={{2,3},{6,7},{10,11},{14,15},{18,19},{22,23},{26,27},{30,31}} | collective-permute-start | bytes 786440 | tf_op jit(solution)/shard_map/ppermute | solution.py:285
  56.8 5.9 %collective-permute-start.14 = (f32[8,2,16,256]{3,2,1,0:T(8,128)S(1)}, f32[8,2,16,256]{3,2,1,0:T(8,128)}, u32[]{:S(2)}, u32[]{:S(2)}) collective-permute-start(f32[8,2,16,256]{3,2,1,0:T(8,128)S(1)} %collective-permute-done.13.refs_12_), channel_id=1, source_target_pairs={{2,3},{6,7},{11,10},{15,14},{16,17},{20,21},{25,24},{29,28}} | collective-permute-start | bytes 786440 | tf_op jit(solution)/shard_map/ppermute | solution.py:285
  61.9 0.8 %copy-start.3 = (f32[128,128]{1,0:T(8,128)S(1)}, f32[128,128]{1,0:T(8,128)}, u32[]{:S(2)}) copy-start(f32[128,128]{1,0:T(8,128)} %copy-done.2) | copy-start | bytes 196612

commit v10 on v9

--- a/solution.py
+++ b/solution.py
@@ -179,15 +179,22 @@
         pl.when(distance == e)(functools.partial(take, ref))
 
 
-def assemble_kernel(map_ref, front_ref, strips_ref, out_ref):
+def assemble_kernel(map_ref, updated_ref, strips_ref, out_ref):
     n_row, n_col = lax.axis_size("row"), lax.axis_size("col")
     col = lax.axis_index("col")
     row_blocks = out_ref.shape[0] // BLK
-    out_ref[...] = front_ref[...]
-    for i in range(strips_ref.shape[0]):
-        local = map_ref[i // n_row, i % n_row * n_col + col] - col * row_blocks
-        start = pl.multiple_of(local * BLK, BLK)
-        out_ref[pl.ds(start, BLK), :] += strips_ref[i]
+    out_ref[...] = updated_ref[...]
+
+    @pl.when(owner_of() != 0)
+    def _():
+        for i in range(strips_ref.shape[0]):
+            local = map_ref[i // n_row, i % n_row * n_col + col] - col * row_blocks
+            start = pl.multiple_of(local * BLK, BLK)
+            out_ref[pl.ds(start, BLK), :] += strips_ref[i]
+
+        @pl.when(col == 0)
+        def _():
+            out_ref[:PIVOTS, :] = jnp.zeros((PIVOTS, out_ref.shape[1]), jnp.float32)
 
 
 def finish_kernel(few, base_ref, *refs):
@@ -366,27 +373,29 @@
         name="pivot_second",
     )(first, side, rest)
     if few:
-        inverses, held = over_col(inverse, [0] * owners)
-        strips, _ = lax.optimization_barrier((last, held))
-        base = pl.pallas_call(
-            assemble_kernel,
-            out_shape=f32(rows, width),
-            in_specs=[SMEM, VMEM, VMEM],
-            out_specs=VMEM,
-            compiler_params=PARAMS,
-            name="assemble",
-        )(child_map, base, strips)
+        inverses, _ = over_col(inverse, [0] * owners)
     else:
         inverses, parts = [inverse], [last]
-    return pl.pallas_call(
+    updated = pl.pallas_call(
         functools.partial(finish_kernel, few),
         out_shape=f32(rows, width),
         in_specs=[VMEM] * (4 + len(panel) + len(inverses) + len(parts)),
         out_specs=VMEM,
         scratch_shapes=[pltpu.VMEM((n, width), jnp.float32) for n in (rows, width, PIVOTS)],
         compiler_params=PARAMS,
+        cost_estimate=pl.CostEstimate(flops=3_000_000_000, bytes_accessed=1 << 20, transcendentals=0),
         name="finish",
     )(base, *panel, upper, side, upper2, *inverses, *parts)
+    if not few:
+        return updated
+    return pl.pallas_call(
+        assemble_kernel,
+        out_shape=f32(rows, width),
+        in_specs=[SMEM, VMEM, VMEM],
+        out_specs=VMEM,
+        compiler_params=PARAMS,
+        name="assemble",
+    )(child_map, updated, last)
 
 
 def solution(mesh):

time: 66 us -> 63.7 us (0.965)
  starting transfers between devices: 36.1 us -> 34 us
  Pallas kernels: 15.4 us -> 14.2 us
  waiting for transfers between devices: 12.2 us -> 13.3 us
    pallas_call x1, Pallas kernels: 2.75 us -> 0.86 us  [body(): pl.pallas_call(functools.partial(finish_kernel, few), out_shape=f32(rows,...]
    ppermute x2, starting transfers between devices: 2.74 us -> 1.34 us  [over_col(): lax.ppermute(over_x, axes, pairs(2, 3))]
    ppermute x2, waiting for transfers between devices: 0.6 us -> 1.97 us  [over_col(): over_x = lax.ppermute(value, axes, pairs(0, 2))]
    ppermute x2, starting transfers between devices: 3.31 us -> 2.61 us  [over_col(): beside = lax.ppermute(value, axes, pairs(0, 1))]
    pallas_call x1, Pallas kernels: 0.7 us -> 1.38 us  [body(): pl.pallas_call(assemble_kernel, out_shape=f32(rows, width), in_specs=[SME...]
  transfers between devices with their start and end apart: 17 -> 17, of which waited for: 7 -> 7; matrix products, arithmetic and copies ran while one was open for 0% -> 0% of each run, Pallas kernels for 18% -> 19%
where the time goes in v10:
time: 63.7 us; the launch traced here: 63.3 us
  starting transfers between devices  34 us (53%)
  Pallas kernels  14.2 us (22%)
  waiting for transfers between devices  13.3 us (21%)
  local copies, waits for them, and re-layouts  1.31 us (2%)
    ppermute x3, starting transfers between devices, gather_pieces(): got = got + lax.ppermute(cut[:, :, r], OWNER, [(0, r)])  9.56 us
    pallas_call x1, Pallas kernels, body(): pl.pallas_call(functools.partial(first_half_kernel, few), out_shape=[half...  4.96 us
    pallas_call x1, Pallas kernels, body(): pl.pallas_call(functools.partial(second_half_kernel, few), out_shape=[hal...  4.66 us
    ppermute x3, starting transfers between devices, gather_pieces(): lax.ppermute(mine, 'row', [(i, i ^ d) for i in range(n_row)])  4.45 us
    all_to_all x1, starting transfers between devices, gather_pieces(): lax.all_to_all(strips, OWNER, split_axis=0, concat_axis=0, tiled=True)  3.56 us
    all_to_all x1, waiting for transfers between devices, gather_pieces(): lax.all_to_all(strips, OWNER, split_axis=0, concat_axis=0, tiled=True)  3.55 us
    ppermute x3, waiting for transfers between devices, gather_pieces(): lax.ppermute(mine, 'row', [(i, i ^ d) for i in range(n_row)])  3.38 us
    all_to_all x1, starting transfers between devices, gather_pieces(): lax.all_to_all(panel, OWNER, split_axis=0, concat_axis=0, tiled=True)  3.37 us
  transfers between devices with their start and end apart: 17, of which 7 were waited for; matrix products, arithmetic and copies ran while one was open for 0% of the time, Pallas kernels for 19%

profile of v10, /device:TPU:0, one launch (start us, length us, event | category | flops | bytes accessed | tf_op | source)
XLA Modules:
  0.0 63.3 jit_solution(2167823156489173279)
XLA Ops:
  0.0 0.0 copy-start
  0.0 1.2 %fusion.4 = (f32[4,2,1,16,256]{4,3,2,1,0:T(8,128)S(1)}, f32[4,2,1,16,256]{4,3,2,1,0:T(8,128)S(1)}, f32[4,2,1,16,256]{4,3,2,1,0:T(8,128)S(1)}, f32[4,2,1,16,256]{4,3,2,1,0:T(8,128)S(1)}) fusion(f32[4,2,4,16,256]{4,3,2,1,0:T(8,128)} %bitcast.28), kind=kLoop, calls=%fused_computation.14 | loop fusion | bytes 1048576 | tf_op jit(solution)/shard_map/slice | solution.py:302
  1.2 7.0 %collective-permute-start.2 = (f32[4,2,16,256]{3,2,0,1:T(8,128)S(1)}, f32[4,2,16,256]{3,2,0,1:T(8,128)S(1)}, u32[]{:S(2)}, u32[]{:S(2)}) collective-permute-start(f32[4,2,16,256]{3,2,0,1:T(8,128)S(1)} %bitcast.30), channel_id=1, source_target_pairs={{0,12},{1,13},{2,14},{3,15}} | collective-permute-start | bytes 393224 | tf_op jit(solution)/shard_map/ppermute | solution.py:304
  8.2 1.3 %collective-permute-start = (f32[4,2,16,256]{3,2,0,1:T(8,128)S(1)}, f32[4,2,16,256]{3,2,0,1:T(8,128)S(1)}, u32[]{:S(2)}, u32[]{:S(2)}) collective-permute-start(f32[4,2,16,256]{3,2,0,1:T(8,128)S(1)} %bitcast.31), channel_id=1, source_target_pairs={{0,4},{1,5},{2,6},{3,7}} | collective-permute-start | bytes 393224 | tf_op jit(solution)/shard_map/ppermute | solution.py:304
  9.6 0.0 copy-start.2
  9.6 1.3 %collective-permute-start.1 = (f32[4,2,16,256]{3,2,0,1:T(8,128)S(1)}, f32[4,2,16,256]{3,2,0,1:T(8,128)S(1)}, u32[]{:S(2)}, u32[]{:S(2)}) collective-permute-start(f32[4,2,16,256]{3,2,0,1:T(8,128)S(1)} %bitcast.32), channel_id=1, source_target_pairs={{0,8},{1,9},{2,10},{3,11}} | collective-permute-start | bytes 393224 | tf_op jit(solution)/shard_map/ppermute | solution.py:304
  10.9 0.0 copy-done
  10.9 0.0 copy-done.2
  10.9 1.7 %split.1 = (f32[8,16,256]{2,1,0:T(8,128)}, f32[8,128,256]{2,1,0:T(8,128)}) custom-call(s32[2,16]{1,0:T(2,128)S(1)} %copy-done.2, f32[128,2048]{1,0:T(8,128)S(1)} %bitcast.27), custom_call_target="tpu_custom_call" | custom-call | tf_op jit(solution)/shard_map/split/pallas_call | solution.py:307
  12.6 3.4 %all-to-all-start = ((f32[8,16,256]{2,1,0:T(8,128)}), f32[8,16,256]{2,1,0:T(8,128)S(1)}, u32[]{:S(2)}, u32[]{:S(2)}) async-start(f32[8,16,256]{2,1,0:T(8,128)} %get-tuple-element.18), calls=%async_computation | async-start | bytes 262144 | tf_op jit(solution)/shard_map/all_to_all | solution.py:316
  16.0 0.0 collective-permute-done.2
  16.0 0.0 collective-permute-done
  16.0 0.9 %collective-permute-done.1 = f32[4,2,16,256]{3,2,0,1:T(8,128)S(1)} collective-permute-done((f32[4,2,16,256]{3,2,0,1:T(8,128)S(1)}, f32[4,2,16,256]{3,2,0,1:T(8,128)S(1)}, u32[]{:S(2)}, u32[]{:S(2)}) %collective-permute-start.1) | collective-permute-done | bytes 131104 | tf_op jit(solution)/shard_map/ppermute | solution.py:304
  17.0 2.9 %collective-permute-start.3 = (f32[4,16,256]{2,1,0:T(8,128)S(1)}, f32[4,16,256]{2,1,0:T(8,128)S(1)}, u32[]{:S(2)}, u32[]{:S(2)}) collective-permute-start(f32[4,16,256]{2,1,0:T(8,128)S(1)} %get-tuple-element.36), channel_id=1, source_target_pairs={{0,16},{4,20},{8,24},{12,28},{1,17},{5,21},{9,25},{13,29},{2,18},{... | collective-permute-start | bytes 196616 | tf_op jit(solution)/shard_map/ppermute | solution.py:306
  20.0 2.0 %collective-permute-done.3.high_ref = f32[4,16,256]{2,1,0:T(8,128)S(1)} collective-permute-done((f32[4,16,256]{2,1,0:T(8,128)S(1)}, f32[4,16,256]{2,1,0:T(8,128)S(1)}, u32[]{:S(2)}, u32[]{:S(2)}) %collective-permute-start.3) | collective-permute-done | bytes 65568 | tf_op jit(solution)/shard_map/ppermute | solution.py:306
  21.9 1.5 %all-to-all-done.pieces_ref = f32[8,16,256]{2,1,0:T(8,128)S(1)} async-done(((f32[8,16,256]{2,1,0:T(8,128)}), f32[8,16,256]{2,1,0:T(8,128)S(1)}, u32[]{:S(2)}, u32[]{:S(2)}) %all-to-all-start) | async-done | bytes 131104 | tf_op jit(solution)/shard_map/all_to_all | solution.py:316
  23.5 0.6 sum_panel.1
  24.1 1.7 %collective-permute-start.6 = (f32[4,16,256]{2,1,0:T(8,128)S(1)}, f32[4,16,256]{2,1,0:T(8,128)S(1)}, u32[]{:S(2)}, u32[]{:S(2)}) collective-permute-start(f32[4,16,256]{2,1,0:T(8,128)S(1)} %sum_panel.1), channel_id=1, source_target_pairs={{0,12},{4,8},{8,4},{12,0},{1,13},{5,9},{9,5},{13,1},{2,14},{6,10},... | collective-permute-start | bytes 196616 | tf_op jit(solution)/shard_map/ppermute | solution.py:326
  25.8 0.0 collective-permute-start.5
  25.8 2.7 %collective-permute-start.4 = (f32[4,16,256]{2,1,0:T(8,128)S(1)}, f32[4,16,256]{2,1,0:T(8,128)S(1)}, u32[]{:S(2)}, u32[]{:S(2)}) collective-permute-start(f32[4,16,256]{2,1,0:T(8,128)S(1)} %sum_panel.1), channel_id=1, source_target_pairs={{0,4},{4,0},{8,12},{12,8},{1,5},{5,1},{9,13},{13,9},{2,6},{6,2},{1... | collective-permute-start | bytes 196616 | tf_op jit(solution)/shard_map/ppermute | solution.py:326
  28.5 1.8 %collective-permute-done.6 = f32[4,16,256]{2,1,0:T(8,128)S(1)} collective-permute-done((f32[4,16,256]{2,1,0:T(8,128)S(1)}, f32[4,16,256]{2,1,0:T(8,128)S(1)}, u32[]{:S(2)}, u32[]{:S(2)}) %collective-permute-start.6) | collective-permute-done | bytes 65568 | tf_op jit(solution)/shard_map/ppermute | solution.py:326
  30.3 1.6 %collective-permute-done.5 = f32[4,16,256]{2,1,0:T(8,128)S(1)} collective-permute-done((f32[4,16,256]{2,1,0:T(8,128)S(1)}, f32[4,16,256]{2,1,0:T(8,128)S(1)}, u32[]{:S(2)}, u32[]{:S(2)}) %collective-permute-start.5) | collective-permute-done | bytes 65568 | tf_op jit(solution)/shard_map/ppermute | solution.py:326
  31.9 0.0 collective-permute-done.4
  32.0 1.5 %collective-permute-start.7 = (f32[4,2,16,256]{3,2,1,0:T(8,128)S(1)}, f32[4,2,16,256]{3,2,1,0:T(8,128)S(1)}, u32[]{:S(2)}, u32[]{:S(2)}) collective-permute-start(f32[4,2,16,256]{3,2,1,0:T(8,128)S(1)} %get-tuple-element.35), channel_id=1, source_target_pairs={{0,16},{16,0},{1,17},{17,1},{2,18},{18,2},{3,19},{19,3},{4,20},{20... | collective-permute-start | bytes 393224 | tf_op jit(solution)/shard_map/ppermute | solution.py:329
  33.4 3.6 %all-to-all-start.1 = ((f32[8,128,256]{2,1,0:T(8,128)}), f32[8,128,256]{2,1,0:T(8,128)S(1)}, u32[]{:S(2)}, u32[]{:S(2)}) async-start(f32[8,128,256]{2,1,0:T(8,128)} %get-tuple-element.28), calls=%async_computation.1 | async-start | bytes 2097152 | tf_op jit(solution)/shard_map/all_to_all | solution.py:328
  37.0 0.0 collective-permute-done.7.refs_1_
  37.0 5.0 %pivot_first.1 = (f32[128,128]{1,0:T(8,128)S(1)}, f32[128,128]{1,0:T(8,128)S(1)}, f32[128,128]{1,0:T(8,128)S(1)}, f32[128,128]{1,0:T(8,128)S(1)}) custom-call(f32[4,4,16,256]{3,2,1,0:T(8,128)S(1)} %pad_maximum_fusion.refs_0_, f32[4,2,16,256]{3,2,1,0:T(8,128)S(1)} %collective-permute-done.7.refs_1_), custom_call_target="tpu_custom_call" | custom-call | flops 8000000000 | bytes 262144 | tf_op jit(solution)/shard_map/pivot_first/pallas_call | solution.py:344
  42.0 2.0 %collective-permute-start.8 = (f32[4,2,16,256]{3,2,1,0:T(8,128)S(1)}, f32[4,2,16,256]{3,2,1,0:T(8,128)S(1)}, u32[]{:S(2)}, u32[]{:S(2)}) collective-permute-start(f32[4,2,16,256]{3,2,1,0:T(8,128)S(1)} %get-tuple-element.21), channel_id=1, source_target_pairs={{0,16},{16,0},{1,17},{17,1},{2,18},{18,2},{3,19},{19,3},{4,20},{20... | collective-permute-start | bytes 393224 | tf_op jit(solution)/shard_map/ppermute | solution.py:358
  44.0 4.7 %pivot_second.1 = (f32[128,128]{1,0:T(8,128)S(1)}, f32[256,256]{1,0:T(8,128)S(1)}) custom-call(f32[128,128]{1,0:T(8,128)S(1)} %get-tuple-element.24.first_ref, f32[128,128]{1,0:T(8,128)S(1)} %get-tuple-element.23.side_ref.refs_4_, f32[128,128]{1,0:T(8,128)S(1)} %get-tuple-element.25.next_ref), custom_call_target="tpu_custom_call" | custom-call | flops 8000000000 | bytes 262144 | tf_op jit(solution)/shard_map/pivot_second/pallas_call | solution.py:365
  48.6 0.0 copy-start.1
  48.7 1.4 %collective-permute-start.10 = (f32[256,256]{1,0:T(8,128)S(1)}, f32[256,256]{1,0:T(8,128)S(1)}, u32[]{:S(2)}, u32[]{:S(2)}) collective-permute-start(f32[256,256]{1,0:T(8,128)S(1)} %get-tuple-element.27.refs_6_), channel_id=1, source_target_pairs={{0,2},{4,6},{8,10},{12,14},{16,18},{20,22},{24,26},{28,30}} | collective-permute-start | bytes 786440 | tf_op jit(solution)/shard_map/ppermute | solution.py:290
  50.1 0.0 collective-permute-done.8.refs_2_
  50.2 1.3 %collective-permute-start.13 = (f32[8,2,16,256]{3,2,1,0:T(8,128)S(1)}, f32[8,2,16,256]{3,2,1,0:T(8,128)S(1)}, u32[]{:S(2)}, u32[]{:S(2)}) collective-permute-start(f32[8,2,16,256]{3,2,1,0:T(8,128)S(1)} %pad_maximum_fusion.1.refs_10_), channel_id=1, source_target_pairs={{0,2},{4,6},{9,11},{13,15},{18,16},{22,20},{27,25},{31,29}} | collective-permute-start | bytes 786440 | tf_op jit(solution)/shard_map/ppermute | solution.py:290
  51.5 1.3 %collective-permute-start.9 = (f32[256,256]{1,0:T(8,128)S(1)}, f32[256,256]{1,0:T(8,128)S(1)}, u32[]{:S(2)}, u32[]{:S(2)}) collective-permute-start(f32[256,256]{1,0:T(8,128)S(1)} %get-tuple-element.27.refs_6_), channel_id=1, source_target_pairs={{0,1},{4,5},{8,9},{12,13},{16,17},{20,21},{24,25},{28,29}} | collective-permute-start | bytes 786440 | tf_op jit(solution)/shard_map/ppermute | solution.py:291
  52.8 1.3 %collective-permute-start.12 = (f32[8,2,16,256]{3,2,1,0:T(8,128)S(1)}, f32[8,2,16,256]{3,2,1,0:T(8,128)S(1)}, u32[]{:S(2)}, u32[]{:S(2)}) collective-permute-start(f32[8,2,16,256]{3,2,1,0:T(8,128)S(1)} %pad_maximum_fusion.1.refs_10_), channel_id=1, source_target_pairs={{0,1},{4,5},{9,8},{13,12},{18,19},{22,23},{27,26},{31,30}} | collective-permute-start | bytes 786440 | tf_op jit(solution)/shard_map/ppermute | solution.py:291
  54.1 0.0 collective-permute-done.10.refs_8_
  54.1 0.7 %collective-permute-start.11 = (f32[256,256]{1,0:T(8,128)S(1)}, f32[256,256]{1,0:T(8,128)S(1)}, u32[]{:S(2)}, u32[]{:S(2)}) collective-permute-start(f32[256,256]{1,0:T(8,128)S(1)} %collective-permute-done.10.refs_8_), channel_id=1, source_target_pairs={{2,3},{6,7},{10,11},{14,15},{18,19},{22,23},{26,27},{30,31}} | collective-permute-start | bytes 786440 | tf_op jit(solution)/shard_map/ppermute | solution.py:292
  54.8 2.0 %collective-permute-done.13.refs_12_ = f32[8,2,16,256]{3,2,1,0:T(8,128)S(1)} collective-permute-done((f32[8,2,16,256]{3,2,1,0:T(8,128)S(1)}, f32[8,2,16,256]{3,2,1,0:T(8,128)S(1)}, u32[]{:S(2)}, u32[]{:S(2)}) %collective-permute-start.13) | collective-permute-done | bytes 262176 | tf_op jit(solution)/shard_map/ppermute | solution.py:290
  56.8 0.7 %collective-permute-start.14 = (f32[8,2,16,256]{3,2,1,0:T(8,128)S(1)}, f32[8,2,16,256]{3,2,1,0:T(8,128)S(1)}, u32[]{:S(2)}, u32[]{:S(2)}) collective-permute-start(f32[8,2,16,256]{3,2,1,0:T(8,128)S(1)} %collective-permute-done.13.refs_12_), channel_id=1, source_target_pairs={{2,3},{6,7},{11,10},{15,14},{16,17},{20,21},{25,24},{29,28}} | collective-permute-start | bytes 786440 | tf_op jit(solution)/shard_map/ppermute | solution.py:292
  57.4 0.0 collective-permute-done.9.refs_7_
  57.5 0.0 collective-permute-done.12.refs_11_
  57.5 0.0 collective-permute-done.11.refs_9_
  57.5 0.0 collective-permute-done.14.refs_13_
  57.5 0.0 copy-done.1
  57.5 0.9 %finish.1.updated_ref = f32[512,256]{1,0:T(8,128)S(1)} custom-call(f32[512,256]{1,0:T(8,128)S(1)} %copy-done.1, f32[4,4,16,256]{3,2,1,0:T(8,128)S(1)} %pad_maximum_fusion.refs_0_, f32[4,2,16,256]{3,2,1,0:T(8,128)S(1)} %collective-permute-done.7.refs_1_, f32[4,2,16,256]{3,2,1,0:T(8,128)S(1)} %collective-permute-done.8.refs_2_, ...), custom_call_target="tpu_custom_call" | custom-call | flops 3000000000 | bytes 1048576 | tf_op jit(solution)/shard_map/finish/pallas_call | solution.py:379
  58.4 3.5 %all-to-all-done.1.strips_ref = f32[8,128,256]{2,1,0:T(8,128)S(1)} async-done(((f32[8,128,256]{2,1,0:T(8,128)}), f32[8,128,256]{2,1,0:T(8,128)S(1)}, u32[]{:S(2)}, u32[]{:S(2)}) %all-to-all-start.1) | async-done | bytes 1048608 | tf_op jit(solution)/shard_map/all_to_all | solution.py:328
  61.9 1.4 %assemble.1 = f32[512,256]{1,0:T(8,128)} custom-call(s32[2,16]{1,0:T(2,128)S(1)} %copy-done.2, f32[512,256]{1,0:T(8,128)S(1)} %finish.1.updated_ref, f32[8,128,256]{2,1,0:T(8,128)S(1)} %all-to-all-done.1.strips_ref), custom_call_target="tpu_custom_call" | custom-call | tf_op jit(solution)/shard_map/assemble/pallas_call | solution.py:391
  (9 shorter events, 0.2 us)
Async XLA Ops:
  0.0 10.9 %copy-start = (f32[1,128,2048]{2,1,0:T(8,128)S(1)}, f32[1,128,2048]{2,1,0:T(8,128)}, u32[]{:S(2)}) copy-start(f32[1,128,2048]{2,1,0:T(8,128)} %param.4) | copy-start | bytes 3145732
  1.2 14.8 %collective-permute-start.2 = (f32[4,2,16,256]{3,2,0,1:T(8,128)S(1)}, f32[4,2,16,256]{3,2,0,1:T(8,128)S(1)}, u32[]{:S(2)}, u32[]{:S(2)}) collective-permute-start(f32[4,2,16,256]{3,2,0,1:T(8,128)S(1)} %bitcast.30), channel_id=1, source_target_pairs={{0,12},{1,13},{2,14},{3,15}} | collective-permute-start | bytes 393224 | tf_op jit(solution)/shard_map/ppermute | solution.py:304
  8.2 7.8 %collective-permute-start = (f32[4,2,16,256]{3,2,0,1:T(8,128)S(1)}, f32[4,2,16,256]{3,2,0,1:T(8,128)S(1)}, u32[]{:S(2)}, u32[]{:S(2)}) collective-permute-start(f32[4,2,16,256]{3,2,0,1:T(8,128)S(1)} %bitcast.31), channel_id=1, source_target_pairs={{0,4},{1,5},{2,6},{3,7}} | collective-permute-start | bytes 393224 | tf_op jit(solution)/shard_map/ppermute | solution.py:304
  9.6 1.3 %copy-start.2 = (s32[2,16]{1,0:T(2,128)S(1)}, s32[2,16]{1,0:T(2,128)}, u32[]{:S(2)}) copy-start(s32[2,16]{1,0:T(2,128)} %map_ref.5) | copy-start | bytes 388
  9.6 7.4 %collective-permute-start.1 = (f32[4,2,16,256]{3,2,0,1:T(8,128)S(1)}, f32[4,2,16,256]{3,2,0,1:T(8,128)S(1)}, u32[]{:S(2)}, u32[]{:S(2)}) collective-permute-start(f32[4,2,16,256]{3,2,0,1:T(8,128)S(1)} %bitcast.32), channel_id=1, source_target_pairs={{0,8},{1,9},{2,10},{3,11}} | collective-permute-start | bytes 393224 | tf_op jit(solution)/shard_map/ppermute | solution.py:304
  12.6 10.8 %all-to-all-start = ((f32[8,16,256]{2,1,0:T(8,128)}), f32[8,16,256]{2,1,0:T(8,128)S(1)}, u32[]{:S(2)}, u32[]{:S(2)}) async-start(f32[8,16,256]{2,1,0:T(8,128)} %get-tuple-element.18), calls=%async_computation | async-start | bytes 262144 | tf_op jit(solution)/shard_map/all_to_all | solution.py:316
  17.0 4.9 %collective-permute-start.3 = (f32[4,16,256]{2,1,0:T(8,128)S(1)}, f32[4,16,256]{2,1,0:T(8,128)S(1)}, u32[]{:S(2)}, u32[]{:S(2)}) collective-permute-start(f32[4,16,256]{2,1,0:T(8,128)S(1)} %get-tuple-element.36), channel_id=1, source_target_pairs={{0,16},{4,20},{8,24},{12,28},{1,17},{5,21},{9,25},{13,29},{2,18},{... | collective-permute-start | bytes 196616 | tf_op jit(solution)/shard_map/ppermute | solution.py:306
  24.1 6.3 %collective-permute-start.6 = (f32[4,16,256]{2,1,0:T(8,128)S(1)}, f32[4,16,256]{2,1,0:T(8,128)S(1)}, u32[]{:S(2)}, u32[]{:S(2)}) collective-permute-start(f32[4,16,256]{2,1,0:T(8,128)S(1)} %sum_panel.1), channel_id=1, source_target_pairs={{0,12},{4,8},{8,4},{12,0},{1,13},{5,9},{9,5},{13,1},{2,14},{6,10},... | collective-permute-start | bytes 196616 | tf_op jit(solution)/shard_map/ppermute | solution.py:326
  25.8 6.1 %collective-permute-start.5 = (f32[4,16,256]{2,1,0:T(8,128)S(1)}, f32[4,16,256]{2,1,0:T(8,128)S(1)}, u32[]{:S(2)}, u32[]{:S(2)}) collective-permute-start(f32[4,16,256]{2,1,0:T(8,128)S(1)} %sum_panel.1), channel_id=1, source_target_pairs={{0,8},{4,12},{8,0},{12,4},{1,9},{5,13},{9,1},{13,5},{2,10},{6,14},... | collective-permute-start | bytes 196616 | tf_op jit(solution)/shard_map/ppermute | solution.py:326
  25.8 6.1 %collective-permute-start.4 = (f32[4,16,256]{2,1,0:T(8,128)S(1)}, f32[4,16,256]{2,1,0:T(8,128)S(1)}, u32[]{:S(2)}, u32[]{:S(2)}) collective-permute-start(f32[4,16,256]{2,1,0:T(8,128)S(1)} %sum_panel.1), channel_id=1, source_target_pairs={{0,4},{4,0},{8,12},{12,8},{1,5},{5,1},{9,13},{13,9},{2,6},{6,2},{1... | collective-permute-start | bytes 196616 | tf_op jit(solution)/shard_map/ppermute | solution.py:326
  32.0 5.0 %collective-permute-start.7 = (f32[4,2,16,256]{3,2,1,0:T(8,128)S(1)}, f32[4,2,16,256]{3,2,1,0:T(8,128)S(1)}, u32[]{:S(2)}, u32[]{:S(2)}) collective-permute-start(f32[4,2,16,256]{3,2,1,0:T(8,128)S(1)} %get-tuple-element.35), channel_id=1, source_target_pairs={{0,16},{16,0},{1,17},{17,1},{2,18},{18,2},{3,19},{19,3},{4,20},{20... | collective-permute-start | bytes 393224 | tf_op jit(solution)/shard_map/ppermute | solution.py:329
  33.4 28.5 %all-to-all-start.1 = ((f32[8,128,256]{2,1,0:T(8,128)}), f32[8,128,256]{2,1,0:T(8,128)S(1)}, u32[]{:S(2)}, u32[]{:S(2)}) async-start(f32[8,128,256]{2,1,0:T(8,128)} %get-tuple-element.28), calls=%async_computation.1 | async-start | bytes 2097152 | tf_op jit(solution)/shard_map/all_to_all | solution.py:328
  42.0 8.1 %collective-permute-start.8 = (f32[4,2,16,256]{3,2,1,0:T(8,128)S(1)}, f32[4,2,16,256]{3,2,1,0:T(8,128)S(1)}, u32[]{:S(2)}, u32[]{:S(2)}) collective-permute-start(f32[4,2,16,256]{3,2,1,0:T(8,128)S(1)} %get-tuple-element.21), channel_id=1, source_target_pairs={{0,16},{16,0},{1,17},{17,1},{2,18},{18,2},{3,19},{19,3},{4,20},{20... | collective-permute-start | bytes 393224 | tf_op jit(solution)/shard_map/ppermute | solution.py:358
  48.6 8.8 %copy-start.1 = (f32[512,256]{1,0:T(8,128)S(1)}, f32[512,256]{1,0:T(8,128)}, u32[]{:S(2)}) copy-start(f32[512,256]{1,0:T(8,128)} %base_ref.1) | copy-start | bytes 1572868
  48.7 5.5 %collective-permute-start.10 = (f32[256,256]{1,0:T(8,128)S(1)}, f32[256,256]{1,0:T(8,128)S(1)}, u32[]{:S(2)}, u32[]{:S(2)}) collective-permute-start(f32[256,256]{1,0:T(8,128)S(1)} %get-tuple-element.27.refs_6_), channel_id=1, source_target_pairs={{0,2},{4,6},{8,10},{12,14},{16,18},{20,22},{24,26},{28,30}} | collective-permute-start | bytes 786440 | tf_op jit(solution)/shard_map/ppermute | solution.py:290
  50.2 6.6 %collective-permute-start.13 = (f32[8,2,16,256]{3,2,1,0:T(8,128)S(1)}, f32[8,2,16,256]{3,2,1,0:T(8,128)S(1)}, u32[]{:S(2)}, u32[]{:S(2)}) collective-permute-start(f32[8,2,16,256]{3,2,1,0:T(8,128)S(1)} %pad_maximum_fusion.1.refs_10_), channel_id=1, source_target_pairs={{0,2},{4,6},{9,11},{13,15},{18,16},{22,20},{27,25},{31,29}} | collective-permute-start | bytes 786440 | tf_op jit(solution)/shard_map/ppermute | solution.py:290
  51.5 6.0 %collective-permute-start.9 = (f32[256,256]{1,0:T(8,128)S(1)}, f32[256,256]{1,0:T(8,128)S(1)}, u32[]{:S(2)}, u32[]{:S(2)}) collective-permute-start(f32[256,256]{1,0:T(8,128)S(1)} %get-tuple-element.27.refs_6_), channel_id=1, source_target_pairs={{0,1},{4,5},{8,9},{12,13},{16,17},{20,21},{24,25},{28,29}} | collective-permute-start | bytes 786440 | tf_op jit(solution)/shard_map/ppermute | solution.py:291
  52.8 4.7 %collective-permute-start.12 = (f32[8,2,16,256]{3,2,1,0:T(8,128)S(1)}, f32[8,2,16,256]{3,2,1,0:T(8,128)S(1)}, u32[]{:S(2)}, u32[]{:S(2)}) collective-permute-start(f32[8,2,16,256]{3,2,1,0:T(8,128)S(1)} %pad_maximum_fusion.1.refs_10_), channel_id=1, source_target_pairs={{0,1},{4,5},{9,8},{13,12},{18,19},{22,23},{27,26},{31,30}} | collective-permute-start | bytes 786440 | tf_op jit(solution)/shard_map/ppermute | solution.py:291
  54.1 3.3 %collective-permute-start.11 = (f32[256,256]{1,0:T(8,128)S(1)}, f32[256,256]{1,0:T(8,128)S(1)}, u32[]{:S(2)}, u32[]{:S(2)}) collective-permute-start(f32[256,256]{1,0:T(8,128)S(1)} %collective-permute-done.10.refs_8_), channel_id=1, source_target_pairs={{2,3},{6,7},{10,11},{14,15},{18,19},{22,23},{26,27},{30,31}} | collective-permute-start | bytes 786440 | tf_op jit(solution)/shard_map/ppermute | solution.py:292
  56.8 0.7 %collective-permute-start.14 = (f32[8,2,16,256]{3,2,1,0:T(8,128)S(1)}, f32[8,2,16,256]{3,2,1,0:T(8,128)S(1)}, u32[]{:S(2)}, u32[]{:S(2)}) collective-permute-start(f32[8,2,16,256]{3,2,1,0:T(8,128)S(1)} %collective-permute-done.13.refs_12_), channel_id=1, source_target_pairs={{2,3},{6,7},{11,10},{15,14},{16,17},{20,21},{25,24},{29,28}} | collective-permute-start | bytes 786440 | tf_op jit(solution)/shard_map/ppermute | solution.py:292

commit v11 on v10

--- a/solution.py
+++ b/solution.py
@@ -340,7 +340,7 @@
     gather = gather_pieces if few else gather_wide
     base, panel, pivot, last = gather(front, child_blocks[0], child_map)
     half = f32(BLK, BLK)
-    cost = pl.CostEstimate(flops=8_000_000_000, bytes_accessed=1 << 18, transcendentals=0)
+    cost = pl.CostEstimate(flops=500_000_000, bytes_accessed=1 << 18, transcendentals=0)
     upper, first, side, rest = pl.pallas_call(
         functools.partial(first_half_kernel, few),
         out_shape=[half] * 4,
@@ -383,7 +383,7 @@
         out_specs=VMEM,
         scratch_shapes=[pltpu.VMEM((n, width), jnp.float32) for n in (rows, width, PIVOTS)],
         compiler_params=PARAMS,
-        cost_estimate=pl.CostEstimate(flops=3_000_000_000, bytes_accessed=1 << 20, transcendentals=0),
+        cost_estimate=pl.CostEstimate(flops=500_000_000, bytes_accessed=1 << 20, transcendentals=0),
         name="finish",
     )(base, *panel, upper, side, upper2, *inverses, *parts)
     if not few:

time: 63.7 us -> 90.2 us (1.42)
  the two profiles are of different devices: /device:TPU:0 before, /device:TPU:5 now
where the time goes in v11:
time: 90.2 us; the launch traced here: 89.7 us
  waiting for transfers between devices  54.9 us (61%)
  starting transfers between devices  27.4 us (30%)
  Pallas kernels  5.83 us (6%)
  local copies, waits for them, and re-layouts  1.31 us (1%)
    ppermute x3, waiting for transfers between devices, gather_pieces(): lax.ppermute(mine, 'row', [(i, i ^ d) for i in range(n_row)])  24.9 us
    ppermute x2, waiting for transfers between devices, over_col(): beside = lax.ppermute(value, axes, pairs(0, 1))  11.3 us
    all_to_all x1, starting transfers between devices, gather_pieces(): lax.all_to_all(panel, OWNER, split_axis=0, concat_axis=0, tiled=True)  9.34 us
    ppermute x2, waiting for transfers between devices, over_col(): lax.ppermute(over_x, axes, pairs(2, 3))  6.95 us
    all_to_all x1, starting transfers between devices, gather_pieces(): lax.all_to_all(strips, OWNER, split_axis=0, concat_axis=0, tiled=True)  5.16 us
    ppermute x1, waiting for transfers between devices, body(): far_rest = lax.ppermute(later, 'grp', [(0, 1), (1, 0)])  4.2 us
    ppermute x1, waiting for transfers between devices, gather_pieces(): lax.ppermute(got[:, 1], OWNER, [(r, n_row + r) for r in range(n_row)])  4.02 us
    ppermute x3, starting transfers between devices, gather_pieces(): lax.ppermute(mine, 'row', [(i, i ^ d) for i in range(n_row)])  3.55 us
  transfers between devices with their start and end apart: 17, of which 7 were waited for; matrix products, arithmetic and copies ran while one was open for 0% of the time, Pallas kernels for 4%

profile of v11, /device:TPU:5, one launch (start us, length us, event | category | flops | bytes accessed | tf_op | source)
XLA Modules:
  0.0 89.7 jit_solution(15179475389669692764)
XLA Ops:
  0.0 0.0 copy-start.1
  0.0 1.2 %fusion.4 = (f32[4,2,1,16,256]{4,3,2,1,0:T(8,128)S(1)}, f32[4,2,1,16,256]{4,3,2,1,0:T(8,128)S(1)}, f32[4,2,1,16,256]{4,3,2,1,0:T(8,128)S(1)}, f32[4,2,1,16,256]{4,3,2,1,0:T(8,128)S(1)}) fusion(f32[4,2,4,16,256]{4,3,2,1,0:T(8,128)} %bitcast.27), kind=kLoop, calls=%fused_computation.14 | loop fusion | bytes 1048576 | tf_op jit(solution)/shard_map/slice | solution.py:302
  1.2 0.7 collective-permute-start.2
  1.9 0.7 collective-permute-start
  2.6 0.0 copy-start.2
  2.6 0.7 collective-permute-start.1
  3.3 0.0 copy-done.1
  3.3 0.0 copy-done.2
  3.3 1.7 %split.1 = (f32[8,16,256]{2,1,0:T(8,128)}, f32[8,128,256]{2,1,0:T(8,128)}) custom-call(s32[2,16]{1,0:T(2,128)S(1)} %copy-done.2, f32[128,2048]{1,0:T(8,128)S(1)} %bitcast.28), custom_call_target="tpu_custom_call" | custom-call | tf_op jit(solution)/shard_map/split/pallas_call | solution.py:307
  5.1 9.3 %all-to-all-start = ((f32[8,16,256]{2,1,0:T(8,128)}), f32[8,16,256]{2,1,0:T(8,128)S(1)}, u32[]{:S(2)}, u32[]{:S(2)}) async-start(f32[8,16,256]{2,1,0:T(8,128)} %get-tuple-element.18), calls=%async_computation | async-start | bytes 262144 | tf_op jit(solution)/shard_map/all_to_all | solution.py:316
  14.4 0.0 collective-permute-done.2
  14.4 0.0 collective-permute-done
  14.4 0.0 collective-permute-done.1
  14.5 1.3 %collective-permute-start.3 = (f32[4,16,256]{2,1,0:T(8,128)S(1)}, f32[4,16,256]{2,1,0:T(8,128)S(1)}, u32[]{:S(2)}, u32[]{:S(2)}) collective-permute-start(f32[4,16,256]{2,1,0:T(8,128)S(1)} %get-tuple-element.36), channel_id=1, source_target_pairs={{0,16},{4,20},{8,24},{12,28},{1,17},{5,21},{9,25},{13,29},{2,18},{... | collective-permute-start | bytes 196616 | tf_op jit(solution)/shard_map/ppermute | solution.py:306
  15.8 4.0 %collective-permute-done.3.high_ref = f32[4,16,256]{2,1,0:T(8,128)S(1)} collective-permute-done((f32[4,16,256]{2,1,0:T(8,128)S(1)}, f32[4,16,256]{2,1,0:T(8,128)S(1)}, u32[]{:S(2)}, u32[]{:S(2)}) %collective-permute-start.3) | collective-permute-done | bytes 65568 | tf_op jit(solution)/shard_map/ppermute | solution.py:306
  19.8 0.0 all-to-all-done.pieces_ref
  19.8 0.6 sum_panel.1
  20.4 5.2 %all-to-all-start.1 = ((f32[8,128,256]{2,1,0:T(8,128)}), f32[8,128,256]{2,1,0:T(8,128)S(1)}, u32[]{:S(2)}, u32[]{:S(2)}) async-start(f32[8,128,256]{2,1,0:T(8,128)} %get-tuple-element.28), calls=%async_computation.1 | async-start | bytes 2097152 | tf_op jit(solution)/shard_map/all_to_all | solution.py:328
  25.6 3.0 %collective-permute-start.6 = (f32[4,16,256]{2,1,0:T(8,128)S(1)}, f32[4,16,256]{2,1,0:T(8,128)S(1)}, u32[]{:S(2)}, u32[]{:S(2)}) collective-permute-start(f32[4,16,256]{2,1,0:T(8,128)S(1)} %sum_panel.1), channel_id=1, source_target_pairs={{0,12},{4,8},{8,4},{12,0},{1,13},{5,9},{9,5},{13,1},{2,14},{6,10},... | collective-permute-start | bytes 196616 | tf_op jit(solution)/shard_map/ppermute | solution.py:326
  28.6 0.0 collective-permute-start.5
  28.6 0.6 collective-permute-start.4
  29.1 15.9 %collective-permute-done.6 = f32[4,16,256]{2,1,0:T(8,128)S(1)} collective-permute-done((f32[4,16,256]{2,1,0:T(8,128)S(1)}, f32[4,16,256]{2,1,0:T(8,128)S(1)}, u32[]{:S(2)}, u32[]{:S(2)}) %collective-permute-start.6) | collective-permute-done | bytes 65568 | tf_op jit(solution)/shard_map/ppermute | solution.py:326
  45.1 8.9 %collective-permute-done.5 = f32[4,16,256]{2,1,0:T(8,128)S(1)} collective-permute-done((f32[4,16,256]{2,1,0:T(8,128)S(1)}, f32[4,16,256]{2,1,0:T(8,128)S(1)}, u32[]{:S(2)}, u32[]{:S(2)}) %collective-permute-start.5) | collective-permute-done | bytes 65568 | tf_op jit(solution)/shard_map/ppermute | solution.py:326
  54.0 0.0 collective-permute-done.4
  54.1 0.3 collective-permute-start.7
  54.4 3.5 %collective-permute-done.7.refs_1_ = f32[4,2,16,256]{3,2,1,0:T(8,128)S(1)} collective-permute-done((f32[4,2,16,256]{3,2,1,0:T(8,128)S(1)}, f32[4,2,16,256]{3,2,1,0:T(8,128)S(1)}, u32[]{:S(2)}, u32[]{:S(2)}) %collective-permute-start.7) | collective-permute-done | bytes 131104 | tf_op jit(solution)/shard_map/ppermute | solution.py:329
  58.0 0.3 collective-permute-start.8
  58.3 0.0 copy-start
  58.3 0.8 collective-permute-start.10
  59.1 4.2 %collective-permute-done.8.refs_2_ = f32[4,2,16,256]{3,2,1,0:T(8,128)S(1)} collective-permute-done((f32[4,2,16,256]{3,2,1,0:T(8,128)S(1)}, f32[4,2,16,256]{3,2,1,0:T(8,128)S(1)}, u32[]{:S(2)}, u32[]{:S(2)}) %collective-permute-start.8) | collective-permute-done | bytes 131104 | tf_op jit(solution)/shard_map/ppermute | solution.py:358
  63.3 0.7 collective-permute-start.13
  64.0 1.3 %collective-permute-start.9 = (f32[256,256]{1,0:T(8,128)S(1)}, f32[256,256]{1,0:T(8,128)S(1)}, u32[]{:S(2)}, u32[]{:S(2)}) collective-permute-start(f32[256,256]{1,0:T(8,128)S(1)} %get-tuple-element.27.refs_6_), channel_id=1, source_target_pairs={{0,1},{4,5},{8,9},{12,13},{16,17},{20,21},{24,25},{28,29}} | collective-permute-start | bytes 786440 | tf_op jit(solution)/shard_map/ppermute | solution.py:291
  65.3 0.7 collective-permute-start.12
  66.0 0.0 collective-permute-done.10.refs_8_
  66.0 0.7 collective-permute-start.11
  66.7 0.0 collective-permute-done.13.refs_12_
  66.7 1.3 %collective-permute-start.14 = (f32[8,2,16,256]{3,2,1,0:T(8,128)S(1)}, f32[8,2,16,256]{3,2,1,0:T(8,128)S(1)}, u32[]{:S(2)}, u32[]{:S(2)}) collective-permute-start(f32[8,2,16,256]{3,2,1,0:T(8,128)S(1)} %collective-permute-done.13.refs_12_), channel_id=1, source_target_pairs={{2,3},{6,7},{11,10},{15,14},{16,17},{20,21},{25,24},{29,28}} | collective-permute-start | bytes 786440 | tf_op jit(solution)/shard_map/ppermute | solution.py:292
  68.0 11.3 %collective-permute-done.9.refs_7_ = f32[256,256]{1,0:T(8,128)S(1)} collective-permute-done((f32[256,256]{1,0:T(8,128)S(1)}, f32[256,256]{1,0:T(8,128)S(1)}, u32[]{:S(2)}, u32[]{:S(2)}) %collective-permute-start.9) | collective-permute-done | bytes 262176 | tf_op jit(solution)/shard_map/ppermute | solution.py:291
  79.3 0.0 collective-permute-done.12.refs_11_
  79.3 0.0 collective-permute-done.11.refs_9_
  79.3 6.9 %collective-permute-done.14.refs_13_ = f32[8,2,16,256]{3,2,1,0:T(8,128)S(1)} collective-permute-done((f32[8,2,16,256]{3,2,1,0:T(8,128)S(1)}, f32[8,2,16,256]{3,2,1,0:T(8,128)S(1)}, u32[]{:S(2)}, u32[]{:S(2)}) %collective-permute-start.14) | collective-permute-done | bytes 262176 | tf_op jit(solution)/shard_map/ppermute | solution.py:292
  86.2 0.0 copy-done
  86.2 2.0 %finish.1.updated_ref = f32[512,256]{1,0:T(8,128)S(1)} custom-call(f32[512,256]{1,0:T(8,128)S(1)} %copy-done, f32[4,4,16,256]{3,2,1,0:T(8,128)S(1)} %pad_maximum_fusion.refs_0_, f32[4,2,16,256]{3,2,1,0:T(8,128)S(1)} %collective-permute-done.7.refs_1_, f32[4,2,16,256]{3,2,1,0:T(8,128)S(1)} %collective-permute-done.8.refs_2_, ...), custom_call_target="tpu_custom_call" | custom-call | flops 500000000 | bytes 1048576 | tf_op jit(solution)/shard_map/finish/pallas_call | solution.py:379
  88.2 0.0 all-to-all-done.1.strips_ref
  88.3 1.5 %assemble.1 = f32[512,256]{1,0:T(8,128)} custom-call(s32[2,16]{1,0:T(2,128)S(1)} %copy-done.2, f32[512,256]{1,0:T(8,128)S(1)} %finish.1.updated_ref, f32[8,128,256]{2,1,0:T(8,128)S(1)} %all-to-all-done.1.strips_ref), custom_call_target="tpu_custom_call" | custom-call | tf_op jit(solution)/shard_map/assemble/pallas_call | solution.py:391
  (11 shorter events, 0.2 us)
Async XLA Ops:
  0.0 3.3 %copy-start.1 = (f32[1,128,2048]{2,1,0:T(8,128)S(1)}, f32[1,128,2048]{2,1,0:T(8,128)}, u32[]{:S(2)}) copy-start(f32[1,128,2048]{2,1,0:T(8,128)} %param.4) | copy-start | bytes 3145732
  1.2 13.2 %collective-permute-start.2 = (f32[4,2,16,256]{3,2,0,1:T(8,128)S(1)}, f32[4,2,16,256]{3,2,0,1:T(8,128)S(1)}, u32[]{:S(2)}, u32[]{:S(2)}) collective-permute-start(f32[4,2,16,256]{3,2,0,1:T(8,128)S(1)} %bitcast.30), channel_id=1, source_target_pairs={{0,12},{1,13},{2,14},{3,15}} | collective-permute-start | bytes 393224 | tf_op jit(solution)/shard_map/ppermute | solution.py:304
  1.9 12.5 %collective-permute-start = (f32[4,2,16,256]{3,2,0,1:T(8,128)S(1)}, f32[4,2,16,256]{3,2,0,1:T(8,128)S(1)}, u32[]{:S(2)}, u32[]{:S(2)}) collective-permute-start(f32[4,2,16,256]{3,2,0,1:T(8,128)S(1)} %bitcast.31), channel_id=1, source_target_pairs={{0,4},{1,5},{2,6},{3,7}} | collective-permute-start | bytes 393224 | tf_op jit(solution)/shard_map/ppermute | solution.py:304
  2.6 0.7 copy-start.2
  2.6 11.8 %collective-permute-start.1 = (f32[4,2,16,256]{3,2,0,1:T(8,128)S(1)}, f32[4,2,16,256]{3,2,0,1:T(8,128)S(1)}, u32[]{:S(2)}, u32[]{:S(2)}) collective-permute-start(f32[4,2,16,256]{3,2,0,1:T(8,128)S(1)} %bitcast.32), channel_id=1, source_target_pairs={{0,8},{1,9},{2,10},{3,11}} | collective-permute-start | bytes 393224 | tf_op jit(solution)/shard_map/ppermute | solution.py:304
  5.1 14.7 %all-to-all-start = ((f32[8,16,256]{2,1,0:T(8,128)}), f32[8,16,256]{2,1,0:T(8,128)S(1)}, u32[]{:S(2)}, u32[]{:S(2)}) async-start(f32[8,16,256]{2,1,0:T(8,128)} %get-tuple-element.18), calls=%async_computation | async-start | bytes 262144 | tf_op jit(solution)/shard_map/all_to_all | solution.py:316
  14.5 5.3 %collective-permute-start.3 = (f32[4,16,256]{2,1,0:T(8,128)S(1)}, f32[4,16,256]{2,1,0:T(8,128)S(1)}, u32[]{:S(2)}, u32[]{:S(2)}) collective-permute-start(f32[4,16,256]{2,1,0:T(8,128)S(1)} %get-tuple-element.36), channel_id=1, source_target_pairs={{0,16},{4,20},{8,24},{12,28},{1,17},{5,21},{9,25},{13,29},{2,18},{... | collective-permute-start | bytes 196616 | tf_op jit(solution)/shard_map/ppermute | solution.py:306
  20.4 67.8 %all-to-all-start.1 = ((f32[8,128,256]{2,1,0:T(8,128)}), f32[8,128,256]{2,1,0:T(8,128)S(1)}, u32[]{:S(2)}, u32[]{:S(2)}) async-start(f32[8,128,256]{2,1,0:T(8,128)} %get-tuple-element.28), calls=%async_computation.1 | async-start | bytes 2097152 | tf_op jit(solution)/shard_map/all_to_all | solution.py:328
  25.6 19.5 %collective-permute-start.6 = (f32[4,16,256]{2,1,0:T(8,128)S(1)}, f32[4,16,256]{2,1,0:T(8,128)S(1)}, u32[]{:S(2)}, u32[]{:S(2)}) collective-permute-start(f32[4,16,256]{2,1,0:T(8,128)S(1)} %sum_panel.1), channel_id=1, source_target_pairs={{0,12},{4,8},{8,4},{12,0},{1,13},{5,9},{9,5},{13,1},{2,14},{6,10},... | collective-permute-start | bytes 196616 | tf_op jit(solution)/shard_map/ppermute | solution.py:326
  28.6 25.4 %collective-permute-start.5 = (f32[4,16,256]{2,1,0:T(8,128)S(1)}, f32[4,16,256]{2,1,0:T(8,128)S(1)}, u32[]{:S(2)}, u32[]{:S(2)}) collective-permute-start(f32[4,16,256]{2,1,0:T(8,128)S(1)} %sum_panel.1), channel_id=1, source_target_pairs={{0,8},{4,12},{8,0},{12,4},{1,9},{5,13},{9,1},{13,5},{2,10},{6,14},... | collective-permute-start | bytes 196616 | tf_op jit(solution)/shard_map/ppermute | solution.py:326
  28.6 25.4 %collective-permute-start.4 = (f32[4,16,256]{2,1,0:T(8,128)S(1)}, f32[4,16,256]{2,1,0:T(8,128)S(1)}, u32[]{:S(2)}, u32[]{:S(2)}) collective-permute-start(f32[4,16,256]{2,1,0:T(8,128)S(1)} %sum_panel.1), channel_id=1, source_target_pairs={{0,4},{4,0},{8,12},{12,8},{1,5},{5,1},{9,13},{13,9},{2,6},{6,2},{1... | collective-permute-start | bytes 196616 | tf_op jit(solution)/shard_map/ppermute | solution.py:326
  54.1 3.9 %collective-permute-start.7 = (f32[4,2,16,256]{3,2,1,0:T(8,128)S(1)}, f32[4,2,16,256]{3,2,1,0:T(8,128)S(1)}, u32[]{:S(2)}, u32[]{:S(2)}) collective-permute-start(f32[4,2,16,256]{3,2,1,0:T(8,128)S(1)} %get-tuple-element.35), channel_id=1, source_target_pairs={{0,16},{16,0},{1,17},{17,1},{2,18},{18,2},{3,19},{19,3},{4,20},{20... | collective-permute-start | bytes 393224 | tf_op jit(solution)/shard_map/ppermute | solution.py:329
  58.0 5.3 %collective-permute-start.8 = (f32[4,2,16,256]{3,2,1,0:T(8,128)S(1)}, f32[4,2,16,256]{3,2,1,0:T(8,128)S(1)}, u32[]{:S(2)}, u32[]{:S(2)}) collective-permute-start(f32[4,2,16,256]{3,2,1,0:T(8,128)S(1)} %get-tuple-element.21), channel_id=1, source_target_pairs={{0,16},{16,0},{1,17},{17,1},{2,18},{18,2},{3,19},{19,3},{4,20},{20... | collective-permute-start | bytes 393224 | tf_op jit(solution)/shard_map/ppermute | solution.py:358
  58.3 28.0 %copy-start = (f32[512,256]{1,0:T(8,128)S(1)}, f32[512,256]{1,0:T(8,128)}, u32[]{:S(2)}) copy-start(f32[512,256]{1,0:T(8,128)} %base_ref.1) | copy-start | bytes 1572868
  58.3 7.7 %collective-permute-start.10 = (f32[256,256]{1,0:T(8,128)S(1)}, f32[256,256]{1,0:T(8,128)S(1)}, u32[]{:S(2)}, u32[]{:S(2)}) collective-permute-start(f32[256,256]{1,0:T(8,128)S(1)} %get-tuple-element.27.refs_6_), channel_id=1, source_target_pairs={{0,2},{4,6},{8,10},{12,14},{16,18},{20,22},{24,26},{28,30}} | collective-permute-start | bytes 786440 | tf_op jit(solution)/shard_map/ppermute | solution.py:290
  63.3 3.4 %collective-permute-start.13 = (f32[8,2,16,256]{3,2,1,0:T(8,128)S(1)}, f32[8,2,16,256]{3,2,1,0:T(8,128)S(1)}, u32[]{:S(2)}, u32[]{:S(2)}) collective-permute-start(f32[8,2,16,256]{3,2,1,0:T(8,128)S(1)} %pad_maximum_fusion.1.refs_10_), channel_id=1, source_target_pairs={{0,2},{4,6},{9,11},{13,15},{18,16},{22,20},{27,25},{31,29}} | collective-permute-start | bytes 786440 | tf_op jit(solution)/shard_map/ppermute | solution.py:290
  64.0 15.3 %collective-permute-start.9 = (f32[256,256]{1,0:T(8,128)S(1)}, f32[256,256]{1,0:T(8,128)S(1)}, u32[]{:S(2)}, u32[]{:S(2)}) collective-permute-start(f32[256,256]{1,0:T(8,128)S(1)} %get-tuple-element.27.refs_6_), channel_id=1, source_target_pairs={{0,1},{4,5},{8,9},{12,13},{16,17},{20,21},{24,25},{28,29}} | collective-permute-start | bytes 786440 | tf_op jit(solution)/shard_map/ppermute | solution.py:291
  65.3 14.0 %collective-permute-start.12 = (f32[8,2,16,256]{3,2,1,0:T(8,128)S(1)}, f32[8,2,16,256]{3,2,1,0:T(8,128)S(1)}, u32[]{:S(2)}, u32[]{:S(2)}) collective-permute-start(f32[8,2,16,256]{3,2,1,0:T(8,128)S(1)} %pad_maximum_fusion.1.refs_10_), channel_id=1, source_target_pairs={{0,1},{4,5},{9,8},{13,12},{18,19},{22,23},{27,26},{31,30}} | collective-permute-start | bytes 786440 | tf_op jit(solution)/shard_map/ppermute | solution.py:291
  66.0 13.3 %collective-permute-start.11 = (f32[256,256]{1,0:T(8,128)S(1)}, f32[256,256]{1,0:T(8,128)S(1)}, u32[]{:S(2)}, u32[]{:S(2)}) collective-permute-start(f32[256,256]{1,0:T(8,128)S(1)} %collective-permute-done.10.refs_8_), channel_id=1, source_target_pairs={{2,3},{6,7},{10,11},{14,15},{18,19},{22,23},{26,27},{30,31}} | collective-permute-start | bytes 786440 | tf_op jit(solution)/shard_map/ppermute | solution.py:292
  66.7 19.5 %collective-permute-start.14 = (f32[8,2,16,256]{3,2,1,0:T(8,128)S(1)}, f32[8,2,16,256]{3,2,1,0:T(8,128)S(1)}, u32[]{:S(2)}, u32[]{:S(2)}) collective-permute-start(f32[8,2,16,256]{3,2,1,0:T(8,128)S(1)} %collective-permute-done.13.refs_12_), channel_id=1, source_target_pairs={{2,3},{6,7},{11,10},{15,14},{16,17},{20,21},{25,24},{29,28}} | collective-permute-start | bytes 786440 | tf_op jit(solution)/shard_map/ppermute | solution.py:292
